TPU v7x, 32 devices: a whole 2x2x4 slice. The times are simulated.
32 devices in a mesh: seq: 8 (over z, x), head: 4 (over y, core).
Axes of the slice: x: 2, y: 2, z: 4, core: 2. Of those that a mesh axis runs over, the one named last changes fastest.
Arguments:
- ssm_input: float32 [4096, 4096], P('seq', 'head'), may hold values from -50 to 50
- gate_input: bfloat16 [4096, 4096], P('seq', 'head'), may hold values from -6 to 6
- step_raw: float32 [4096, 64], P('seq', 'head'), may hold values from -6 to 8192
- decay_log: float32 [64], P('head')
- state_in: float32 [4096, 4, 128], P('seq', 'head'), may hold values from -0.5 to 0.5
- state_out: float32 [4096, 4, 128], P('seq', 'head'), may hold values from -6 to 6
- skip_gain: float32 [64], P('head'), may hold values from 0.5 to 2
- norm_gain: float32 [4096], P('head'), may hold values from 0.25 to 1.75
- out_weight: bfloat16 [4096, 4096], P('head'), may hold values from -0.09375 to 0.09375
Outputs:
- layer_out: bfloat16 [4096, 4096], P(('seq', 'head'))
All inputs are finite; a program needn't handle non-finite values.
Results may differ from a plain program's by a relative error of at most 0.015.
Values may be sent and summed in bfloat16 or wider, within the bound.
No kernel may reach another device: no remote copies, remote signals or barrier semaphores. Data moves between devices by JAX's collectives and lax.ppermute only.
A program may use at most 192 MiB of HBM per device.

v0:
```python
import functools

import jax
import jax.numpy as jnp
from jax import lax
from jax.experimental import pallas as pl
from jax.experimental.pallas import tpu as pltpu
from jax.sharding import PartitionSpec as P

P_SIZE = 64
N = 128
CHUNK = 128
LANES = 128
BF = jnp.bfloat16
F32 = jnp.float32
VMEM_LIMIT = 16 * 1024 * 1024
WHOLE_VMEM = 61 * 1024 * 1024 + 512 * 1024
PIECES = ((0, 1024), (1024, 1536), (2560, 1536))


def dot(a, b, contract=((1,), (0,)), precision=None):
    return lax.dot_general(a, b, (contract, ((), ())), precision=precision, preferred_element_type=F32)


def split2(v):
    hi = v.astype(BF)
    return hi, (v - hi.astype(F32)).astype(BF)


def split3(v):
    hi, rest = v.astype(BF), v
    rest = v - hi.astype(F32)
    mid = rest.astype(BF)
    return hi, mid, (rest - mid.astype(F32)).astype(BF)


def pick(rows, lanes, heads, per_head, first):
    r = lax.broadcasted_iota(jnp.int32, (rows, lanes), 0) % heads
    l = lax.broadcasted_iota(jnp.int32, (rows, lanes), 1) // per_head + first
    return jnp.where(r == l, 1.0, 0.0).astype(BF)


def step_vectors(raw, rate_row, wk, aux_ref):
    heads, tok = raw.shape
    chunks = tok // CHUNK
    step = jnp.maximum(raw, 0.0) + jnp.log1p(jnp.exp(-jnp.abs(raw)))
    r = lax.broadcasted_iota(jnp.int32, (heads, heads), 0)
    l = lax.broadcasted_iota(jnp.int32, (heads, heads), 1)
    rate = jnp.sum(jnp.where(r == l, rate_row, 0.0), axis=1, keepdims=True)
    logs = -step * jnp.exp(rate)
    parts = split3(logs)
    stacked = jnp.concatenate(
        [p[:, c * CHUNK:(c + 1) * CHUNK] for c in range(chunks) for p in parts], axis=0
    )
    s = lax.broadcasted_iota(jnp.int32, (CHUNK, 2 * CHUNK), 0)
    t = lax.broadcasted_iota(jnp.int32, (CHUNK, 2 * CHUNK), 1)
    tri = jnp.where(jnp.where(t < CHUNK, t - s, s - t + (CHUNK - 1)) >= 0, 1.0, 0.0).astype(BF)
    sums = dot(stacked, tri)
    pre, suf = [], []
    for c in range(chunks):
        base = 3 * heads * c
        total = (
            sums[base:base + heads] + sums[base + heads:base + 2 * heads]
        ) + sums[base + 2 * heads:base + 3 * heads]
        pre.append(total[:, :CHUNK])
        suf.append(total[:, CHUNK:])
    after = jnp.zeros((heads, 1), F32)
    for c in reversed(range(chunks)):
        w = step[:, c * CHUNK:(c + 1) * CHUNK] * jnp.exp(suf[c] + after)
        hi, lo = split2(w)
        wk[:heads, c * CHUNK:(c + 1) * CHUNK] = hi
        wk[heads:, c * CHUNK:(c + 1) * CHUNK] = lo
        after = after + pre[c][:, CHUNK - 1:]
    hi, lo = split2(jnp.broadcast_to(jnp.exp(after), (heads, CHUNK)))
    wk[:heads, tok:] = hi
    wk[heads:, tok:] = lo
    for c in range(chunks):
        aux_ref[c, :heads] = step[:, c * CHUNK:(c + 1) * CHUNK]
        aux_ref[c, heads:2 * heads] = pre[c]
        aux_ref[c, 2 * heads:] = suf[c]


def tail_rows(decays):
    r = lax.broadcasted_iota(jnp.int32, (16, LANES), 0)
    tail = jnp.zeros((16, LANES), F32)
    for k, decay in enumerate(decays):
        hi, lo = split2(decay)
        tail = jnp.where(r == 2 * k, hi.astype(F32), tail)
        tail = jnp.where(r == 2 * k + 1, lo.astype(F32), tail)
    return tail.astype(BF)


def decays_of(msg):
    blocks = (msg.shape[0] - 16) // N
    tail = msg[blocks * N:].astype(F32)
    return [tail[2 * k:2 * k + 1] + tail[2 * k + 1:2 * k + 2] for k in range(blocks)]


def half_message(x_ref, b, wk, first_head, msg):
    tok, lanes = x_ref.shape
    heads2 = wk.shape[0]
    width = 256
    decays = []
    for g in range(lanes // width):
        chosen = pick(heads2, width, heads2 // 2, P_SIZE, first_head + g * (width // P_SIZE))
        spread = dot(wk[...], chosen, ((0,), (0,)))
        weighted = (x_ref[:, g * width:(g + 1) * width] * spread[:tok]).astype(BF)
        state = dot(b, weighted, ((0,), (0,)))
        for i in range(width // LANES):
            k = g * (width // LANES) + i
            msg[k * N:(k + 1) * N] = state[:, i * LANES:(i + 1) * LANES].astype(BF)
            decays.append(spread[tok:tok + 1, i * LANES:(i + 1) * LANES])
    msg[msg.shape[0] - 16:] = tail_rows(decays)


def half_kernel(give, raw, rate, x, b, msg, wk, aux, raw_v, rate_v, x_v, b_v, sems):
    lanes = x_v.shape[1]
    mine = lax.axis_index("seq") % 2
    half = 1 - mine if give else mine
    loads = [
        pltpu.make_async_copy(b, b_v, sems.at[0]),
        pltpu.make_async_copy(
            x.at[:, pl.ds(pl.multiple_of(half * lanes, lanes), lanes)], x_v, sems.at[1]
        ),
    ]
    if give:
        loads += [
            pltpu.make_async_copy(raw, raw_v, sems.at[2]),
            pltpu.make_async_copy(rate, rate_v, sems.at[3]),
        ]
    for load in reversed(loads):
        load.start()
    if give:
        loads[2].wait()
        loads[3].wait()
        step_vectors(raw_v[...], rate_v[...], wk, aux)
    loads[0].wait()
    loads[1].wait()
    half_message(x_v, b_v[...].astype(BF), wk, half * (lanes // P_SIZE), msg)


def give_kernel(raw, rate, x, b, msg, wk, aux, raw_v, rate_v, x_v, b_v, sems):
    half_kernel(True, raw, rate, x, b, msg, wk, aux, raw_v, rate_v, x_v, b_v, sems)


def keep_kernel(wk, x, b, msg, x_v, b_v, sems):
    half_kernel(False, None, None, x, b, msg, wk, None, None, None, x_v, b_v, sems)


HBM = pl.BlockSpec(memory_space=pltpu.HBM)
VMEM = pl.BlockSpec(memory_space=pltpu.VMEM)


def give_states(raw, rate, x, b):
    heads, tok = raw.shape
    lanes = x.shape[1] // 2
    return pl.pallas_call(
        give_kernel,
        in_specs=[HBM] * 4,
        out_shape=[
            jax.ShapeDtypeStruct((lanes + 16, LANES), BF),
            jax.ShapeDtypeStruct((2 * heads, tok + CHUNK), BF),
            jax.ShapeDtypeStruct((tok // CHUNK, 3 * heads, CHUNK), F32),
        ],
        scratch_shapes=[
            pltpu.VMEM((heads, tok), F32),
            pltpu.VMEM((1, heads), F32),
            pltpu.VMEM((tok, lanes), F32),
            pltpu.VMEM((tok, N), F32),
            pltpu.SemaphoreType.DMA((4,)),
        ],
        compiler_params=pltpu.CompilerParams(vmem_limit_bytes=WHOLE_VMEM),
        cost_estimate=pl.CostEstimate(flops=200_000_000, bytes_accessed=1_500_000, transcendentals=0),
        name="give_states",
    )(raw, rate, x, b)


def keep_states(wk, x, b):
    tok = x.shape[0]
    lanes = x.shape[1] // 2
    return pl.pallas_call(
        keep_kernel,
        in_specs=[pl.BlockSpec(memory_space=pltpu.VMEM), HBM, HBM],
        out_shape=jax.ShapeDtypeStruct((lanes + 16, LANES), BF),
        scratch_shapes=[
            pltpu.VMEM((tok, lanes), F32),
            pltpu.VMEM((tok, N), F32),
            pltpu.SemaphoreType.DMA((2,)),
        ],
        compiler_params=pltpu.CompilerParams(vmem_limit_bytes=VMEM_LIMIT),
        cost_estimate=pl.CostEstimate(flops=200_000_000, bytes_accessed=1_500_000, transcendentals=0),
        name="keep_states",
    )(wk, x, b)


def link(later, earlier, out):
    ahead, behind = decays_of(later), decays_of(earlier)
    for k, decay in enumerate(ahead):
        rows = slice(k * N, (k + 1) * N)
        out[rows] = (later[rows].astype(F32) + decay * earlier[rows].astype(F32)).astype(BF)
    out[len(ahead) * N:] = tail_rows([p * q for p, q in zip(ahead, behind)])


def pair_kernel(own, come, out):
    odd = lax.axis_index("seq") % 2

    @pl.when(odd == 0)
    def _():
        link(come, own, out)

    @pl.when(odd == 1)
    def _():
        link(own, come, out)


def end_kernel(last, before, own, come, mine, theirs):
    blocks = mine.shape[0] // N
    odd = lax.axis_index("seq") % 2

    def fill(even_section, ahead_ref, behind_ref):
        step, span = decays_of(last), decays_of(even_section)
        for k in range(blocks):
            rows = slice(k * N, (k + 1) * N)
            start = last[rows].astype(F32)
            if before is not None:
                start = start + step[k] * before[rows].astype(F32)
            ahead_ref[rows] = start.astype(BF)
            behind_ref[rows] = (even_section[rows].astype(F32) + span[k] * start).astype(BF)

    @pl.when(odd == 0)
    def _():
        fill(own, mine, theirs)

    @pl.when(odd == 1)
    def _():
        fill(come, theirs, mine)


def scan_call(kernel, operands, shapes, name):
    return pl.pallas_call(
        kernel,
        out_shape=[jax.ShapeDtypeStruct(shape, BF) for shape in shapes],
        compiler_params=pltpu.CompilerParams(vmem_limit_bytes=VMEM_LIMIT),
        cost_estimate=pl.CostEstimate(flops=500_000, bytes_accessed=400_000, transcendentals=0),
        name=name,
    )(*operands)


def incoming_states(give, keep, count, hold):
    pair = [(s, s ^ 1) for s in range(count)]
    come = lax.ppermute(give, "seq", pair)
    run = scan_call(pair_kernel, (keep, come), [keep.shape], "join_pair")[0]
    start, distance = None, 2
    while distance < count:
        got = lax.ppermute(run, "seq", [(s, s + distance) for s in range(count - distance)])
        if distance * 2 >= count:
            break
        run = scan_call(link, (run, got), [keep.shape], "join_run")[0]
        start = got if start is None else scan_call(link, (start, got), [keep.shape], "join_start")[0]
        distance *= 2
    hold, got = hold(got)
    half = (keep.shape[0] - 16, LANES)
    mine, theirs = scan_call(end_kernel, (start, got, keep, come), [half, half], "join_end")
    return hold, mine, lax.ppermute(theirs, "seq", pair)


def rows_of(ref, block):
    return ref[pl.ds(pl.multiple_of(block * CHUNK, CHUNK), CHUNK), :]


def within_kernel(far, aux, x_ref, b_ref, c_ref, gate_ref, skip_ref, own_ref, lead_ref):
    channels = x_ref.shape[1]
    heads = aux.shape[1] // 3
    width = 256
    here = width // P_SIZE
    half = lax.axis_index("head") // 2
    half = 1 - half if far else half
    second = half == 1

    def vectors(c):
        return [aux[c, k * heads:(k + 1) * heads] for k in range(3)]

    def put(values):
        return jnp.concatenate([jnp.concatenate(split2(v), axis=0) for v in values], axis=1)

    first, then = vectors(0), vectors(1)
    ends = [v[1][:, CHUNK - 1:] for v in (first, then)]
    early = put(
        [
            jnp.where(second, first[0] * jnp.exp(first[2] + ends[1]), 0.0),
            jnp.where(second, then[0] * jnp.exp(then[2]), 0.0),
        ]
    )
    before = jnp.where(second, ends[0] + ends[1], 0.0)
    r = lax.broadcasted_iota(jnp.int32, (CHUNK, CHUNK), 0)
    l = lax.broadcasted_iota(jnp.int32, (CHUNK, CHUNK), 1)
    duo, trip, lines, scores, rows_b, rows_c, rows_x, rows_g = ([] for _ in range(8))
    for i in range(2):
        block = 2 * half + i
        step, pre, suf = vectors(block)
        duo.append(put((step, step * jnp.exp(suf), jnp.exp(pre), jnp.exp(pre + before))))
        trip.append(jnp.concatenate(split3(pre), axis=0))
        lines.append(pre)
        before = before + pre[:, CHUNK - 1:]
        b, c = rows_of(b_ref, block), rows_of(c_ref, block)
        raw = dot(c, b, ((1,), (1,)), lax.Precision.HIGHEST)
        scores.append(jnp.where(r >= l, raw, 0.0))
        rows_b.append(b.astype(BF))
        rows_c.append(c.astype(BF))
        rows_x.append(rows_of(x_ref, block))
        rows_g.append(rows_of(gate_ref, block))
    early_b = b_ref[:2 * CHUNK].astype(BF)
    gains = jnp.broadcast_to(jnp.concatenate(split3(skip_ref[...]), axis=1), (8, 3 * heads))
    lane = lax.broadcasted_iota(jnp.int32, (CHUNK, LANES), 1)
    for g in range(channels // width):
        at = slice(g * width, (g + 1) * width)
        spread = pick(2 * heads, width, heads, P_SIZE, g * here)
        columns = pick(3 * heads, here * CHUNK, heads, CHUNK, g * here)
        skip = dot(gains, pick(3 * heads, width, heads, P_SIZE, g * here))[:1]
        weights = dot(early, spread, ((0,), (0,)))
        state = dot(early_b, (x_ref[:2 * CHUNK, at] * weights).astype(BF), ((0,), (0,)))
        for i in range(2):
            cut = slice(i * CHUNK, (i + 1) * CHUNK)
            wide = dot(duo[i], spread, ((0,), (0,)))
            x = rows_x[i][:, at]
            stepped = x * wide[:CHUNK]
            lead = wide[2 * CHUNK:3 * CHUNK]
            tall = dot(trip[i], columns, ((0,), (0,)))
            outs = []
            for pair in range(here // 2):
                mixes = []
                for h in (2 * pair, 2 * pair + 1):
                    line = lines[i][g * here + h:g * here + h + 1]
                    gap = tall[:, h * CHUNK:(h + 1) * CHUNK] - line
                    mixes.append((scores[i] * jnp.exp(jnp.minimum(gap, 0.0))).astype(BF))
                both = stepped[:, pair * LANES:(pair + 1) * LANES]
                stacked = jnp.concatenate(
                    [
                        jnp.where(lane < P_SIZE, both, 0.0).astype(BF),
                        jnp.where(lane < P_SIZE, 0.0, both).astype(BF),
                    ],
                    axis=0,
                )
                outs.append(dot(jnp.concatenate(mixes, axis=1), stacked))
            y = jnp.concatenate(outs, axis=1) + skip * x
            y = y + lead * dot(rows_c[i], state.astype(BF))
            v = rows_g[i][:, at].astype(F32)
            silu = v / (1.0 + jnp.exp(-v))
            own_ref[cut, at] = y * silu
            lead_ref[cut, at] = wide[3 * CHUNK:] * silu
            if i == 0:
                weighted = (x * wide[CHUNK:2 * CHUNK]).astype(BF)
                state = state * lead[CHUNK - 1:] + dot(rows_b[i], weighted, ((0,), (0,)))


def within(far, aux, x, b, c, gate, skip):
    channels = x.shape[1]
    return pl.pallas_call(
        functools.partial(within_kernel, far),
        in_specs=[VMEM] * 6,
        out_specs=[VMEM] * 2,
        out_shape=[jax.ShapeDtypeStruct((2 * CHUNK, channels), F32)] * 2,
        compiler_params=pltpu.CompilerParams(vmem_limit_bytes=VMEM_LIMIT),
        cost_estimate=pl.CostEstimate(
            flops=4_000_000_000, bytes_accessed=3_000_000, transcendentals=500_000
        ),
        name="within_far" if far else "within_near",
    )(aux, x, b, c, gate, skip)


def finish_rows(own, lead, c, incoming, gain):
    c = c.astype(BF)
    blocks = incoming.shape[1] // N
    carried = jnp.concatenate(
        [dot(c, incoming[h, k * N:(k + 1) * N]) for h in range(2) for k in range(blocks)], axis=1
    )
    gated = own + lead * carried
    mean = jnp.mean(gated * gated, axis=1, keepdims=True)
    return (gated * lax.rsqrt(mean + 1e-05) * gain).astype(BF)


def finish_block(block, own, lead, c, incoming, gain):
    return finish_rows(
        rows_of(own, block % 2), rows_of(lead, block % 2), rows_of(c, block), incoming, gain[...]
    )


def fill_incoming(here, there, incoming):
    odd = lax.axis_index("seq") % 2
    incoming[odd] = here[...]
    incoming[1 - odd] = there[...]


def project_both(normed, w, start, columns, theirs, mine, at=0):
    wide = 512
    for k in range(0, columns, wide):
        out = dot(normed[...], w[:, start + k:start + k + wide])
        theirs[:, at + k:at + k + wide] = out[:CHUNK].astype(BF)
        mine[:, k:k + wide] = out[CHUNK:]


def far_kernel(columns, own, lead, c, here, there, gain, w, theirs, mine, normed, incoming):
    me = lax.axis_index("head")
    fill_incoming(here, there, incoming)
    normed[:CHUNK] = finish_block(me ^ 3, own, lead, c, incoming, gain)
    normed[CHUNK:] = finish_block(me ^ 2, own, lead, c, incoming, gain)
    project_both(normed, w, 0, columns, theirs, mine)


def more_kernel(start, columns, normed, w, theirs, mine):
    project_both(normed, w, start, columns, theirs, mine)


def mixed_kernel(
    start, columns, normed, own, lead, c, here, there, gain, w, theirs, mine, kept, incoming, given
):
    me = lax.axis_index("head")
    project_both(normed, w, start, columns, theirs, mine)
    fill_incoming(here, there, incoming)
    given[...] = finish_block(me ^ 1, own, lead, c, incoming, gain)
    kept[...] = finish_block(me, own, lead, c, incoming, gain)
    wide = 512
    for k in range(0, w.shape[1], wide):
        theirs[:, columns + k:columns + k + wide] = dot(given[...], w[:, k:k + wide]).astype(BF)


def kept_kernel(columns, kept, come, w, out):
    wide = 512
    for k in range(0, w.shape[1], wide):
        out[:, k:k + wide] = dot(kept[...], w[:, k:k + wide]) + come[
            :, columns + k:columns + k + wide
        ].astype(F32)


def add_kernel(mine, come, out):
    out[...] = (mine[...] + come[:, :out.shape[1]].astype(F32)).astype(BF)


def local_call(kernel, operands, outs, name, scratch=(), flops=0, limit=VMEM_LIMIT):
    return pl.pallas_call(
        kernel,
        in_specs=[VMEM] * len(operands),
        out_specs=[VMEM] * len(outs),
        out_shape=[jax.ShapeDtypeStruct(shape, dtype) for shape, dtype in outs],
        scratch_shapes=list(scratch),
        compiler_params=pltpu.CompilerParams(vmem_limit_bytes=limit),
        cost_estimate=pl.CostEstimate(flops=flops, bytes_accessed=0, transcendentals=0),
        name=name,
    )(*operands)


def pass_kernel(*refs):
    pass


def await_piece(piece, *earlier):
    arrays = [piece, *earlier]
    return pl.pallas_call(
        pass_kernel,
        in_specs=[pl.BlockSpec(memory_space=pl.ANY)] * len(arrays),
        out_specs=[pl.BlockSpec(memory_space=pl.ANY)] * len(arrays),
        out_shape=[jax.ShapeDtypeStruct(v.shape, v.dtype) for v in arrays],
        input_output_aliases={k: k for k in range(len(arrays))},
        compiler_params=pltpu.CompilerParams(vmem_limit_bytes=1024 * 1024),
        cost_estimate=pl.CostEstimate(
            flops=20_000_000_000, bytes_accessed=100_000_000, transcendentals=0
        ),
        name="await_piece",
    )(*arrays)


def early_kernel(kept, first, second, out):
    at = 0
    for piece in (first, second):
        cut = slice(at, at + piece.shape[1])
        out[:, cut] = (kept[:, cut] + piece[...].astype(F32)).astype(BF)
        at += piece.shape[1]


def early_sums(kept, first, second):
    rows = first.shape[0]
    wide = first.shape[1] + second.shape[1]
    return pl.pallas_call(
        early_kernel,
        grid=(1,),
        in_specs=[VMEM] * 3,
        out_specs=pl.BlockSpec((rows, wide), lambda j: (0, 0)),
        out_shape=jax.ShapeDtypeStruct(kept.shape, BF),
        compiler_params=pltpu.CompilerParams(vmem_limit_bytes=VMEM_LIMIT),
        name="early_sums",
    )(kept, first, second)


def last_kernel(kept, third, filled, out):
    out[...] = (kept[...] + third[...].astype(F32)).astype(BF)


def last_sums(kept, third, filled):
    rows, wide = third.shape
    block = 512
    start = (kept.shape[1] - wide) // block
    return pl.pallas_call(
        last_kernel,
        grid=(wide // block,),
        in_specs=[
            pl.BlockSpec((rows, block), lambda j: (0, j + start)),
            pl.BlockSpec((rows, block), lambda j: (0, j)),
            pl.BlockSpec(memory_space=pl.ANY),
        ],
        out_specs=pl.BlockSpec((rows, block), lambda j: (0, j + start)),
        out_shape=jax.ShapeDtypeStruct(kept.shape, BF),
        input_output_aliases={2: 0},
        compiler_params=pltpu.CompilerParams(vmem_limit_bytes=VMEM_LIMIT),
        name="last_sums",
    )(kept, third, filled)


def per_device(
    seq_count,
    ssm_input,
    gate_input,
    step_raw,
    decay_log,
    state_in,
    state_out,
    skip_gain,
    norm_gain,
    out_weight,
):
    tok = ssm_input.shape[0]
    heads = decay_log.shape[0]
    b = state_in.reshape(tok, N)
    c = state_out.reshape(tok, N)
    give, wk, aux = give_states(step_raw.T, decay_log.reshape(1, heads), ssm_input, b)
    keep = keep_states(wk, ssm_input, b)
    inputs = (ssm_input, b, c, gate_input, skip_gain.reshape(1, heads))
    local = within(True, aux, *inputs)
    (own, lead), here, there = incoming_states(
        give, keep, seq_count, lambda got: lax.optimization_barrier((local, got))
    )

    near = [(h, h ^ 1) for h in range(4)]
    far = [(h, h ^ 2) for h in range(4)]
    gain = norm_gain.reshape(1, -1)
    channels, dout = out_weight.shape
    rows = CHUNK
    states = pltpu.VMEM((2,) + here.shape, BF)
    finish = (own, lead, c, here, there, gain, out_weight)
    (_, one), (start2, two), (start3, three) = PIECES

    def piece_outs(columns, extra=0):
        return [((rows, columns + extra), BF), ((rows, columns), F32)]

    def add(mine, theirs):
        come = lax.ppermute(theirs, "head", near)
        return local_call(add_kernel, (mine, come), [(mine.shape, BF)], "add_pair", limit=1 << 22)[0], come

    theirs, mine, normed = local_call(
        functools.partial(far_kernel, one),
        finish,
        piece_outs(one) + [((2 * rows, channels), BF)],
        "finish_far",
        [states],
        4 * rows * channels * one,
    )
    first, _ = add(mine, theirs)
    normed, aux, first = lax.optimization_barrier((normed, aux, first))
    theirs, mine = local_call(
        functools.partial(more_kernel, start2, two),
        (normed, out_weight),
        piece_outs(two),
        "project_more",
        flops=4 * rows * channels * two,
    )
    second, _ = add(mine, theirs)
    near_own, near_lead = within(False, aux, *inputs)
    normed, second = lax.optimization_barrier((normed, second))
    theirs, mine, kept = local_call(
        functools.partial(mixed_kernel, start3, three),
        (normed, near_own, near_lead) + finish[2:],
        piece_outs(three, dout) + [((rows, channels), BF)],
        "finish_near",
        [states, pltpu.VMEM((rows, channels), BF)],
        2 * rows * channels * (2 * three + dout),
    )
    third, come = add(mine, theirs)
    kept = local_call(
        functools.partial(kept_kernel, three),
        (kept, come, out_weight),
        [((rows, dout), F32)],
        "project_kept",
        flops=2 * rows * channels * dout,
    )[0]
    first = await_piece(lax.ppermute(first, "head", far))[0]
    second, first = await_piece(lax.ppermute(second, "head", far), first)
    filled = early_sums(kept, first, second)
    third, filled = await_piece(lax.ppermute(third, "head", far), filled)
    return last_sums(kept, third, filled)


def solution(mesh):
    in_specs = (
        P("seq", "head"),
        P("seq", "head"),
        P("seq", "head"),
        P("head"),
        P("seq", "head", None),
        P("seq", "head", None),
        P("head"),
        P("head"),
        P("head", None),
    )
    out_specs = P(("seq", "head"), None)
    return jax.shard_map(
        functools.partial(per_device, mesh.shape["seq"]),
        mesh=mesh,
        in_specs=in_specs,
        out_specs=out_specs,
        check_vma=False,
    )
```

profile of v0, /device:TPU:0, one launch (start us, length us, event | category | flops | bytes accessed | tf_op | source)
XLA Modules:
  0.0 61.0 jit_solution(16212459440719110490)
XLA Ops:
  0.0 2.9 %give_states.1 = (bf16[528,128]{1,0:T(8,128)(2,1)}, bf16[32,640]{1,0:T(8,128)(2,1)}, f32[4,48,128]{2,1,0:T(8,128)}) custom-call(f32[16,512]{1,0:T(8,128)} %bitcast.20, f32[1,16]{1,0:T(1,128)} %bitcast.21, f32[512,1024]{1,0:T(8,128)} %x_ref.3, f32[512,128]{1,0:T(8,128)} %bitcast.8), custom_call_target="tpu_custom_call" | custom-call | flops 200000000 | bytes 1500000 | tf_op jit(solution)/shard_map/give_states/pallas_call | solution.py:157
  2.9 3.0 %collective-permute-start = (bf16[528,128]{1,0:T(8,128)(2,1)}, bf16[528,128]{1,0:T(8,128)(2,1)S(1)}, u32[]{:S(2)}, u32[]{:S(2)}) collective-permute-start(bf16[528,128]{1,0:T(8,128)(2,1)} %get-tuple-element.38), channel_id=1, source_target_pairs={{0,4},{4,0},{8,12},{12,8},{16,20},{20,16},{24,28},{28,24},{1,5},{5... | collective-permute-start | bytes 405512 | tf_op jit(solution)/shard_map/ppermute | solution.py:251
  6.7 1.0 %keep_states.1.own = bf16[528,128]{1,0:T(8,128)(2,1)S(1)} custom-call(bf16[32,640]{1,0:T(8,128)(2,1)S(1)} %copy-done.3, f32[512,1024]{1,0:T(8,128)S(1)} %copy-done, f32[512,128]{1,0:T(8,128)S(1)} %bitcast.9), custom_call_target="tpu_custom_call" | custom-call | flops 200000000 | bytes 1500000 | tf_op jit(solution)/shard_map/keep_states/pallas_call | solution.py:181
  7.7 2.0 %collective-permute-done.come = bf16[528,128]{1,0:T(8,128)(2,1)S(1)} collective-permute-done((bf16[528,128]{1,0:T(8,128)(2,1)}, bf16[528,128]{1,0:T(8,128)(2,1)S(1)}, u32[]{:S(2)}, u32[]{:S(2)}) %collective-permute-start) | collective-permute-done | bytes 135200 | tf_op jit(solution)/shard_map/ppermute | solution.py:251
  9.8 3.7 %collective-permute-start.1 = (bf16[528,128]{1,0:T(8,128)(2,1)S(1)}, bf16[528,128]{1,0:T(8,128)(2,1)S(1)}, u32[]{:S(2)}, u32[]{:S(2)}) collective-permute-start(bf16[528,128]{1,0:T(8,128)(2,1)S(1)} %join_pair.1.later), channel_id=1, source_target_pairs={{0,8},{4,12},{8,16},{12,20},{16,24},{20,28},{1,9},{5,13},{9,17},{1... | collective-permute-start | bytes 405512 | tf_op jit(solution)/shard_map/ppermute | solution.py:255
  13.5 2.5 %collective-permute-done.1.earlier.last = bf16[528,128]{1,0:T(8,128)(2,1)S(1)} collective-permute-done((bf16[528,128]{1,0:T(8,128)(2,1)S(1)}, bf16[528,128]{1,0:T(8,128)(2,1)S(1)}, u32[]{:S(2)}, u32[]{:S(2)}) %collective-permute-start.1) | collective-permute-done | bytes 135200 | tf_op jit(solution)/shard_map/ppermute | solution.py:255
  16.1 5.4 %collective-permute-start.2 = (bf16[528,128]{1,0:T(8,128)(2,1)S(1)}, bf16[528,128]{1,0:T(8,128)(2,1)S(1)}, u32[]{:S(2)}, u32[]{:S(2)}) collective-permute-start(bf16[528,128]{1,0:T(8,128)(2,1)S(1)} %join_run.1), channel_id=1, source_target_pairs={{0,16},{4,20},{8,24},{12,28},{1,17},{5,21},{9,25},{13,29},{2,18},{... | collective-permute-start | bytes 405512 | tf_op jit(solution)/shard_map/ppermute | solution.py:255
  21.6 3.2 %within_far.1 = (f32[256,1024]{1,0:T(8,128)S(1)}, f32[256,1024]{1,0:T(8,128)S(1)}) custom-call(f32[4,48,128]{2,1,0:T(8,128)S(1)} %copy-done.6, f32[512,1024]{1,0:T(8,128)S(1)} %copy-done, f32[512,128]{1,0:T(8,128)S(1)} %bitcast.10, f32[512,128]{1,0:T(8,128)S(1)} %bitcast.12, bf16[512,1024]{1,0:T(8,128)(2,1)S(1)} %copy-done.5, f32[1,16]{1,0:T(1,128)S(1)} %bitcast.18), custom_call_target="tpu_custom_call" | custom-call | flops 4000000000 | bytes 3000000 | tf_op jit(solution)/shard_map/within_far/pallas_call | solution.py:358
  25.1 1.6 %collective-permute-start.3 = (bf16[512,128]{1,0:T(8,128)(2,1)S(1)}, bf16[512,128]{1,0:T(8,128)(2,1)S(1)}, u32[]{:S(2)}, u32[]{:S(2)}) collective-permute-start(bf16[512,128]{1,0:T(8,128)(2,1)S(1)} %get-tuple-element.43), channel_id=1, source_target_pairs={{0,4},{4,0},{8,12},{12,8},{16,20},{20,16},{24,28},{28,24},{1,5},{5... | collective-permute-start | bytes 393224 | tf_op jit(solution)/shard_map/ppermute | solution.py:264
  26.6 3.5 %collective-permute-done.3.there = bf16[512,128]{1,0:T(8,128)(2,1)S(1)} collective-permute-done((bf16[512,128]{1,0:T(8,128)(2,1)S(1)}, bf16[512,128]{1,0:T(8,128)(2,1)S(1)}, u32[]{:S(2)}, u32[]{:S(2)}) %collective-permute-start.3) | collective-permute-done | bytes 131104 | tf_op jit(solution)/shard_map/ppermute | solution.py:264
  30.1 1.1 %finish_far.1 = (bf16[128,1024]{1,0:T(8,128)(2,1)S(1)}, f32[128,1024]{1,0:T(8,128)S(1)}, bf16[256,1024]{1,0:T(8,128)(2,1)S(1)}) custom-call(f32[256,1024]{1,0:T(8,128)S(1)} %get-tuple-element.39.own, f32[256,1024]{1,0:T(8,128)S(1)} %get-tuple-element.40.lead, f32[512,128]{1,0:T(8,128)S(1)} %bitcast.13, bf16[512,128]{1,0:T(8,128)(2,1)S(1)} %get-tuple-element.42.here, ...), custom_call_target="tpu_custom_call" | custom-call | flops 536870912 | tf_op jit(solution)/shard_map/finish_far/pallas_call | solution.py:440
  31.3 1.5 %collective-permute-done.4.come = bf16[128,1024]{1,0:T(8,128)(2,1)S(1)} collective-permute-done((bf16[128,1024]{1,0:T(8,128)(2,1)S(1)}, bf16[128,1024]{1,0:T(8,128)(2,1)S(1)}, u32[]{:S(2)}, u32[]{:S(2)}) %collective-permute-start.4) | collective-permute-done | bytes 262176 | tf_op jit(solution)/shard_map/ppermute | solution.py:555
  32.9 1.0 %project_more.1 = (bf16[128,1536]{1,0:T(8,128)(2,1)S(1)}, f32[128,1536]{1,0:T(8,128)S(1)}) custom-call(bf16[256,1024]{1,0:T(8,128)(2,1)S(1)} %get-tuple-element.50.normed, bf16[1024,4096]{1,0:T(8,128)(2,1)S(1)} %bitcast.7), custom_call_target="tpu_custom_call" | custom-call | flops 805306368 | tf_op jit(solution)/shard_map/project_more/pallas_call | solution.py:440
  34.1 1.5 %collective-permute-start.9 = (bf16[128,1024]{1,0:T(8,128)(2,1)S(1)}, bf16[128,1024]{1,0:T(8,128)(2,1)S(1)}, u32[]{:S(2)}, u32[]{:S(2)}) collective-permute-start(bf16[128,1024]{1,0:T(8,128)(2,1)S(1)} %add_pair.3), channel_id=1, source_target_pairs={{0,2},{1,3},{2,0},{3,1},{4,6},{5,7},{6,4},{7,5},{8,10},{9,11},{10,... | collective-permute-start | bytes 786440 | tf_op jit(solution)/shard_map/ppermute | solution.py:594
  35.6 3.2 %within_near.1 = (f32[256,1024]{1,0:T(8,128)S(1)}, f32[256,1024]{1,0:T(8,128)S(1)}) custom-call(f32[4,48,128]{2,1,0:T(8,128)S(1)} %copy-done.6, f32[512,1024]{1,0:T(8,128)S(1)} %copy-done, f32[512,128]{1,0:T(8,128)S(1)} %bitcast.11, f32[512,128]{1,0:T(8,128)S(1)} %bitcast.14, bf16[512,1024]{1,0:T(8,128)(2,1)S(1)} %copy-done.5, f32[1,16]{1,0:T(1,128)S(1)} %bitcast.19), custom_call_target="tpu_custom_call" | custom-call | flops 4000000000 | bytes 3000000 | tf_op jit(solution)/shard_map/within_near/pallas_call | solution.py:358
  39.5 2.5 %finish_near.1 = (bf16[128,5632]{1,0:T(8,128)(2,1)S(1)}, f32[128,1536]{1,0:T(8,128)S(1)}, bf16[128,1024]{1,0:T(8,128)(2,1)S(1)}) custom-call(bf16[256,1024]{1,0:T(8,128)(2,1)S(1)} %get-tuple-element.50.normed, f32[256,1024]{1,0:T(8,128)S(1)} %get-tuple-element.52.own, f32[256,1024]{1,0:T(8,128)S(1)} %get-tuple-element.53.lead, f32[512,128]{1,0:T(8,128)S(1)} %bitcast.15, ...), custom_call_target="tpu_custom_call" | custom-call | flops 1879048192 | tf_op jit(solution)/shard_map/finish_near/pallas_call | solution.py:440
  42.0 1.2 %collective-permute-done.9.refs_0_ = bf16[128,1024]{1,0:T(8,128)(2,1)S(1)} collective-permute-done((bf16[128,1024]{1,0:T(8,128)(2,1)S(1)}, bf16[128,1024]{1,0:T(8,128)(2,1)S(1)}, u32[]{:S(2)}, u32[]{:S(2)}) %collective-permute-start.9) | collective-permute-done | bytes 262176 | tf_op jit(solution)/shard_map/ppermute | solution.py:594
  43.2 2.0 %collective-permute-done.6.come = bf16[128,5632]{1,0:T(8,128)(2,1)S(1)} collective-permute-done((bf16[128,5632]{1,0:T(8,128)(2,1)S(1)}, bf16[128,5632]{1,0:T(8,128)(2,1)S(1)}, u32[]{:S(2)}, u32[]{:S(2)}) %collective-permute-start.6) | collective-permute-done | bytes 1441824 | tf_op jit(solution)/shard_map/ppermute | solution.py:555
  45.3 1.6 %collective-permute-start.7 = (bf16[128,1536]{1,0:T(8,128)(2,1)S(1)}, bf16[128,1536]{1,0:T(8,128)(2,1)S(1)}, u32[]{:S(2)}, u32[]{:S(2)}) collective-permute-start(bf16[128,1536]{1,0:T(8,128)(2,1)S(1)} %add_pair.5), channel_id=1, source_target_pairs={{0,2},{1,3},{2,0},{3,1},{4,6},{5,7},{6,4},{7,5},{8,10},{9,11},{10,... | collective-permute-start | bytes 1179656 | tf_op jit(solution)/shard_map/ppermute | solution.py:597
  46.9 4.7 %collective-permute-done.8.refs_0_ = bf16[128,1536]{1,0:T(8,128)(2,1)S(1)} collective-permute-done((bf16[128,1536]{1,0:T(8,128)(2,1)S(1)}, bf16[128,1536]{1,0:T(8,128)(2,1)S(1)}, u32[]{:S(2)}, u32[]{:S(2)}) %collective-permute-start.8) | collective-permute-done | bytes 393248 | tf_op jit(solution)/shard_map/ppermute | solution.py:595
  51.6 1.3 %project_kept.1.kept = f32[128,4096]{1,0:T(8,128)S(1)} custom-call(bf16[128,1024]{1,0:T(8,128)(2,1)S(1)} %get-tuple-element.54.kept, bf16[128,5632]{1,0:T(8,128)(2,1)S(1)} %collective-permute-done.6.come, bf16[1024,4096]{1,0:T(8,128)(2,1)S(1)} %bitcast.7), custom_call_target="tpu_custom_call" | custom-call | flops 1073741824 | tf_op jit(solution)/shard_map/project_kept/pallas_call | solution.py:440
  53.0 0.9 %early_sums.1.refs_1_ = bf16[128,4096]{1,0:T(8,128)(2,1)} custom-call(f32[128,4096]{1,0:T(8,128)S(1)} %project_kept.1.kept, bf16[128,1024]{1,0:T(8,128)(2,1)S(1)} %get-tuple-element.59.first, bf16[128,1536]{1,0:T(8,128)(2,1)S(1)} %get-tuple-element.60.second), custom_call_target="tpu_custom_call" | custom-call | tf_op jit(solution)/shard_map/early_sums/pallas_call | solution.py:483
  53.9 5.6 %collective-permute-done.7.refs_0_ = bf16[128,1536]{1,0:T(8,128)(2,1)S(1)} collective-permute-done((bf16[128,1536]{1,0:T(8,128)(2,1)S(1)}, bf16[128,1536]{1,0:T(8,128)(2,1)S(1)}, u32[]{:S(2)}, u32[]{:S(2)}) %collective-permute-start.7) | collective-permute-done | bytes 393248 | tf_op jit(solution)/shard_map/ppermute | solution.py:597
  59.5 1.4 %last_sums.1 = bf16[128,4096]{1,0:T(8,128)(2,1)} custom-call(f32[128,4096]{1,0:T(8,128)S(1)} %project_kept.1.kept, bf16[128,1536]{1,0:T(8,128)(2,1)S(1)} %get-tuple-element.61.third, bf16[128,4096]{1,0:T(8,128)(2,1)} %get-tuple-element.62.filled), custom_call_target="tpu_custom_call", output_to_operand_aliasing={{}: (2, {})} | custom-call | tf_op jit(solution)/shard_map/last_sums/pallas_call | solution.py:502
  (36 shorter events, 2.3 us)
Async XLA Ops:
  0.0 5.9 %copy-start = (f32[512,1024]{1,0:T(8,128)S(1)}, f32[512,1024]{1,0:T(8,128)}, u32[]{:S(2)}) copy-start(f32[512,1024]{1,0:T(8,128)} %x_ref.3) | copy-start | bytes 6291460
  0.0 5.9 %copy-start.1 = (f32[512,1,128]{2,1,0:T(1,128)S(1)}, f32[512,1,128]{2,1,0:T(1,128)}, u32[]{:S(2)}) copy-start(f32[512,1,128]{2,1,0:T(1,128)} %param.13) | copy-start | bytes 786436
  0.0 21.5 %copy-start.7 = (f32[16]{0:T(128)S(1)}, f32[16]{0:T(128)}, u32[]{:S(2)}) copy-start(f32[16]{0:T(128)} %param.15) | copy-start | bytes 196
  2.9 18.6 %copy-start.2 = (f32[512,1,128]{2,1,0:T(1,128)S(1)}, f32[512,1,128]{2,1,0:T(1,128)}, u32[]{:S(2)}) copy-start(f32[512,1,128]{2,1,0:T(1,128)} %param.14) | copy-start | bytes 786436
  2.9 6.8 %collective-permute-start = (bf16[528,128]{1,0:T(8,128)(2,1)}, bf16[528,128]{1,0:T(8,128)(2,1)S(1)}, u32[]{:S(2)}, u32[]{:S(2)}) collective-permute-start(bf16[528,128]{1,0:T(8,128)(2,1)} %get-tuple-element.38), channel_id=1, source_target_pairs={{0,4},{4,0},{8,12},{12,8},{16,20},{20,16},{24,28},{28,24},{1,5},{5... | collective-permute-start | bytes 405512 | tf_op jit(solution)/shard_map/ppermute | solution.py:251
  5.9 0.8 %copy-start.3 = (bf16[32,640]{1,0:T(8,128)(2,1)S(1)}, bf16[32,640]{1,0:T(8,128)(2,1)}, u32[]{:S(2)}) copy-start(bf16[32,640]{1,0:T(8,128)(2,1)} %get-tuple-element.37.wk) | copy-start | bytes 122884
  6.7 14.8 %copy-start.5 = (bf16[512,1024]{1,0:T(8,128)(2,1)S(1)}, bf16[512,1024]{1,0:T(8,128)(2,1)}, u32[]{:S(2)}) copy-start(bf16[512,1024]{1,0:T(8,128)(2,1)} %gate_ref.3) | copy-start | bytes 3145732
  6.7 14.8 %copy-start.6 = (f32[4,48,128]{2,1,0:T(8,128)S(1)}, f32[4,48,128]{2,1,0:T(8,128)}, u32[]{:S(2)}) copy-start(f32[4,48,128]{2,1,0:T(8,128)} %get-tuple-element.51.aux) | copy-start | bytes 294916
  9.8 6.3 %collective-permute-start.1 = (bf16[528,128]{1,0:T(8,128)(2,1)S(1)}, bf16[528,128]{1,0:T(8,128)(2,1)S(1)}, u32[]{:S(2)}, u32[]{:S(2)}) collective-permute-start(bf16[528,128]{1,0:T(8,128)(2,1)S(1)} %join_pair.1.later), channel_id=1, source_target_pairs={{0,8},{4,12},{8,16},{12,20},{16,24},{20,28},{1,9},{5,13},{9,17},{1... | collective-permute-start | bytes 405512 | tf_op jit(solution)/shard_map/ppermute | solution.py:255
  16.1 8.7 %collective-permute-start.2 = (bf16[528,128]{1,0:T(8,128)(2,1)S(1)}, bf16[528,128]{1,0:T(8,128)(2,1)S(1)}, u32[]{:S(2)}, u32[]{:S(2)}) collective-permute-start(bf16[528,128]{1,0:T(8,128)(2,1)S(1)} %join_run.1), channel_id=1, source_target_pairs={{0,16},{4,20},{8,24},{12,28},{1,17},{5,21},{9,25},{13,29},{2,18},{... | collective-permute-start | bytes 405512 | tf_op jit(solution)/shard_map/ppermute | solution.py:255
  21.5 8.6 %slice-start = ((s8[8388608]{0:T(1024)(128)(4,1)}), s8[4194304]{0:T(1024)(128)(4,1)S(1)}, s32[]{:S(2)}) async-start(s8[8388608]{0:T(1024)(128)(4,1)} %bitcast.6), calls=%async_computation | async-start | bytes 8388608
  21.6 8.6 %slice-start.1 = ((s8[8388608]{0:T(1024)(128)(4,1)}), s8[4194304]{0:T(1024)(128)(4,1)S(1)}, s32[]{:S(2)}) async-start(s8[8388608]{0:T(1024)(128)(4,1)} %bitcast.6), calls=%async_computation.1 | async-start | bytes 8388608
  21.6 8.5 %copy-start.4 = (f32[1024]{0:T(1024)S(1)}, f32[1024]{0:T(1024)}, u32[]{:S(2)}) copy-start(f32[1024]{0:T(1024)} %param.16) | copy-start | bytes 12292
  25.1 5.0 %collective-permute-start.3 = (bf16[512,128]{1,0:T(8,128)(2,1)S(1)}, bf16[512,128]{1,0:T(8,128)(2,1)S(1)}, u32[]{:S(2)}, u32[]{:S(2)}) collective-permute-start(bf16[512,128]{1,0:T(8,128)(2,1)S(1)} %get-tuple-element.43), channel_id=1, source_target_pairs={{0,4},{4,0},{8,12},{12,8},{16,20},{20,16},{24,28},{28,24},{1,5},{5... | collective-permute-start | bytes 393224 | tf_op jit(solution)/shard_map/ppermute | solution.py:264
  31.2 1.6 %collective-permute-start.4 = (bf16[128,1024]{1,0:T(8,128)(2,1)S(1)}, bf16[128,1024]{1,0:T(8,128)(2,1)S(1)}, u32[]{:S(2)}, u32[]{:S(2)}) collective-permute-start(bf16[128,1024]{1,0:T(8,128)(2,1)S(1)} %get-tuple-element.46), channel_id=1, source_target_pairs={{0,1},{1,0},{2,3},{3,2},{4,5},{5,4},{6,7},{7,6},{8,9},{9,8},{10,11... | collective-permute-start | bytes 786440 | tf_op jit(solution)/shard_map/ppermute | solution.py:555
  33.9 4.9 %collective-permute-start.5 = (bf16[128,1536]{1,0:T(8,128)(2,1)S(1)}, bf16[128,1536]{1,0:T(8,128)(2,1)S(1)}, u32[]{:S(2)}, u32[]{:S(2)}) collective-permute-start(bf16[128,1536]{1,0:T(8,128)(2,1)S(1)} %get-tuple-element.49), channel_id=1, source_target_pairs={{0,1},{1,0},{2,3},{3,2},{4,5},{5,4},{6,7},{7,6},{8,9},{9,8},{10,11... | collective-permute-start | bytes 1179656 | tf_op jit(solution)/shard_map/ppermute | solution.py:555
  34.1 9.1 %collective-permute-start.9 = (bf16[128,1024]{1,0:T(8,128)(2,1)S(1)}, bf16[128,1024]{1,0:T(8,128)(2,1)S(1)}, u32[]{:S(2)}, u32[]{:S(2)}) collective-permute-start(bf16[128,1024]{1,0:T(8,128)(2,1)S(1)} %add_pair.3), channel_id=1, source_target_pairs={{0,2},{1,3},{2,0},{3,1},{4,6},{5,7},{6,4},{7,5},{8,10},{9,11},{10,... | collective-permute-start | bytes 786440 | tf_op jit(solution)/shard_map/ppermute | solution.py:594
  38.9 12.8 %collective-permute-start.8 = (bf16[128,1536]{1,0:T(8,128)(2,1)S(1)}, bf16[128,1536]{1,0:T(8,128)(2,1)S(1)}, u32[]{:S(2)}, u32[]{:S(2)}) collective-permute-start(bf16[128,1536]{1,0:T(8,128)(2,1)S(1)} %add_pair.4), channel_id=1, source_target_pairs={{0,2},{1,3},{2,0},{3,1},{4,6},{5,7},{6,4},{7,5},{8,10},{9,11},{10,... | collective-permute-start | bytes 1179656 | tf_op jit(solution)/shard_map/ppermute | solution.py:595
  41.9 3.3 %collective-permute-start.6 = (bf16[128,5632]{1,0:T(8,128)(2,1)S(1)}, bf16[128,5632]{1,0:T(8,128)(2,1)S(1)}, u32[]{:S(2)}, u32[]{:S(2)}) collective-permute-start(bf16[128,5632]{1,0:T(8,128)(2,1)S(1)} %get-tuple-element.55), channel_id=1, source_target_pairs={{0,1},{1,0},{2,3},{3,2},{4,5},{5,4},{6,7},{7,6},{8,9},{9,8},{10,11... | collective-permute-start | bytes 4325384 | tf_op jit(solution)/shard_map/ppermute | solution.py:555
  45.3 14.2 %collective-permute-start.7 = (bf16[128,1536]{1,0:T(8,128)(2,1)S(1)}, bf16[128,1536]{1,0:T(8,128)(2,1)S(1)}, u32[]{:S(2)}, u32[]{:S(2)}) collective-permute-start(bf16[128,1536]{1,0:T(8,128)(2,1)S(1)} %add_pair.5), channel_id=1, source_target_pairs={{0,2},{1,3},{2,0},{3,1},{4,6},{5,7},{6,4},{7,5},{8,10},{9,11},{10,... | collective-permute-start | bytes 1179656 | tf_op jit(solution)/shard_map/ppermute | solution.py:597
where the time goes:
time: 61.2 us; the launch traced here: 61 us
  waiting for transfers between devices  23.1 us (38%)
  Pallas kernels  19.1 us (31%)
  starting transfers between devices  17.7 us (29%)
  local copies, waits for them, and re-layouts  0.82 us (1%)
    ppermute x2, starting transfers between devices, incoming_states(): lax.ppermute(run, 'seq', [(s, s + distance) for s in range(count - distan...  9.11 us
    pallas_call x2, Pallas kernels, within(): pl.pallas_call(functools.partial(within_kernel, far), in_specs=[VMEM] * 6...  6.38 us
    pallas_call x7, Pallas kernels, local_call(): pl.pallas_call(kernel, in_specs=[VMEM] * len(operands), out_specs=[VMEM]...  6.06 us
    ppermute x1, waiting for transfers between devices, per_device(): third, filled = await_piece(lax.ppermute(third, 'head', far), filled)  5.58 us
    ppermute x1, waiting for transfers between devices, per_device(): second, first = await_piece(lax.ppermute(second, 'head', far), first)  4.75 us
    ppermute x3, waiting for transfers between devices, add(): come = lax.ppermute(theirs, 'head', near)  3.53 us
    ppermute x1, waiting for transfers between devices, incoming_states(): return (hold, mine, lax.ppermute(theirs, 'seq', pair))  3.48 us
    ppermute x1, starting transfers between devices, incoming_states(): come = lax.ppermute(give, 'seq', pair)  3.01 us
  transfers between devices with their start and end apart: 10, of which 8 were waited for; matrix products, arithmetic and copies ran while one was open for 0% of the time, Pallas kernels for 20%

commit v1 on v0

--- a/solution.py
+++ b/solution.py
@@ -491,25 +491,34 @@
     )(kept, first, second)
 
 
-def last_kernel(kept, third, filled, out):
-    out[...] = (kept[...] + third[...].astype(F32)).astype(BF)
+def last_kernel(kept, third, filled, out, part, sems):
+    wide = third.shape[1]
+    start = kept.shape[1] - wide
+    block = wide // 2
+    stores = []
+    for k in range(2):
+        cut = slice(k * block, (k + 1) * block)
+        part[:, cut] = (
+            kept[:, start + k * block:start + (k + 1) * block] + third[:, cut].astype(F32)
+        ).astype(BF)
+        stores.append(
+            pltpu.make_async_copy(
+                part.at[:, cut], out.at[:, start + k * block:start + (k + 1) * block], sems.at[k]
+            )
+        )
+        stores[k].start()
+    for store in stores:
+        store.wait()
 
 
 def last_sums(kept, third, filled):
-    rows, wide = third.shape
-    block = 512
-    start = (kept.shape[1] - wide) // block
     return pl.pallas_call(
         last_kernel,
-        grid=(wide // block,),
-        in_specs=[
-            pl.BlockSpec((rows, block), lambda j: (0, j + start)),
-            pl.BlockSpec((rows, block), lambda j: (0, j)),
-            pl.BlockSpec(memory_space=pl.ANY),
-        ],
-        out_specs=pl.BlockSpec((rows, block), lambda j: (0, j + start)),
+        in_specs=[VMEM, VMEM, pl.BlockSpec(memory_space=pl.ANY)],
+        out_specs=pl.BlockSpec(memory_space=pl.ANY),
         out_shape=jax.ShapeDtypeStruct(kept.shape, BF),
         input_output_aliases={2: 0},
+        scratch_shapes=[pltpu.VMEM(third.shape, BF), pltpu.SemaphoreType.DMA((2,))],
         compiler_params=pltpu.CompilerParams(vmem_limit_bytes=VMEM_LIMIT),
         name="last_sums",
     )(kept, third, filled)
@@ -564,7 +573,7 @@
         4 * rows * channels * one,
     )
     first, _ = add(mine, theirs)
-    normed, aux, first = lax.optimization_barrier((normed, aux, first))
+    aux, first = lax.optimization_barrier((aux, first))
     theirs, mine = local_call(
         functools.partial(more_kernel, start2, two),
         (normed, out_weight),

time: 61.2 us -> 59.3 us (0.969)
  waiting for transfers between devices: 23.1 us -> 21.3 us
    ppermute x3, waiting for transfers between devices: 3.53 us -> 2 us  [add(): come = lax.ppermute(theirs, 'head', near)]
    pallas_call x1, Pallas kernels: 1.44 us -> 0.79 us  [last_sums(): pl.pallas_call(last_kernel, in_specs=[VMEM, VMEM, pl.BlockSpec(memory_spa...]
  transfers between devices with their start and end apart: 10 -> 10, of which waited for: 8 -> 7; matrix products, arithmetic and copies ran while one was open for 0% -> 0% of each run, Pallas kernels for 20% -> 23%
where the time goes in v1:
time: 59.3 us; the launch traced here: 59.1 us
  waiting for transfers between devices  21.3 us (36%)
  Pallas kernels  18.5 us (31%)
  starting transfers between devices  18.1 us (31%)
  local copies, waits for them, and re-layouts  0.82 us (1%)
    ppermute x2, starting transfers between devices, incoming_states(): lax.ppermute(run, 'seq', [(s, s + distance) for s in range(count - distan...  9.11 us
    pallas_call x2, Pallas kernels, within(): pl.pallas_call(functools.partial(within_kernel, far), in_specs=[VMEM] * 6...  6.38 us
    pallas_call x7, Pallas kernels, local_call(): pl.pallas_call(kernel, in_specs=[VMEM] * len(operands), out_specs=[VMEM]...  6.07 us
    ppermute x1, waiting for transfers between devices, per_device(): third, filled = await_piece(lax.ppermute(third, 'head', far), filled)  5.31 us
    ppermute x1, waiting for transfers between devices, per_device(): second, first = await_piece(lax.ppermute(second, 'head', far), first)  4.79 us
    ppermute x1, waiting for transfers between devices, incoming_states(): return (hold, mine, lax.ppermute(theirs, 'seq', pair))  3.48 us
    ppermute x1, starting transfers between devices, incoming_states(): come = lax.ppermute(give, 'seq', pair)  3.01 us
    pallas_call x1, Pallas kernels, give_states(): pl.pallas_call(give_kernel, in_specs=[HBM] * 4, out_shape=[jax.ShapeDtype...  2.9 us
  transfers between devices with their start and end apart: 10, of which 7 were waited for; matrix products, arithmetic and copies ran while one was open for 0% of the time, Pallas kernels for 23%

profile of v1, /device:TPU:0, one launch (start us, length us, event | category | flops | bytes accessed | tf_op | source)
XLA Modules:
  0.0 59.1 jit_solution(2788806712437767120)
XLA Ops:
  0.0 2.9 %give_states.1 = (bf16[528,128]{1,0:T(8,128)(2,1)}, bf16[32,640]{1,0:T(8,128)(2,1)}, f32[4,48,128]{2,1,0:T(8,128)}) custom-call(f32[16,512]{1,0:T(8,128)} %bitcast.20, f32[1,16]{1,0:T(1,128)} %bitcast.21, f32[512,1024]{1,0:T(8,128)} %x_ref.3, f32[512,128]{1,0:T(8,128)} %bitcast.8), custom_call_target="tpu_custom_call" | custom-call | flops 200000000 | bytes 1500000 | tf_op jit(solution)/shard_map/give_states/pallas_call | solution.py:157
  2.9 3.0 %collective-permute-start = (bf16[528,128]{1,0:T(8,128)(2,1)}, bf16[528,128]{1,0:T(8,128)(2,1)S(1)}, u32[]{:S(2)}, u32[]{:S(2)}) collective-permute-start(bf16[528,128]{1,0:T(8,128)(2,1)} %get-tuple-element.37), channel_id=1, source_target_pairs={{0,4},{4,0},{8,12},{12,8},{16,20},{20,16},{24,28},{28,24},{1,5},{5... | collective-permute-start | bytes 405512 | tf_op jit(solution)/shard_map/ppermute | solution.py:251
  5.9 0.8 %copy-done.3 = bf16[32,640]{1,0:T(8,128)(2,1)S(1)} copy-done((bf16[32,640]{1,0:T(8,128)(2,1)S(1)}, bf16[32,640]{1,0:T(8,128)(2,1)}, u32[]{:S(2)}) %copy-start.3) | copy-done | bytes 40984
  6.7 1.0 %keep_states.1.own = bf16[528,128]{1,0:T(8,128)(2,1)S(1)} custom-call(bf16[32,640]{1,0:T(8,128)(2,1)S(1)} %copy-done.3, f32[512,1024]{1,0:T(8,128)S(1)} %copy-done, f32[512,128]{1,0:T(8,128)S(1)} %bitcast.9), custom_call_target="tpu_custom_call" | custom-call | flops 200000000 | bytes 1500000 | tf_op jit(solution)/shard_map/keep_states/pallas_call | solution.py:181
  7.7 2.0 %collective-permute-done.come = bf16[528,128]{1,0:T(8,128)(2,1)S(1)} collective-permute-done((bf16[528,128]{1,0:T(8,128)(2,1)}, bf16[528,128]{1,0:T(8,128)(2,1)S(1)}, u32[]{:S(2)}, u32[]{:S(2)}) %collective-permute-start) | collective-permute-done | bytes 135200 | tf_op jit(solution)/shard_map/ppermute | solution.py:251
  9.8 3.7 %collective-permute-start.1 = (bf16[528,128]{1,0:T(8,128)(2,1)S(1)}, bf16[528,128]{1,0:T(8,128)(2,1)S(1)}, u32[]{:S(2)}, u32[]{:S(2)}) collective-permute-start(bf16[528,128]{1,0:T(8,128)(2,1)S(1)} %join_pair.1.later), channel_id=1, source_target_pairs={{0,8},{4,12},{8,16},{12,20},{16,24},{20,28},{1,9},{5,13},{9,17},{1... | collective-permute-start | bytes 405512 | tf_op jit(solution)/shard_map/ppermute | solution.py:255
  13.5 2.5 %collective-permute-done.1.earlier.last = bf16[528,128]{1,0:T(8,128)(2,1)S(1)} collective-permute-done((bf16[528,128]{1,0:T(8,128)(2,1)S(1)}, bf16[528,128]{1,0:T(8,128)(2,1)S(1)}, u32[]{:S(2)}, u32[]{:S(2)}) %collective-permute-start.1) | collective-permute-done | bytes 135200 | tf_op jit(solution)/shard_map/ppermute | solution.py:255
  16.1 5.4 %collective-permute-start.2 = (bf16[528,128]{1,0:T(8,128)(2,1)S(1)}, bf16[528,128]{1,0:T(8,128)(2,1)S(1)}, u32[]{:S(2)}, u32[]{:S(2)}) collective-permute-start(bf16[528,128]{1,0:T(8,128)(2,1)S(1)} %join_run.1), channel_id=1, source_target_pairs={{0,16},{4,20},{8,24},{12,28},{1,17},{5,21},{9,25},{13,29},{2,18},{... | collective-permute-start | bytes 405512 | tf_op jit(solution)/shard_map/ppermute | solution.py:255
  21.6 3.2 %within_far.1 = (f32[256,1024]{1,0:T(8,128)S(1)}, f32[256,1024]{1,0:T(8,128)S(1)}) custom-call(f32[4,48,128]{2,1,0:T(8,128)S(1)} %copy-done.6, f32[512,1024]{1,0:T(8,128)S(1)} %copy-done, f32[512,128]{1,0:T(8,128)S(1)} %bitcast.10, f32[512,128]{1,0:T(8,128)S(1)} %bitcast.12, bf16[512,1024]{1,0:T(8,128)(2,1)S(1)} %copy-done.5, f32[1,16]{1,0:T(1,128)S(1)} %bitcast.18), custom_call_target="tpu_custom_call" | custom-call | flops 4000000000 | bytes 3000000 | tf_op jit(solution)/shard_map/within_far/pallas_call | solution.py:358
  25.1 1.6 %collective-permute-start.3 = (bf16[512,128]{1,0:T(8,128)(2,1)S(1)}, bf16[512,128]{1,0:T(8,128)(2,1)S(1)}, u32[]{:S(2)}, u32[]{:S(2)}) collective-permute-start(bf16[512,128]{1,0:T(8,128)(2,1)S(1)} %get-tuple-element.42), channel_id=1, source_target_pairs={{0,4},{4,0},{8,12},{12,8},{16,20},{20,16},{24,28},{28,24},{1,5},{5... | collective-permute-start | bytes 393224 | tf_op jit(solution)/shard_map/ppermute | solution.py:264
  26.6 3.5 %collective-permute-done.3.there = bf16[512,128]{1,0:T(8,128)(2,1)S(1)} collective-permute-done((bf16[512,128]{1,0:T(8,128)(2,1)S(1)}, bf16[512,128]{1,0:T(8,128)(2,1)S(1)}, u32[]{:S(2)}, u32[]{:S(2)}) %collective-permute-start.3) | collective-permute-done | bytes 131104 | tf_op jit(solution)/shard_map/ppermute | solution.py:264
  30.1 1.1 %finish_far.1 = (bf16[128,1024]{1,0:T(8,128)(2,1)S(1)}, f32[128,1024]{1,0:T(8,128)S(1)}, bf16[256,1024]{1,0:T(8,128)(2,1)S(1)}) custom-call(f32[256,1024]{1,0:T(8,128)S(1)} %get-tuple-element.38.own, f32[256,1024]{1,0:T(8,128)S(1)} %get-tuple-element.39.lead, f32[512,128]{1,0:T(8,128)S(1)} %bitcast.13, bf16[512,128]{1,0:T(8,128)(2,1)S(1)} %get-tuple-element.41.here, ...), custom_call_target="tpu_custom_call" | custom-call | flops 536870912 | tf_op jit(solution)/shard_map/finish_far/pallas_call | solution.py:440
  31.3 1.0 %project_more.1 = (bf16[128,1536]{1,0:T(8,128)(2,1)S(1)}, f32[128,1536]{1,0:T(8,128)S(1)}) custom-call(bf16[256,1024]{1,0:T(8,128)(2,1)S(1)} %get-tuple-element.46.normed, bf16[1024,4096]{1,0:T(8,128)(2,1)S(1)} %bitcast.7), custom_call_target="tpu_custom_call" | custom-call | flops 805306368 | tf_op jit(solution)/shard_map/project_more/pallas_call | solution.py:440
  32.9 1.6 %collective-permute-start.9 = (bf16[128,1024]{1,0:T(8,128)(2,1)S(1)}, bf16[128,1024]{1,0:T(8,128)(2,1)S(1)}, u32[]{:S(2)}, u32[]{:S(2)}) collective-permute-start(bf16[128,1024]{1,0:T(8,128)(2,1)S(1)} %add_pair.4), channel_id=1, source_target_pairs={{0,2},{1,3},{2,0},{3,1},{4,6},{5,7},{6,4},{7,5},{8,10},{9,11},{10,... | collective-permute-start | bytes 786440 | tf_op jit(solution)/shard_map/ppermute | solution.py:603
  34.5 3.2 %within_near.1 = (f32[256,1024]{1,0:T(8,128)S(1)}, f32[256,1024]{1,0:T(8,128)S(1)}) custom-call(f32[4,48,128]{2,1,0:T(8,128)S(1)} %copy-done.6, f32[512,1024]{1,0:T(8,128)S(1)} %copy-done, f32[512,128]{1,0:T(8,128)S(1)} %bitcast.11, f32[512,128]{1,0:T(8,128)S(1)} %bitcast.14, bf16[512,1024]{1,0:T(8,128)(2,1)S(1)} %copy-done.5, f32[1,16]{1,0:T(1,128)S(1)} %bitcast.19), custom_call_target="tpu_custom_call" | custom-call | flops 4000000000 | bytes 3000000 | tf_op jit(solution)/shard_map/within_near/pallas_call | solution.py:358
  38.4 2.5 %finish_near.1 = (bf16[128,5632]{1,0:T(8,128)(2,1)S(1)}, f32[128,1536]{1,0:T(8,128)S(1)}, bf16[128,1024]{1,0:T(8,128)(2,1)S(1)}) custom-call(bf16[256,1024]{1,0:T(8,128)(2,1)S(1)} %get-tuple-element.46.normed, f32[256,1024]{1,0:T(8,128)S(1)} %get-tuple-element.50.own, f32[256,1024]{1,0:T(8,128)S(1)} %get-tuple-element.51.lead, f32[512,128]{1,0:T(8,128)S(1)} %bitcast.15, ...), custom_call_target="tpu_custom_call" | custom-call | flops 1879048192 | tf_op jit(solution)/shard_map/finish_near/pallas_call | solution.py:440
  40.9 1.2 %collective-permute-done.9.refs_0_ = bf16[128,1024]{1,0:T(8,128)(2,1)S(1)} collective-permute-done((bf16[128,1024]{1,0:T(8,128)(2,1)S(1)}, bf16[128,1024]{1,0:T(8,128)(2,1)S(1)}, u32[]{:S(2)}, u32[]{:S(2)}) %collective-permute-start.9) | collective-permute-done | bytes 262176 | tf_op jit(solution)/shard_map/ppermute | solution.py:603
  42.1 2.0 %collective-permute-done.6.come = bf16[128,5632]{1,0:T(8,128)(2,1)S(1)} collective-permute-done((bf16[128,5632]{1,0:T(8,128)(2,1)S(1)}, bf16[128,5632]{1,0:T(8,128)(2,1)S(1)}, u32[]{:S(2)}, u32[]{:S(2)}) %collective-permute-start.6) | collective-permute-done | bytes 1441824 | tf_op jit(solution)/shard_map/ppermute | solution.py:564
  44.2 1.6 %collective-permute-start.7 = (bf16[128,1536]{1,0:T(8,128)(2,1)S(1)}, bf16[128,1536]{1,0:T(8,128)(2,1)S(1)}, u32[]{:S(2)}, u32[]{:S(2)}) collective-permute-start(bf16[128,1536]{1,0:T(8,128)(2,1)S(1)} %add_pair.5), channel_id=1, source_target_pairs={{0,2},{1,3},{2,0},{3,1},{4,6},{5,7},{6,4},{7,5},{8,10},{9,11},{10,... | collective-permute-start | bytes 1179656 | tf_op jit(solution)/shard_map/ppermute | solution.py:606
  45.8 4.8 %collective-permute-done.8.refs_0_ = bf16[128,1536]{1,0:T(8,128)(2,1)S(1)} collective-permute-done((bf16[128,1536]{1,0:T(8,128)(2,1)S(1)}, bf16[128,1536]{1,0:T(8,128)(2,1)S(1)}, u32[]{:S(2)}, u32[]{:S(2)}) %collective-permute-start.8) | collective-permute-done | bytes 393248 | tf_op jit(solution)/shard_map/ppermute | solution.py:604
  50.6 1.3 %project_kept.1.kept = f32[128,4096]{1,0:T(8,128)S(1)} custom-call(bf16[128,1024]{1,0:T(8,128)(2,1)S(1)} %get-tuple-element.52.kept, bf16[128,5632]{1,0:T(8,128)(2,1)S(1)} %collective-permute-done.6.come, bf16[1024,4096]{1,0:T(8,128)(2,1)S(1)} %bitcast.7), custom_call_target="tpu_custom_call" | custom-call | flops 1073741824 | tf_op jit(solution)/shard_map/project_kept/pallas_call | solution.py:440
  51.9 0.9 %early_sums.1.refs_1_ = bf16[128,4096]{1,0:T(8,128)(2,1)} custom-call(f32[128,4096]{1,0:T(8,128)S(1)} %project_kept.1.kept, bf16[128,1024]{1,0:T(8,128)(2,1)S(1)} %get-tuple-element.57.first, bf16[128,1536]{1,0:T(8,128)(2,1)S(1)} %get-tuple-element.58.second), custom_call_target="tpu_custom_call" | custom-call | tf_op jit(solution)/shard_map/early_sums/pallas_call | solution.py:483
  52.9 5.3 %collective-permute-done.7.refs_0_ = bf16[128,1536]{1,0:T(8,128)(2,1)S(1)} collective-permute-done((bf16[128,1536]{1,0:T(8,128)(2,1)S(1)}, bf16[128,1536]{1,0:T(8,128)(2,1)S(1)}, u32[]{:S(2)}, u32[]{:S(2)}) %collective-permute-start.7) | collective-permute-done | bytes 393248 | tf_op jit(solution)/shard_map/ppermute | solution.py:606
  58.2 0.8 %last_sums.1 = bf16[128,4096]{1,0:T(8,128)(2,1)} custom-call(f32[128,4096]{1,0:T(8,128)S(1)} %project_kept.1.kept, bf16[128,1536]{1,0:T(8,128)(2,1)S(1)} %get-tuple-element.59.third, bf16[128,4096]{1,0:T(8,128)(2,1)} %get-tuple-element.60.filled), custom_call_target="tpu_custom_call", output_to_operand_aliasing={{}: (2, {})} | custom-call | tf_op jit(solution)/shard_map/last_sums/pallas_call | solution.py:515
  (36 shorter events, 1.9 us)
Async XLA Ops:
  0.0 5.9 %copy-start = (f32[512,1024]{1,0:T(8,128)S(1)}, f32[512,1024]{1,0:T(8,128)}, u32[]{:S(2)}) copy-start(f32[512,1024]{1,0:T(8,128)} %x_ref.3) | copy-start | bytes 6291460
  0.0 5.9 %copy-start.1 = (f32[512,1,128]{2,1,0:T(1,128)S(1)}, f32[512,1,128]{2,1,0:T(1,128)}, u32[]{:S(2)}) copy-start(f32[512,1,128]{2,1,0:T(1,128)} %param.13) | copy-start | bytes 786436
  0.0 21.5 %copy-start.7 = (f32[16]{0:T(128)S(1)}, f32[16]{0:T(128)}, u32[]{:S(2)}) copy-start(f32[16]{0:T(128)} %param.15) | copy-start | bytes 196
  2.9 18.6 %copy-start.2 = (f32[512,1,128]{2,1,0:T(1,128)S(1)}, f32[512,1,128]{2,1,0:T(1,128)}, u32[]{:S(2)}) copy-start(f32[512,1,128]{2,1,0:T(1,128)} %param.14) | copy-start | bytes 786436
  2.9 6.8 %collective-permute-start = (bf16[528,128]{1,0:T(8,128)(2,1)}, bf16[528,128]{1,0:T(8,128)(2,1)S(1)}, u32[]{:S(2)}, u32[]{:S(2)}) collective-permute-start(bf16[528,128]{1,0:T(8,128)(2,1)} %get-tuple-element.37), channel_id=1, source_target_pairs={{0,4},{4,0},{8,12},{12,8},{16,20},{20,16},{24,28},{28,24},{1,5},{5... | collective-permute-start | bytes 405512 | tf_op jit(solution)/shard_map/ppermute | solution.py:251
  5.9 0.8 %copy-start.3 = (bf16[32,640]{1,0:T(8,128)(2,1)S(1)}, bf16[32,640]{1,0:T(8,128)(2,1)}, u32[]{:S(2)}) copy-start(bf16[32,640]{1,0:T(8,128)(2,1)} %get-tuple-element.36.wk) | copy-start | bytes 122884
  6.7 14.8 %copy-start.5 = (bf16[512,1024]{1,0:T(8,128)(2,1)S(1)}, bf16[512,1024]{1,0:T(8,128)(2,1)}, u32[]{:S(2)}) copy-start(bf16[512,1024]{1,0:T(8,128)(2,1)} %gate_ref.3) | copy-start | bytes 3145732
  6.7 14.8 %copy-start.6 = (f32[4,48,128]{2,1,0:T(8,128)S(1)}, f32[4,48,128]{2,1,0:T(8,128)}, u32[]{:S(2)}) copy-start(f32[4,48,128]{2,1,0:T(8,128)} %get-tuple-element.49.aux) | copy-start | bytes 294916
  9.8 6.3 %collective-permute-start.1 = (bf16[528,128]{1,0:T(8,128)(2,1)S(1)}, bf16[528,128]{1,0:T(8,128)(2,1)S(1)}, u32[]{:S(2)}, u32[]{:S(2)}) collective-permute-start(bf16[528,128]{1,0:T(8,128)(2,1)S(1)} %join_pair.1.later), channel_id=1, source_target_pairs={{0,8},{4,12},{8,16},{12,20},{16,24},{20,28},{1,9},{5,13},{9,17},{1... | collective-permute-start | bytes 405512 | tf_op jit(solution)/shard_map/ppermute | solution.py:255
  16.1 8.7 %collective-permute-start.2 = (bf16[528,128]{1,0:T(8,128)(2,1)S(1)}, bf16[528,128]{1,0:T(8,128)(2,1)S(1)}, u32[]{:S(2)}, u32[]{:S(2)}) collective-permute-start(bf16[528,128]{1,0:T(8,128)(2,1)S(1)} %join_run.1), channel_id=1, source_target_pairs={{0,16},{4,20},{8,24},{12,28},{1,17},{5,21},{9,25},{13,29},{2,18},{... | collective-permute-start | bytes 405512 | tf_op jit(solution)/shard_map/ppermute | solution.py:255
  21.5 8.6 %slice-start = ((s8[8388608]{0:T(1024)(128)(4,1)}), s8[4194304]{0:T(1024)(128)(4,1)S(1)}, s32[]{:S(2)}) async-start(s8[8388608]{0:T(1024)(128)(4,1)} %bitcast.6), calls=%async_computation | async-start | bytes 8388608
  21.6 8.6 %slice-start.1 = ((s8[8388608]{0:T(1024)(128)(4,1)}), s8[4194304]{0:T(1024)(128)(4,1)S(1)}, s32[]{:S(2)}) async-start(s8[8388608]{0:T(1024)(128)(4,1)} %bitcast.6), calls=%async_computation.1 | async-start | bytes 8388608
  21.6 8.5 %copy-start.4 = (f32[1024]{0:T(1024)S(1)}, f32[1024]{0:T(1024)}, u32[]{:S(2)}) copy-start(f32[1024]{0:T(1024)} %param.16) | copy-start | bytes 12292
  25.1 5.0 %collective-permute-start.3 = (bf16[512,128]{1,0:T(8,128)(2,1)S(1)}, bf16[512,128]{1,0:T(8,128)(2,1)S(1)}, u32[]{:S(2)}, u32[]{:S(2)}) collective-permute-start(bf16[512,128]{1,0:T(8,128)(2,1)S(1)} %get-tuple-element.42), channel_id=1, source_target_pairs={{0,4},{4,0},{8,12},{12,8},{16,20},{20,16},{24,28},{28,24},{1,5},{5... | collective-permute-start | bytes 393224 | tf_op jit(solution)/shard_map/ppermute | solution.py:264
  31.2 1.6 %collective-permute-start.5 = (bf16[128,1024]{1,0:T(8,128)(2,1)S(1)}, bf16[128,1024]{1,0:T(8,128)(2,1)S(1)}, u32[]{:S(2)}, u32[]{:S(2)}) collective-permute-start(bf16[128,1024]{1,0:T(8,128)(2,1)S(1)} %get-tuple-element.48), channel_id=1, source_target_pairs={{0,1},{1,0},{2,3},{3,2},{4,5},{5,4},{6,7},{7,6},{8,9},{9,8},{10,11... | collective-permute-start | bytes 786440 | tf_op jit(solution)/shard_map/ppermute | solution.py:564
  32.3 5.4 %collective-permute-start.4 = (bf16[128,1536]{1,0:T(8,128)(2,1)S(1)}, bf16[128,1536]{1,0:T(8,128)(2,1)S(1)}, u32[]{:S(2)}, u32[]{:S(2)}) collective-permute-start(bf16[128,1536]{1,0:T(8,128)(2,1)S(1)} %get-tuple-element.45), channel_id=1, source_target_pairs={{0,1},{1,0},{2,3},{3,2},{4,5},{5,4},{6,7},{7,6},{8,9},{9,8},{10,11... | collective-permute-start | bytes 1179656 | tf_op jit(solution)/shard_map/ppermute | solution.py:564
  32.9 9.2 %collective-permute-start.9 = (bf16[128,1024]{1,0:T(8,128)(2,1)S(1)}, bf16[128,1024]{1,0:T(8,128)(2,1)S(1)}, u32[]{:S(2)}, u32[]{:S(2)}) collective-permute-start(bf16[128,1024]{1,0:T(8,128)(2,1)S(1)} %add_pair.4), channel_id=1, source_target_pairs={{0,2},{1,3},{2,0},{3,1},{4,6},{5,7},{6,4},{7,5},{8,10},{9,11},{10,... | collective-permute-start | bytes 786440 | tf_op jit(solution)/shard_map/ppermute | solution.py:603
  37.8 12.8 %collective-permute-start.8 = (bf16[128,1536]{1,0:T(8,128)(2,1)S(1)}, bf16[128,1536]{1,0:T(8,128)(2,1)S(1)}, u32[]{:S(2)}, u32[]{:S(2)}) collective-permute-start(bf16[128,1536]{1,0:T(8,128)(2,1)S(1)} %add_pair.3), channel_id=1, source_target_pairs={{0,2},{1,3},{2,0},{3,1},{4,6},{5,7},{6,4},{7,5},{8,10},{9,11},{10,... | collective-permute-start | bytes 1179656 | tf_op jit(solution)/shard_map/ppermute | solution.py:604
  40.8 3.3 %collective-permute-start.6 = (bf16[128,5632]{1,0:T(8,128)(2,1)S(1)}, bf16[128,5632]{1,0:T(8,128)(2,1)S(1)}, u32[]{:S(2)}, u32[]{:S(2)}) collective-permute-start(bf16[128,5632]{1,0:T(8,128)(2,1)S(1)} %get-tuple-element.53), channel_id=1, source_target_pairs={{0,1},{1,0},{2,3},{3,2},{4,5},{5,4},{6,7},{7,6},{8,9},{9,8},{10,11... | collective-permute-start | bytes 4325384 | tf_op jit(solution)/shard_map/ppermute | solution.py:564
  44.2 14.0 %collective-permute-start.7 = (bf16[128,1536]{1,0:T(8,128)(2,1)S(1)}, bf16[128,1536]{1,0:T(8,128)(2,1)S(1)}, u32[]{:S(2)}, u32[]{:S(2)}) collective-permute-start(bf16[128,1536]{1,0:T(8,128)(2,1)S(1)} %add_pair.5), channel_id=1, source_target_pairs={{0,2},{1,3},{2,0},{3,1},{4,6},{5,7},{6,4},{7,5},{8,10},{9,11},{10,... | collective-permute-start | bytes 1179656 | tf_op jit(solution)/shard_map/ppermute | solution.py:606

commit v2 on v1

--- a/solution.py
+++ b/solution.py
@@ -201,29 +201,58 @@
     out[len(ahead) * N:] = tail_rows([p * q for p, q in zip(ahead, behind)])
 
 
-def pair_kernel(own, come, out):
-    odd = lax.axis_index("seq") % 2
-
-    @pl.when(odd == 0)
+def is_later(distance):
+    return (lax.axis_index("seq") // distance) % 2
+
+
+def run_kernel(distance, own, come, out):
+    later = is_later(distance)
+
+    @pl.when(later == 0)
     def _():
         link(come, own, out)
 
-    @pl.when(odd == 1)
+    @pl.when(later == 1)
     def _():
         link(own, come, out)
 
 
-def end_kernel(last, before, own, come, mine, theirs):
+def first_ahead_kernel(distance, come, out):
+    later = is_later(distance)
+    rows = out.shape[0] - 16
+
+    @pl.when(later == 0)
+    def _():
+        out[:rows] = jnp.zeros((rows, LANES), BF)
+        out[rows:] = tail_rows([jnp.ones((1, LANES), F32)] * (rows // N))
+
+    @pl.when(later == 1)
+    def _():
+        out[...] = come[...]
+
+
+def ahead_kernel(distance, ahead, come, out):
+    later = is_later(distance)
+
+    @pl.when(later == 0)
+    def _():
+        out[...] = ahead[...]
+
+    @pl.when(later == 1)
+    def _():
+        link(ahead, come, out)
+
+
+def end_kernel(distance, ahead, last, own, come, mine, theirs):
     blocks = mine.shape[0] // N
-    odd = lax.axis_index("seq") % 2
+    weight = is_later(distance).astype(F32)
+    odd = is_later(1)
 
     def fill(even_section, ahead_ref, behind_ref):
-        step, span = decays_of(last), decays_of(even_section)
+        step, span = decays_of(ahead), decays_of(even_section)
         for k in range(blocks):
             rows = slice(k * N, (k + 1) * N)
-            start = last[rows].astype(F32)
-            if before is not None:
-                start = start + step[k] * before[rows].astype(F32)
+            start = ahead[rows].astype(F32) + (weight * step[k]) * last[rows].astype(F32)
             ahead_ref[rows] = start.astype(BF)
             behind_ref[rows] = (even_section[rows].astype(F32) + span[k] * start).astype(BF)
 
@@ -247,21 +276,28 @@
 
 
 def incoming_states(give, keep, count, hold):
-    pair = [(s, s ^ 1) for s in range(count)]
-    come = lax.ppermute(give, "seq", pair)
-    run = scan_call(pair_kernel, (keep, come), [keep.shape], "join_pair")[0]
-    start, distance = None, 2
-    while distance < count:
-        got = lax.ppermute(run, "seq", [(s, s + distance) for s in range(count - distance)])
-        if distance * 2 >= count:
-            break
-        run = scan_call(link, (run, got), [keep.shape], "join_run")[0]
-        start = got if start is None else scan_call(link, (start, got), [keep.shape], "join_start")[0]
-        distance *= 2
+    def exchange(value, distance):
+        return lax.ppermute(value, "seq", [(s, s ^ distance) for s in range(count)])
+
+    def joined(kernel, distance, *operands):
+        name = kernel.__name__[:-len("_kernel")]
+        return scan_call(functools.partial(kernel, distance), operands, [keep.shape], name)[0]
+
+    come = exchange(give, 1)
+    run, distance = joined(run_kernel, 1, keep, come), 2
+    got = exchange(run, distance)
+    ahead = joined(first_ahead_kernel, distance, got)
+    while distance * 2 < count:
+        run, distance = joined(run_kernel, distance, run, got), distance * 2
+        got = exchange(run, distance)
+        if distance * 2 < count:
+            ahead = joined(ahead_kernel, distance, ahead, got)
     hold, got = hold(got)
     half = (keep.shape[0] - 16, LANES)
-    mine, theirs = scan_call(end_kernel, (start, got, keep, come), [half, half], "join_end")
-    return hold, mine, lax.ppermute(theirs, "seq", pair)
+    mine, theirs = scan_call(
+        functools.partial(end_kernel, distance), (ahead, got, keep, come), [half, half], "join_end"
+    )
+    return hold, mine, exchange(theirs, 1)
 
 
 def rows_of(ref, block):

time: 59.3 us -> 56.9 us (0.960)
  starting transfers between devices: 18.1 us -> 14.2 us
  waiting for transfers between devices: 21.3 us -> 22.9 us
    ppermute x4, starting transfers between devices: 13.7 us -> 9.54 us  [exchange(): return lax.ppermute(value, 'seq', [(s, s ^ distance) for s in range(count)])]
    ppermute x4, waiting for transfers between devices: 8.02 us -> 9.76 us  [exchange(): return lax.ppermute(value, 'seq', [(s, s ^ distance) for s in range(count)])]
  transfers between devices with their start and end apart: 10 -> 10, of which waited for: 7 -> 8; matrix products, arithmetic and copies ran while one was open for 0% -> 0% of each run, Pallas kernels for 23% -> 24%
where the time goes in v2:
time: 56.9 us; the launch traced here: 56.7 us
  waiting for transfers between devices  22.9 us (40%)
  Pallas kernels  18.5 us (33%)
  starting transfers between devices  14.2 us (25%)
  local copies, waits for them, and re-layouts  0.82 us (1%)
    ppermute x4, waiting for transfers between devices, exchange(): return lax.ppermute(value, 'seq', [(s, s ^ distance) for s in range(count)])  9.76 us
    ppermute x4, starting transfers between devices, exchange(): return lax.ppermute(value, 'seq', [(s, s ^ distance) for s in range(count)])  9.54 us
    pallas_call x2, Pallas kernels, within(): pl.pallas_call(functools.partial(within_kernel, far), in_specs=[VMEM] * 6...  6.38 us
    pallas_call x7, Pallas kernels, local_call(): pl.pallas_call(kernel, in_specs=[VMEM] * len(operands), out_specs=[VMEM]...  6.07 us
    ppermute x1, waiting for transfers between devices, per_device(): third, filled = await_piece(lax.ppermute(third, 'head', far), filled)  5.31 us
    ppermute x1, waiting for transfers between devices, per_device(): second, first = await_piece(lax.ppermute(second, 'head', far), first)  4.6 us
    pallas_call x1, Pallas kernels, give_states(): pl.pallas_call(give_kernel, in_specs=[HBM] * 4, out_shape=[jax.ShapeDtype...  2.9 us
    ppermute x3, waiting for transfers between devices, add(): come = lax.ppermute(theirs, 'head', near)  2 us
  transfers between devices with their start and end apart: 10, of which 8 were waited for; matrix products, arithmetic and copies ran while one was open for 0% of the time, Pallas kernels for 24%

profile of v2, /device:TPU:0, one launch (start us, length us, event | category | flops | bytes accessed | tf_op | source)
XLA Modules:
  0.0 56.7 jit_solution(10741993423106810672)
XLA Ops:
  0.0 2.9 %give_states.1 = (bf16[528,128]{1,0:T(8,128)(2,1)}, bf16[32,640]{1,0:T(8,128)(2,1)}, f32[4,48,128]{2,1,0:T(8,128)}) custom-call(f32[16,512]{1,0:T(8,128)} %bitcast.20, f32[1,16]{1,0:T(1,128)} %bitcast.21, f32[512,1024]{1,0:T(8,128)} %x_ref.3, f32[512,128]{1,0:T(8,128)} %bitcast.8), custom_call_target="tpu_custom_call" | custom-call | flops 200000000 | bytes 1500000 | tf_op jit(solution)/shard_map/give_states/pallas_call | solution.py:157
  2.9 3.0 %collective-permute-start = (bf16[528,128]{1,0:T(8,128)(2,1)}, bf16[528,128]{1,0:T(8,128)(2,1)S(1)}, u32[]{:S(2)}, u32[]{:S(2)}) collective-permute-start(bf16[528,128]{1,0:T(8,128)(2,1)} %get-tuple-element.37), channel_id=1, source_target_pairs={{0,4},{4,0},{8,12},{12,8},{16,20},{20,16},{24,28},{28,24},{1,5},{5... | collective-permute-start | bytes 405512 | tf_op jit(solution)/shard_map/ppermute | solution.py:280
  6.7 1.0 %keep_states.1.own = bf16[528,128]{1,0:T(8,128)(2,1)S(1)} custom-call(bf16[32,640]{1,0:T(8,128)(2,1)S(1)} %copy-done.3, f32[512,1024]{1,0:T(8,128)S(1)} %copy-done, f32[512,128]{1,0:T(8,128)S(1)} %bitcast.9), custom_call_target="tpu_custom_call" | custom-call | flops 200000000 | bytes 1500000 | tf_op jit(solution)/shard_map/keep_states/pallas_call | solution.py:181
  7.7 2.0 %collective-permute-done.come = bf16[528,128]{1,0:T(8,128)(2,1)S(1)} collective-permute-done((bf16[528,128]{1,0:T(8,128)(2,1)}, bf16[528,128]{1,0:T(8,128)(2,1)S(1)}, u32[]{:S(2)}, u32[]{:S(2)}) %collective-permute-start) | collective-permute-done | bytes 135200 | tf_op jit(solution)/shard_map/ppermute | solution.py:280
  9.8 1.9 %collective-permute-start.1 = (bf16[528,128]{1,0:T(8,128)(2,1)S(1)}, bf16[528,128]{1,0:T(8,128)(2,1)S(1)}, u32[]{:S(2)}, u32[]{:S(2)}) collective-permute-start(bf16[528,128]{1,0:T(8,128)(2,1)S(1)} %run.2.own), channel_id=1, source_target_pairs={{0,8},{4,12},{8,0},{12,4},{16,24},{20,28},{24,16},{28,20},{1,9},{5... | collective-permute-start | bytes 405512 | tf_op jit(solution)/shard_map/ppermute | solution.py:280
  11.7 3.2 %collective-permute-done.1.come = bf16[528,128]{1,0:T(8,128)(2,1)S(1)} collective-permute-done((bf16[528,128]{1,0:T(8,128)(2,1)S(1)}, bf16[528,128]{1,0:T(8,128)(2,1)S(1)}, u32[]{:S(2)}, u32[]{:S(2)}) %collective-permute-start.1) | collective-permute-done | bytes 135200 | tf_op jit(solution)/shard_map/ppermute | solution.py:280
  14.9 2.9 %collective-permute-start.2 = (bf16[528,128]{1,0:T(8,128)(2,1)S(1)}, bf16[528,128]{1,0:T(8,128)(2,1)S(1)}, u32[]{:S(2)}, u32[]{:S(2)}) collective-permute-start(bf16[528,128]{1,0:T(8,128)(2,1)S(1)} %run.3), channel_id=1, source_target_pairs={{0,16},{4,20},{8,24},{12,28},{16,0},{20,4},{24,8},{28,12},{1,17},{... | collective-permute-start | bytes 405512 | tf_op jit(solution)/shard_map/ppermute | solution.py:280
  17.9 3.2 %within_far.1 = (f32[256,1024]{1,0:T(8,128)S(1)}, f32[256,1024]{1,0:T(8,128)S(1)}) custom-call(f32[4,48,128]{2,1,0:T(8,128)S(1)} %copy-done.6, f32[512,1024]{1,0:T(8,128)S(1)} %copy-done, f32[512,128]{1,0:T(8,128)S(1)} %bitcast.10, f32[512,128]{1,0:T(8,128)S(1)} %bitcast.12, bf16[512,1024]{1,0:T(8,128)(2,1)S(1)} %copy-done.5, f32[1,16]{1,0:T(1,128)S(1)} %bitcast.18), custom_call_target="tpu_custom_call" | custom-call | flops 4000000000 | bytes 3000000 | tf_op jit(solution)/shard_map/within_far/pallas_call | solution.py:394
  21.1 1.3 %collective-permute-done.2.last = bf16[528,128]{1,0:T(8,128)(2,1)S(1)} collective-permute-done((bf16[528,128]{1,0:T(8,128)(2,1)S(1)}, bf16[528,128]{1,0:T(8,128)(2,1)S(1)}, u32[]{:S(2)}, u32[]{:S(2)}) %collective-permute-start.2) | collective-permute-done | bytes 135200 | tf_op jit(solution)/shard_map/ppermute | solution.py:280
  22.7 1.7 %collective-permute-start.3 = (bf16[512,128]{1,0:T(8,128)(2,1)S(1)}, bf16[512,128]{1,0:T(8,128)(2,1)S(1)}, u32[]{:S(2)}, u32[]{:S(2)}) collective-permute-start(bf16[512,128]{1,0:T(8,128)(2,1)S(1)} %get-tuple-element.42), channel_id=1, source_target_pairs={{0,4},{4,0},{8,12},{12,8},{16,20},{20,16},{24,28},{28,24},{1,5},{5... | collective-permute-start | bytes 393224 | tf_op jit(solution)/shard_map/ppermute | solution.py:280
  24.4 3.3 %collective-permute-done.3.there = bf16[512,128]{1,0:T(8,128)(2,1)S(1)} collective-permute-done((bf16[512,128]{1,0:T(8,128)(2,1)S(1)}, bf16[512,128]{1,0:T(8,128)(2,1)S(1)}, u32[]{:S(2)}, u32[]{:S(2)}) %collective-permute-start.3) | collective-permute-done | bytes 131104 | tf_op jit(solution)/shard_map/ppermute | solution.py:280
  27.7 1.1 %finish_far.1 = (bf16[128,1024]{1,0:T(8,128)(2,1)S(1)}, f32[128,1024]{1,0:T(8,128)S(1)}, bf16[256,1024]{1,0:T(8,128)(2,1)S(1)}) custom-call(f32[256,1024]{1,0:T(8,128)S(1)} %get-tuple-element.38.own, f32[256,1024]{1,0:T(8,128)S(1)} %get-tuple-element.39.lead, f32[512,128]{1,0:T(8,128)S(1)} %bitcast.13, bf16[512,128]{1,0:T(8,128)(2,1)S(1)} %get-tuple-element.41.here, ...), custom_call_target="tpu_custom_call" | custom-call | flops 536870912 | tf_op jit(solution)/shard_map/finish_far/pallas_call | solution.py:476
  28.9 1.0 %project_more.1 = (bf16[128,1536]{1,0:T(8,128)(2,1)S(1)}, f32[128,1536]{1,0:T(8,128)S(1)}) custom-call(bf16[256,1024]{1,0:T(8,128)(2,1)S(1)} %get-tuple-element.46.normed, bf16[1024,4096]{1,0:T(8,128)(2,1)S(1)} %bitcast.7), custom_call_target="tpu_custom_call" | custom-call | flops 805306368 | tf_op jit(solution)/shard_map/project_more/pallas_call | solution.py:476
  30.5 1.8 %collective-permute-start.9 = (bf16[128,1024]{1,0:T(8,128)(2,1)S(1)}, bf16[128,1024]{1,0:T(8,128)(2,1)S(1)}, u32[]{:S(2)}, u32[]{:S(2)}) collective-permute-start(bf16[128,1024]{1,0:T(8,128)(2,1)S(1)} %add_pair.4), channel_id=1, source_target_pairs={{0,2},{1,3},{2,0},{3,1},{4,6},{5,7},{6,4},{7,5},{8,10},{9,11},{10,... | collective-permute-start | bytes 786440 | tf_op jit(solution)/shard_map/ppermute | solution.py:639
  32.3 3.2 %within_near.1 = (f32[256,1024]{1,0:T(8,128)S(1)}, f32[256,1024]{1,0:T(8,128)S(1)}) custom-call(f32[4,48,128]{2,1,0:T(8,128)S(1)} %copy-done.6, f32[512,1024]{1,0:T(8,128)S(1)} %copy-done, f32[512,128]{1,0:T(8,128)S(1)} %bitcast.11, f32[512,128]{1,0:T(8,128)S(1)} %bitcast.14, bf16[512,1024]{1,0:T(8,128)(2,1)S(1)} %copy-done.5, f32[1,16]{1,0:T(1,128)S(1)} %bitcast.19), custom_call_target="tpu_custom_call" | custom-call | flops 4000000000 | bytes 3000000 | tf_op jit(solution)/shard_map/within_near/pallas_call | solution.py:394
  35.9 2.5 %finish_near.1 = (bf16[128,5632]{1,0:T(8,128)(2,1)S(1)}, f32[128,1536]{1,0:T(8,128)S(1)}, bf16[128,1024]{1,0:T(8,128)(2,1)S(1)}) custom-call(bf16[256,1024]{1,0:T(8,128)(2,1)S(1)} %get-tuple-element.46.normed, f32[256,1024]{1,0:T(8,128)S(1)} %get-tuple-element.50.own, f32[256,1024]{1,0:T(8,128)S(1)} %get-tuple-element.51.lead, f32[512,128]{1,0:T(8,128)S(1)} %bitcast.15, ...), custom_call_target="tpu_custom_call" | custom-call | flops 1879048192 | tf_op jit(solution)/shard_map/finish_near/pallas_call | solution.py:476
  38.5 1.2 %collective-permute-done.9.refs_0_ = bf16[128,1024]{1,0:T(8,128)(2,1)S(1)} collective-permute-done((bf16[128,1024]{1,0:T(8,128)(2,1)S(1)}, bf16[128,1024]{1,0:T(8,128)(2,1)S(1)}, u32[]{:S(2)}, u32[]{:S(2)}) %collective-permute-start.9) | collective-permute-done | bytes 262176 | tf_op jit(solution)/shard_map/ppermute | solution.py:639
  39.7 2.0 %collective-permute-done.6.come = bf16[128,5632]{1,0:T(8,128)(2,1)S(1)} collective-permute-done((bf16[128,5632]{1,0:T(8,128)(2,1)S(1)}, bf16[128,5632]{1,0:T(8,128)(2,1)S(1)}, u32[]{:S(2)}, u32[]{:S(2)}) %collective-permute-start.6) | collective-permute-done | bytes 1441824 | tf_op jit(solution)/shard_map/ppermute | solution.py:600
  41.8 1.8 %collective-permute-start.7 = (bf16[128,1536]{1,0:T(8,128)(2,1)S(1)}, bf16[128,1536]{1,0:T(8,128)(2,1)S(1)}, u32[]{:S(2)}, u32[]{:S(2)}) collective-permute-start(bf16[128,1536]{1,0:T(8,128)(2,1)S(1)} %add_pair.5), channel_id=1, source_target_pairs={{0,2},{1,3},{2,0},{3,1},{4,6},{5,7},{6,4},{7,5},{8,10},{9,11},{10,... | collective-permute-start | bytes 1179656 | tf_op jit(solution)/shard_map/ppermute | solution.py:642
  43.6 4.6 %collective-permute-done.8.refs_0_ = bf16[128,1536]{1,0:T(8,128)(2,1)S(1)} collective-permute-done((bf16[128,1536]{1,0:T(8,128)(2,1)S(1)}, bf16[128,1536]{1,0:T(8,128)(2,1)S(1)}, u32[]{:S(2)}, u32[]{:S(2)}) %collective-permute-start.8) | collective-permute-done | bytes 393248 | tf_op jit(solution)/shard_map/ppermute | solution.py:640
  48.2 1.3 %project_kept.1.kept = f32[128,4096]{1,0:T(8,128)S(1)} custom-call(bf16[128,1024]{1,0:T(8,128)(2,1)S(1)} %get-tuple-element.52.kept, bf16[128,5632]{1,0:T(8,128)(2,1)S(1)} %collective-permute-done.6.come, bf16[1024,4096]{1,0:T(8,128)(2,1)S(1)} %bitcast.7), custom_call_target="tpu_custom_call" | custom-call | flops 1073741824 | tf_op jit(solution)/shard_map/project_kept/pallas_call | solution.py:476
  49.5 0.9 %early_sums.1.refs_1_ = bf16[128,4096]{1,0:T(8,128)(2,1)} custom-call(f32[128,4096]{1,0:T(8,128)S(1)} %project_kept.1.kept, bf16[128,1024]{1,0:T(8,128)(2,1)S(1)} %get-tuple-element.57.first, bf16[128,1536]{1,0:T(8,128)(2,1)S(1)} %get-tuple-element.58.second), custom_call_target="tpu_custom_call" | custom-call | tf_op jit(solution)/shard_map/early_sums/pallas_call | solution.py:519
  50.4 5.3 %collective-permute-done.7.refs_0_ = bf16[128,1536]{1,0:T(8,128)(2,1)S(1)} collective-permute-done((bf16[128,1536]{1,0:T(8,128)(2,1)S(1)}, bf16[128,1536]{1,0:T(8,128)(2,1)S(1)}, u32[]{:S(2)}, u32[]{:S(2)}) %collective-permute-start.7) | collective-permute-done | bytes 393248 | tf_op jit(solution)/shard_map/ppermute | solution.py:642
  55.8 0.8 %last_sums.1 = bf16[128,4096]{1,0:T(8,128)(2,1)} custom-call(f32[128,4096]{1,0:T(8,128)S(1)} %project_kept.1.kept, bf16[128,1536]{1,0:T(8,128)(2,1)S(1)} %get-tuple-element.59.third, bf16[128,4096]{1,0:T(8,128)(2,1)} %get-tuple-element.60.filled), custom_call_target="tpu_custom_call", output_to_operand_aliasing={{}: (2, {})} | custom-call | tf_op jit(solution)/shard_map/last_sums/pallas_call | solution.py:551
  (37 shorter events, 2.5 us)
Async XLA Ops:
  0.0 5.9 %copy-start = (f32[512,1024]{1,0:T(8,128)S(1)}, f32[512,1024]{1,0:T(8,128)}, u32[]{:S(2)}) copy-start(f32[512,1024]{1,0:T(8,128)} %x_ref.3) | copy-start | bytes 6291460
  0.0 5.9 %copy-start.1 = (f32[512,1,128]{2,1,0:T(1,128)S(1)}, f32[512,1,128]{2,1,0:T(1,128)}, u32[]{:S(2)}) copy-start(f32[512,1,128]{2,1,0:T(1,128)} %param.13) | copy-start | bytes 786436
  0.0 17.8 %copy-start.7 = (f32[16]{0:T(128)S(1)}, f32[16]{0:T(128)}, u32[]{:S(2)}) copy-start(f32[16]{0:T(128)} %param.15) | copy-start | bytes 196
  2.9 14.9 %copy-start.2 = (f32[512,1,128]{2,1,0:T(1,128)S(1)}, f32[512,1,128]{2,1,0:T(1,128)}, u32[]{:S(2)}) copy-start(f32[512,1,128]{2,1,0:T(1,128)} %param.14) | copy-start | bytes 786436
  2.9 6.8 %collective-permute-start = (bf16[528,128]{1,0:T(8,128)(2,1)}, bf16[528,128]{1,0:T(8,128)(2,1)S(1)}, u32[]{:S(2)}, u32[]{:S(2)}) collective-permute-start(bf16[528,128]{1,0:T(8,128)(2,1)} %get-tuple-element.37), channel_id=1, source_target_pairs={{0,4},{4,0},{8,12},{12,8},{16,20},{20,16},{24,28},{28,24},{1,5},{5... | collective-permute-start | bytes 405512 | tf_op jit(solution)/shard_map/ppermute | solution.py:280
  5.9 0.8 %copy-start.3 = (bf16[32,640]{1,0:T(8,128)(2,1)S(1)}, bf16[32,640]{1,0:T(8,128)(2,1)}, u32[]{:S(2)}) copy-start(bf16[32,640]{1,0:T(8,128)(2,1)} %get-tuple-element.36.wk) | copy-start | bytes 122884
  6.7 11.1 %copy-start.5 = (bf16[512,1024]{1,0:T(8,128)(2,1)S(1)}, bf16[512,1024]{1,0:T(8,128)(2,1)}, u32[]{:S(2)}) copy-start(bf16[512,1024]{1,0:T(8,128)(2,1)} %gate_ref.3) | copy-start | bytes 3145732
  6.7 11.1 %copy-start.6 = (f32[4,48,128]{2,1,0:T(8,128)S(1)}, f32[4,48,128]{2,1,0:T(8,128)}, u32[]{:S(2)}) copy-start(f32[4,48,128]{2,1,0:T(8,128)} %get-tuple-element.49.aux) | copy-start | bytes 294916
  9.8 5.1 %collective-permute-start.1 = (bf16[528,128]{1,0:T(8,128)(2,1)S(1)}, bf16[528,128]{1,0:T(8,128)(2,1)S(1)}, u32[]{:S(2)}, u32[]{:S(2)}) collective-permute-start(bf16[528,128]{1,0:T(8,128)(2,1)S(1)} %run.2.own), channel_id=1, source_target_pairs={{0,8},{4,12},{8,0},{12,4},{16,24},{20,28},{24,16},{28,20},{1,9},{5... | collective-permute-start | bytes 405512 | tf_op jit(solution)/shard_map/ppermute | solution.py:280
  14.9 7.5 %collective-permute-start.2 = (bf16[528,128]{1,0:T(8,128)(2,1)S(1)}, bf16[528,128]{1,0:T(8,128)(2,1)S(1)}, u32[]{:S(2)}, u32[]{:S(2)}) collective-permute-start(bf16[528,128]{1,0:T(8,128)(2,1)S(1)} %run.3), channel_id=1, source_target_pairs={{0,16},{4,20},{8,24},{12,28},{16,0},{20,4},{24,8},{28,12},{1,17},{... | collective-permute-start | bytes 405512 | tf_op jit(solution)/shard_map/ppermute | solution.py:280
  17.8 9.9 %slice-start = ((s8[8388608]{0:T(1024)(128)(4,1)}), s8[4194304]{0:T(1024)(128)(4,1)S(1)}, s32[]{:S(2)}) async-start(s8[8388608]{0:T(1024)(128)(4,1)} %bitcast.6), calls=%async_computation | async-start | bytes 8388608
  17.9 9.9 %slice-start.1 = ((s8[8388608]{0:T(1024)(128)(4,1)}), s8[4194304]{0:T(1024)(128)(4,1)S(1)}, s32[]{:S(2)}) async-start(s8[8388608]{0:T(1024)(128)(4,1)} %bitcast.6), calls=%async_computation.1 | async-start | bytes 8388608
  17.9 9.9 %copy-start.4 = (f32[1024]{0:T(1024)S(1)}, f32[1024]{0:T(1024)}, u32[]{:S(2)}) copy-start(f32[1024]{0:T(1024)} %param.16) | copy-start | bytes 12292
  22.7 5.0 %collective-permute-start.3 = (bf16[512,128]{1,0:T(8,128)(2,1)S(1)}, bf16[512,128]{1,0:T(8,128)(2,1)S(1)}, u32[]{:S(2)}, u32[]{:S(2)}) collective-permute-start(bf16[512,128]{1,0:T(8,128)(2,1)S(1)} %get-tuple-element.42), channel_id=1, source_target_pairs={{0,4},{4,0},{8,12},{12,8},{16,20},{20,16},{24,28},{28,24},{1,5},{5... | collective-permute-start | bytes 393224 | tf_op jit(solution)/shard_map/ppermute | solution.py:280
  28.8 1.6 %collective-permute-start.5 = (bf16[128,1024]{1,0:T(8,128)(2,1)S(1)}, bf16[128,1024]{1,0:T(8,128)(2,1)S(1)}, u32[]{:S(2)}, u32[]{:S(2)}) collective-permute-start(bf16[128,1024]{1,0:T(8,128)(2,1)S(1)} %get-tuple-element.48), channel_id=1, source_target_pairs={{0,1},{1,0},{2,3},{3,2},{4,5},{5,4},{6,7},{7,6},{8,9},{9,8},{10,11... | collective-permute-start | bytes 786440 | tf_op jit(solution)/shard_map/ppermute | solution.py:600
  29.9 5.6 %collective-permute-start.4 = (bf16[128,1536]{1,0:T(8,128)(2,1)S(1)}, bf16[128,1536]{1,0:T(8,128)(2,1)S(1)}, u32[]{:S(2)}, u32[]{:S(2)}) collective-permute-start(bf16[128,1536]{1,0:T(8,128)(2,1)S(1)} %get-tuple-element.45), channel_id=1, source_target_pairs={{0,1},{1,0},{2,3},{3,2},{4,5},{5,4},{6,7},{7,6},{8,9},{9,8},{10,11... | collective-permute-start | bytes 1179656 | tf_op jit(solution)/shard_map/ppermute | solution.py:600
  30.5 9.2 %collective-permute-start.9 = (bf16[128,1024]{1,0:T(8,128)(2,1)S(1)}, bf16[128,1024]{1,0:T(8,128)(2,1)S(1)}, u32[]{:S(2)}, u32[]{:S(2)}) collective-permute-start(bf16[128,1024]{1,0:T(8,128)(2,1)S(1)} %add_pair.4), channel_id=1, source_target_pairs={{0,2},{1,3},{2,0},{3,1},{4,6},{5,7},{6,4},{7,5},{8,10},{9,11},{10,... | collective-permute-start | bytes 786440 | tf_op jit(solution)/shard_map/ppermute | solution.py:639
  35.6 12.6 %collective-permute-start.8 = (bf16[128,1536]{1,0:T(8,128)(2,1)S(1)}, bf16[128,1536]{1,0:T(8,128)(2,1)S(1)}, u32[]{:S(2)}, u32[]{:S(2)}) collective-permute-start(bf16[128,1536]{1,0:T(8,128)(2,1)S(1)} %add_pair.3), channel_id=1, source_target_pairs={{0,2},{1,3},{2,0},{3,1},{4,6},{5,7},{6,4},{7,5},{8,10},{9,11},{10,... | collective-permute-start | bytes 1179656 | tf_op jit(solution)/shard_map/ppermute | solution.py:640
  38.4 3.3 %collective-permute-start.6 = (bf16[128,5632]{1,0:T(8,128)(2,1)S(1)}, bf16[128,5632]{1,0:T(8,128)(2,1)S(1)}, u32[]{:S(2)}, u32[]{:S(2)}) collective-permute-start(bf16[128,5632]{1,0:T(8,128)(2,1)S(1)} %get-tuple-element.53), channel_id=1, source_target_pairs={{0,1},{1,0},{2,3},{3,2},{4,5},{5,4},{6,7},{7,6},{8,9},{9,8},{10,11... | collective-permute-start | bytes 4325384 | tf_op jit(solution)/shard_map/ppermute | solution.py:600
  41.8 14.0 %collective-permute-start.7 = (bf16[128,1536]{1,0:T(8,128)(2,1)S(1)}, bf16[128,1536]{1,0:T(8,128)(2,1)S(1)}, u32[]{:S(2)}, u32[]{:S(2)}) collective-permute-start(bf16[128,1536]{1,0:T(8,128)(2,1)S(1)} %add_pair.5), channel_id=1, source_target_pairs={{0,2},{1,3},{2,0},{3,1},{4,6},{5,7},{6,4},{7,5},{8,10},{9,11},{10,... | collective-permute-start | bytes 1179656 | tf_op jit(solution)/shard_map/ppermute | solution.py:642

commit v3 on v2

--- a/solution.py
+++ b/solution.py
@@ -96,24 +96,23 @@
     return [tail[2 * k:2 * k + 1] + tail[2 * k + 1:2 * k + 2] for k in range(blocks)]
 
 
-def half_message(x_ref, b, wk, first_head, msg):
+def half_messages(x_ref, b, wk, first_head, msgs):
     tok, lanes = x_ref.shape
     heads2 = wk.shape[0]
-    width = 256
-    decays = []
-    for g in range(lanes // width):
+    width = lanes // len(msgs)
+    for g, msg in enumerate(msgs):
         chosen = pick(heads2, width, heads2 // 2, P_SIZE, first_head + g * (width // P_SIZE))
         spread = dot(wk[...], chosen, ((0,), (0,)))
         weighted = (x_ref[:, g * width:(g + 1) * width] * spread[:tok]).astype(BF)
         state = dot(b, weighted, ((0,), (0,)))
-        for i in range(width // LANES):
-            k = g * (width // LANES) + i
-            msg[k * N:(k + 1) * N] = state[:, i * LANES:(i + 1) * LANES].astype(BF)
-            decays.append(spread[tok:tok + 1, i * LANES:(i + 1) * LANES])
-    msg[msg.shape[0] - 16:] = tail_rows(decays)
-
-
-def half_kernel(give, raw, rate, x, b, msg, wk, aux, raw_v, rate_v, x_v, b_v, sems):
+        decays = []
+        for k in range(width // LANES):
+            msg[k * N:(k + 1) * N] = state[:, k * LANES:(k + 1) * LANES].astype(BF)
+            decays.append(spread[tok:tok + 1, k * LANES:(k + 1) * LANES])
+        msg[msg.shape[0] - 16:] = tail_rows(decays)
+
+
+def half_kernel(give, raw, rate, x, b, msgs, wk, aux, raw_v, rate_v, x_v, b_v, sems):
     lanes = x_v.shape[1]
     mine = lax.axis_index("seq") % 2
     half = 1 - mine if give else mine
@@ -136,15 +135,15 @@
         step_vectors(raw_v[...], rate_v[...], wk, aux)
     loads[0].wait()
     loads[1].wait()
-    half_message(x_v, b_v[...].astype(BF), wk, half * (lanes // P_SIZE), msg)
-
-
-def give_kernel(raw, rate, x, b, msg, wk, aux, raw_v, rate_v, x_v, b_v, sems):
-    half_kernel(True, raw, rate, x, b, msg, wk, aux, raw_v, rate_v, x_v, b_v, sems)
-
-
-def keep_kernel(wk, x, b, msg, x_v, b_v, sems):
-    half_kernel(False, None, None, x, b, msg, wk, None, None, None, x_v, b_v, sems)
+    half_messages(x_v, b_v[...].astype(BF), wk, half * (lanes // P_SIZE), msgs)
+
+
+def give_kernel(raw, rate, x, b, msg0, msg1, wk, aux, raw_v, rate_v, x_v, b_v, sems):
+    half_kernel(True, raw, rate, x, b, (msg0, msg1), wk, aux, raw_v, rate_v, x_v, b_v, sems)
+
+
+def keep_kernel(wk, x, b, msg0, msg1, x_v, b_v, sems):
+    half_kernel(False, None, None, x, b, (msg0, msg1), wk, None, None, None, x_v, b_v, sems)
 
 
 HBM = pl.BlockSpec(memory_space=pltpu.HBM)
@@ -158,7 +157,8 @@
         give_kernel,
         in_specs=[HBM] * 4,
         out_shape=[
-            jax.ShapeDtypeStruct((lanes + 16, LANES), BF),
+            jax.ShapeDtypeStruct((lanes // 2 + 16, LANES), BF),
+            jax.ShapeDtypeStruct((lanes // 2 + 16, LANES), BF),
             jax.ShapeDtypeStruct((2 * heads, tok + CHUNK), BF),
             jax.ShapeDtypeStruct((tok // CHUNK, 3 * heads, CHUNK), F32),
         ],
@@ -181,7 +181,7 @@
     return pl.pallas_call(
         keep_kernel,
         in_specs=[pl.BlockSpec(memory_space=pltpu.VMEM), HBM, HBM],
-        out_shape=jax.ShapeDtypeStruct((lanes + 16, LANES), BF),
+        out_shape=[jax.ShapeDtypeStruct((lanes // 2 + 16, LANES), BF)] * 2,
         scratch_shapes=[
             pltpu.VMEM((tok, lanes), F32),
             pltpu.VMEM((tok, N), F32),
@@ -292,7 +292,8 @@
         got = exchange(run, distance)
         if distance * 2 < count:
             ahead = joined(ahead_kernel, distance, ahead, got)
-    hold, got = hold(got)
+    if hold is not None:
+        hold, got = lax.optimization_barrier((hold, got))
     half = (keep.shape[0] - 16, LANES)
     mine, theirs = scan_call(
         functools.partial(end_kernel, distance), (ahead, got, keep, come), [half, half], "join_end"
@@ -421,10 +422,13 @@
     )
 
 
-def fill_incoming(here, there, incoming):
+def fill_incoming(here0, here1, there0, there1, incoming):
     odd = lax.axis_index("seq") % 2
-    incoming[odd] = here[...]
-    incoming[1 - odd] = there[...]
+    rows = here0.shape[0]
+    incoming[odd, :rows] = here0[...]
+    incoming[odd, rows:] = here1[...]
+    incoming[1 - odd, :rows] = there0[...]
+    incoming[1 - odd, rows:] = there1[...]
 
 
 def project_both(normed, w, start, columns, theirs, mine, at=0):
@@ -435,9 +439,11 @@
         mine[:, k:k + wide] = out[CHUNK:]
 
 
-def far_kernel(columns, own, lead, c, here, there, gain, w, theirs, mine, normed, incoming):
+def far_kernel(
+    columns, own, lead, c, here0, here1, there0, there1, gain, w, theirs, mine, normed, incoming
+):
     me = lax.axis_index("head")
-    fill_incoming(here, there, incoming)
+    fill_incoming(here0, here1, there0, there1, incoming)
     normed[:CHUNK] = finish_block(me ^ 3, own, lead, c, incoming, gain)
     normed[CHUNK:] = finish_block(me ^ 2, own, lead, c, incoming, gain)
     project_both(normed, w, 0, columns, theirs, mine)
@@ -448,11 +454,12 @@
 
 
 def mixed_kernel(
-    start, columns, normed, own, lead, c, here, there, gain, w, theirs, mine, kept, incoming, given
+    start, columns, normed, own, lead, c, here0, here1, there0, there1, gain, w,
+    theirs, mine, kept, incoming, given,
 ):
     me = lax.axis_index("head")
     project_both(normed, w, start, columns, theirs, mine)
-    fill_incoming(here, there, incoming)
+    fill_incoming(here0, here1, there0, there1, incoming)
     given[...] = finish_block(me ^ 1, own, lead, c, incoming, gain)
     kept[...] = finish_block(me, own, lead, c, incoming, gain)
     wide = 512
@@ -576,21 +583,20 @@
     heads = decay_log.shape[0]
     b = state_in.reshape(tok, N)
     c = state_out.reshape(tok, N)
-    give, wk, aux = give_states(step_raw.T, decay_log.reshape(1, heads), ssm_input, b)
-    keep = keep_states(wk, ssm_input, b)
+    give0, give1, wk, aux = give_states(step_raw.T, decay_log.reshape(1, heads), ssm_input, b)
+    keep0, keep1 = keep_states(wk, ssm_input, b)
     inputs = (ssm_input, b, c, gate_input, skip_gain.reshape(1, heads))
     local = within(True, aux, *inputs)
-    (own, lead), here, there = incoming_states(
-        give, keep, seq_count, lambda got: lax.optimization_barrier((local, got))
-    )
+    (own, lead), here0, there0 = incoming_states(give0, keep0, seq_count, local)
+    _, here1, there1 = incoming_states(give1, keep1, seq_count, None)
 
     near = [(h, h ^ 1) for h in range(4)]
     far = [(h, h ^ 2) for h in range(4)]
     gain = norm_gain.reshape(1, -1)
     channels, dout = out_weight.shape
     rows = CHUNK
-    states = pltpu.VMEM((2,) + here.shape, BF)
-    finish = (own, lead, c, here, there, gain, out_weight)
+    states = pltpu.VMEM((2, 2 * here0.shape[0], LANES), BF)
+    finish = (own, lead, c, here0, here1, there0, there1, gain, out_weight)
     (_, one), (start2, two), (start3, three) = PIECES
 
     def piece_outs(columns, extra=0):

time: 56.9 us -> 57.1 us (level)
  starting transfers between devices: 14.2 us -> 17.4 us
  waiting for transfers between devices: 22.9 us -> 19.7 us
    ppermute x4 -> x8, starting transfers between devices: 9.54 us -> 13 us  [exchange(): return lax.ppermute(value, 'seq', [(s, s ^ distance) for s in range(count)])]
    ppermute x4 -> x8, waiting for transfers between devices: 9.76 us -> 6.44 us  [exchange(): return lax.ppermute(value, 'seq', [(s, s ^ distance) for s in range(count)])]
  transfers between devices with their start and end apart: 10 -> 14, of which waited for: 8 -> 9; matrix products, arithmetic and copies ran while one was open for 0% -> 0% of each run, Pallas kernels for 24% -> 24%
where the time goes in v3:
time: 57.1 us; the launch traced here: 56.9 us
  waiting for transfers between devices  19.7 us (35%)
  Pallas kernels  18.6 us (33%)
  starting transfers between devices  17.4 us (30%)
  local copies, waits for them, and re-layouts  0.82 us (1%)
    ppermute x8, starting transfers between devices, exchange(): return lax.ppermute(value, 'seq', [(s, s ^ distance) for s in range(count)])  13 us
    ppermute x8, waiting for transfers between devices, exchange(): return lax.ppermute(value, 'seq', [(s, s ^ distance) for s in range(count)])  6.44 us
    pallas_call x2, Pallas kernels, within(): pl.pallas_call(functools.partial(within_kernel, far), in_specs=[VMEM] * 6...  6.38 us
    pallas_call x7, Pallas kernels, local_call(): pl.pallas_call(kernel, in_specs=[VMEM] * len(operands), out_specs=[VMEM]...  6.08 us
    ppermute x1, waiting for transfers between devices, per_device(): third, filled = await_piece(lax.ppermute(third, 'head', far), filled)  5.29 us
    ppermute x1, waiting for transfers between devices, per_device(): second, first = await_piece(lax.ppermute(second, 'head', far), first)  4.78 us
    pallas_call x1, Pallas kernels, give_states(): pl.pallas_call(give_kernel, in_specs=[HBM] * 4, out_shape=[jax.ShapeDtype...  2.88 us
    ppermute x3, waiting for transfers between devices, add(): come = lax.ppermute(theirs, 'head', near)  1.99 us
  transfers between devices with their start and end apart: 14, of which 9 were waited for; matrix products, arithmetic and copies ran while one was open for 0% of the time, Pallas kernels for 24%

profile of v3, /device:TPU:0, one launch (start us, length us, event | category | flops | bytes accessed | tf_op | source)
XLA Modules:
  0.0 56.9 jit_solution(2276392794061214853)
XLA Ops:
  0.0 2.9 %give_states.1 = (bf16[272,128]{1,0:T(8,128)(2,1)}, bf16[272,128]{1,0:T(8,128)(2,1)}, bf16[32,640]{1,0:T(8,128)(2,1)}, f32[4,48,128]{2,1,0:T(8,128)}) custom-call(f32[16,512]{1,0:T(8,128)} %bitcast.20, f32[1,16]{1,0:T(1,128)} %bitcast.21, f32[512,1024]{1,0:T(8,128)} %x_ref.3, f32[512,128]{1,0:T(8,128)} %bitcast.8), custom_call_target="tpu_custom_call" | custom-call | flops 200000000 | bytes 1500000 | tf_op jit(solution)/shard_map/give_states/pallas_call | solution.py:156
  2.9 3.0 %collective-permute-start.3 = (bf16[272,128]{1,0:T(8,128)(2,1)}, bf16[272,128]{1,0:T(8,128)(2,1)S(1)}, u32[]{:S(2)}, u32[]{:S(2)}) collective-permute-start(bf16[272,128]{1,0:T(8,128)(2,1)} %get-tuple-element.49), channel_id=1, source_target_pairs={{0,4},{4,0},{8,12},{12,8},{16,20},{20,16},{24,28},{28,24},{1,5},{5... | collective-permute-start | bytes 208904 | tf_op jit(solution)/shard_map/ppermute | solution.py:280
  6.8 1.0 %keep_states.1 = (bf16[272,128]{1,0:T(8,128)(2,1)S(1)}, bf16[272,128]{1,0:T(8,128)(2,1)S(1)}) custom-call(bf16[32,640]{1,0:T(8,128)(2,1)S(1)} %copy-done.3, f32[512,1024]{1,0:T(8,128)S(1)} %copy-done, f32[512,128]{1,0:T(8,128)S(1)} %bitcast.9), custom_call_target="tpu_custom_call" | custom-call | flops 200000000 | bytes 1500000 | tf_op jit(solution)/shard_map/keep_states/pallas_call | solution.py:181
  7.8 0.8 %collective-permute-done.3.come = bf16[272,128]{1,0:T(8,128)(2,1)S(1)} collective-permute-done((bf16[272,128]{1,0:T(8,128)(2,1)}, bf16[272,128]{1,0:T(8,128)(2,1)S(1)}, u32[]{:S(2)}, u32[]{:S(2)}) %collective-permute-start.3) | collective-permute-done | bytes 69664 | tf_op jit(solution)/shard_map/ppermute | solution.py:280
  8.6 2.6 %collective-permute-start.4 = (bf16[272,128]{1,0:T(8,128)(2,1)S(1)}, bf16[272,128]{1,0:T(8,128)(2,1)S(1)}, u32[]{:S(2)}, u32[]{:S(2)}) collective-permute-start(bf16[272,128]{1,0:T(8,128)(2,1)S(1)} %run.6.own), channel_id=1, source_target_pairs={{0,8},{4,12},{8,0},{12,4},{16,24},{20,28},{24,16},{28,20},{1,9},{5... | collective-permute-start | bytes 208904 | tf_op jit(solution)/shard_map/ppermute | solution.py:280
  12.1 1.6 %collective-permute-done.4.come = bf16[272,128]{1,0:T(8,128)(2,1)S(1)} collective-permute-done((bf16[272,128]{1,0:T(8,128)(2,1)S(1)}, bf16[272,128]{1,0:T(8,128)(2,1)S(1)}, u32[]{:S(2)}, u32[]{:S(2)}) %collective-permute-start.4) | collective-permute-done | bytes 69664 | tf_op jit(solution)/shard_map/ppermute | solution.py:280
  13.8 3.5 %collective-permute-start.5 = (bf16[272,128]{1,0:T(8,128)(2,1)S(1)}, bf16[272,128]{1,0:T(8,128)(2,1)S(1)}, u32[]{:S(2)}, u32[]{:S(2)}) collective-permute-start(bf16[272,128]{1,0:T(8,128)(2,1)S(1)} %run.7), channel_id=1, source_target_pairs={{0,16},{4,20},{8,24},{12,28},{16,0},{20,4},{24,8},{28,12},{1,17},{... | collective-permute-start | bytes 208904 | tf_op jit(solution)/shard_map/ppermute | solution.py:280
  17.3 1.1 %collective-permute-start.2 = (bf16[272,128]{1,0:T(8,128)(2,1)S(1)}, bf16[272,128]{1,0:T(8,128)(2,1)S(1)}, u32[]{:S(2)}, u32[]{:S(2)}) collective-permute-start(bf16[272,128]{1,0:T(8,128)(2,1)S(1)} %run.5), channel_id=1, source_target_pairs={{0,16},{4,20},{8,24},{12,28},{16,0},{20,4},{24,8},{28,12},{1,17},{... | collective-permute-start | bytes 208904 | tf_op jit(solution)/shard_map/ppermute | solution.py:280
  18.5 3.2 %within_far.1 = (f32[256,1024]{1,0:T(8,128)S(1)}, f32[256,1024]{1,0:T(8,128)S(1)}) custom-call(f32[4,48,128]{2,1,0:T(8,128)S(1)} %copy-done.6, f32[512,1024]{1,0:T(8,128)S(1)} %copy-done, f32[512,128]{1,0:T(8,128)S(1)} %bitcast.10, f32[512,128]{1,0:T(8,128)S(1)} %bitcast.12, bf16[512,1024]{1,0:T(8,128)(2,1)S(1)} %copy-done.5, f32[1,16]{1,0:T(1,128)S(1)} %bitcast.18), custom_call_target="tpu_custom_call" | custom-call | flops 4000000000 | bytes 3000000 | tf_op jit(solution)/shard_map/within_far/pallas_call | solution.py:395
  21.8 1.2 %collective-permute-start.7 = (bf16[256,128]{1,0:T(8,128)(2,1)S(1)}, bf16[256,128]{1,0:T(8,128)(2,1)S(1)}, u32[]{:S(2)}, u32[]{:S(2)}) collective-permute-start(bf16[256,128]{1,0:T(8,128)(2,1)S(1)} %get-tuple-element.52), channel_id=1, source_target_pairs={{0,4},{4,0},{8,12},{12,8},{16,20},{20,16},{24,28},{28,24},{1,5},{5... | collective-permute-start | bytes 196616 | tf_op jit(solution)/shard_map/ppermute | solution.py:280
  24.2 1.9 %collective-permute-done.7.there1 = bf16[256,128]{1,0:T(8,128)(2,1)S(1)} collective-permute-done((bf16[256,128]{1,0:T(8,128)(2,1)S(1)}, bf16[256,128]{1,0:T(8,128)(2,1)S(1)}, u32[]{:S(2)}, u32[]{:S(2)}) %collective-permute-start.7) | collective-permute-done | bytes 65568 | tf_op jit(solution)/shard_map/ppermute | solution.py:280
  26.2 1.7 %collective-permute-done.6.there0 = bf16[256,128]{1,0:T(8,128)(2,1)S(1)} collective-permute-done((bf16[256,128]{1,0:T(8,128)(2,1)S(1)}, bf16[256,128]{1,0:T(8,128)(2,1)S(1)}, u32[]{:S(2)}, u32[]{:S(2)}) %collective-permute-start.6) | collective-permute-done | bytes 65568 | tf_op jit(solution)/shard_map/ppermute | solution.py:280
  27.9 1.1 %finish_far.1 = (bf16[128,1024]{1,0:T(8,128)(2,1)S(1)}, f32[128,1024]{1,0:T(8,128)S(1)}, bf16[256,1024]{1,0:T(8,128)(2,1)S(1)}) custom-call(f32[256,1024]{1,0:T(8,128)S(1)} %get-tuple-element.44.own, f32[256,1024]{1,0:T(8,128)S(1)} %get-tuple-element.45.lead, f32[512,128]{1,0:T(8,128)S(1)} %bitcast.13, bf16[256,128]{1,0:T(8,128)(2,1)S(1)} %get-tuple-element.47.here0, ...), custom_call_target="tpu_custom_call" | custom-call | flops 536870912 | tf_op jit(solution)/shard_map/finish_far/pallas_call | solution.py:483
  29.1 1.0 %project_more.1 = (bf16[128,1536]{1,0:T(8,128)(2,1)S(1)}, f32[128,1536]{1,0:T(8,128)S(1)}) custom-call(bf16[256,1024]{1,0:T(8,128)(2,1)S(1)} %get-tuple-element.56.normed, bf16[1024,4096]{1,0:T(8,128)(2,1)S(1)} %bitcast.7), custom_call_target="tpu_custom_call" | custom-call | flops 805306368 | tf_op jit(solution)/shard_map/project_more/pallas_call | solution.py:483
  30.7 1.6 %collective-permute-start.13 = (bf16[128,1024]{1,0:T(8,128)(2,1)S(1)}, bf16[128,1024]{1,0:T(8,128)(2,1)S(1)}, u32[]{:S(2)}, u32[]{:S(2)}) collective-permute-start(bf16[128,1024]{1,0:T(8,128)(2,1)S(1)} %add_pair.4), channel_id=1, source_target_pairs={{0,2},{1,3},{2,0},{3,1},{4,6},{5,7},{6,4},{7,5},{8,10},{9,11},{10,... | collective-permute-start | bytes 786440 | tf_op jit(solution)/shard_map/ppermute | solution.py:645
  32.3 3.2 %within_near.1 = (f32[256,1024]{1,0:T(8,128)S(1)}, f32[256,1024]{1,0:T(8,128)S(1)}) custom-call(f32[4,48,128]{2,1,0:T(8,128)S(1)} %copy-done.6, f32[512,1024]{1,0:T(8,128)S(1)} %copy-done, f32[512,128]{1,0:T(8,128)S(1)} %bitcast.11, f32[512,128]{1,0:T(8,128)S(1)} %bitcast.14, bf16[512,1024]{1,0:T(8,128)(2,1)S(1)} %copy-done.5, f32[1,16]{1,0:T(1,128)S(1)} %bitcast.19), custom_call_target="tpu_custom_call" | custom-call | flops 4000000000 | bytes 3000000 | tf_op jit(solution)/shard_map/within_near/pallas_call | solution.py:395
  36.1 2.5 %finish_near.1 = (bf16[128,5632]{1,0:T(8,128)(2,1)S(1)}, f32[128,1536]{1,0:T(8,128)S(1)}, bf16[128,1024]{1,0:T(8,128)(2,1)S(1)}) custom-call(bf16[256,1024]{1,0:T(8,128)(2,1)S(1)} %get-tuple-element.56.normed, f32[256,1024]{1,0:T(8,128)S(1)} %get-tuple-element.60.own, f32[256,1024]{1,0:T(8,128)S(1)} %get-tuple-element.61.lead, f32[512,128]{1,0:T(8,128)S(1)} %bitcast.15, ...), custom_call_target="tpu_custom_call" | custom-call | flops 1879048192 | tf_op jit(solution)/shard_map/finish_near/pallas_call | solution.py:483
  38.7 1.2 %collective-permute-done.13.refs_0_ = bf16[128,1024]{1,0:T(8,128)(2,1)S(1)} collective-permute-done((bf16[128,1024]{1,0:T(8,128)(2,1)S(1)}, bf16[128,1024]{1,0:T(8,128)(2,1)S(1)}, u32[]{:S(2)}, u32[]{:S(2)}) %collective-permute-start.13) | collective-permute-done | bytes 262176 | tf_op jit(solution)/shard_map/ppermute | solution.py:645
  39.9 2.0 %collective-permute-done.10.come = bf16[128,5632]{1,0:T(8,128)(2,1)S(1)} collective-permute-done((bf16[128,5632]{1,0:T(8,128)(2,1)S(1)}, bf16[128,5632]{1,0:T(8,128)(2,1)S(1)}, u32[]{:S(2)}, u32[]{:S(2)}) %collective-permute-start.10) | collective-permute-done | bytes 1441824 | tf_op jit(solution)/shard_map/ppermute | solution.py:606
  42.0 1.6 %collective-permute-start.11 = (bf16[128,1536]{1,0:T(8,128)(2,1)S(1)}, bf16[128,1536]{1,0:T(8,128)(2,1)S(1)}, u32[]{:S(2)}, u32[]{:S(2)}) collective-permute-start(bf16[128,1536]{1,0:T(8,128)(2,1)S(1)} %add_pair.5), channel_id=1, source_target_pairs={{0,2},{1,3},{2,0},{3,1},{4,6},{5,7},{6,4},{7,5},{8,10},{9,11},{10,... | collective-permute-start | bytes 1179656 | tf_op jit(solution)/shard_map/ppermute | solution.py:648
  43.6 4.8 %collective-permute-done.12.refs_0_ = bf16[128,1536]{1,0:T(8,128)(2,1)S(1)} collective-permute-done((bf16[128,1536]{1,0:T(8,128)(2,1)S(1)}, bf16[128,1536]{1,0:T(8,128)(2,1)S(1)}, u32[]{:S(2)}, u32[]{:S(2)}) %collective-permute-start.12) | collective-permute-done | bytes 393248 | tf_op jit(solution)/shard_map/ppermute | solution.py:646
  48.4 1.3 %project_kept.1.kept = f32[128,4096]{1,0:T(8,128)S(1)} custom-call(bf16[128,1024]{1,0:T(8,128)(2,1)S(1)} %get-tuple-element.62.kept, bf16[128,5632]{1,0:T(8,128)(2,1)S(1)} %collective-permute-done.10.come, bf16[1024,4096]{1,0:T(8,128)(2,1)S(1)} %bitcast.7), custom_call_target="tpu_custom_call" | custom-call | flops 1073741824 | tf_op jit(solution)/shard_map/project_kept/pallas_call | solution.py:483
  49.7 1.0 %early_sums.1.refs_1_ = bf16[128,4096]{1,0:T(8,128)(2,1)} custom-call(f32[128,4096]{1,0:T(8,128)S(1)} %project_kept.1.kept, bf16[128,1024]{1,0:T(8,128)(2,1)S(1)} %get-tuple-element.67.first, bf16[128,1536]{1,0:T(8,128)(2,1)S(1)} %get-tuple-element.68.second), custom_call_target="tpu_custom_call" | custom-call | tf_op jit(solution)/shard_map/early_sums/pallas_call | solution.py:526
  50.7 5.3 %collective-permute-done.11.refs_0_ = bf16[128,1536]{1,0:T(8,128)(2,1)S(1)} collective-permute-done((bf16[128,1536]{1,0:T(8,128)(2,1)S(1)}, bf16[128,1536]{1,0:T(8,128)(2,1)S(1)}, u32[]{:S(2)}, u32[]{:S(2)}) %collective-permute-start.11) | collective-permute-done | bytes 393248 | tf_op jit(solution)/shard_map/ppermute | solution.py:648
  (49 shorter events, 5.4 us)
Async XLA Ops:
  0.0 6.0 %copy-start = (f32[512,1024]{1,0:T(8,128)S(1)}, f32[512,1024]{1,0:T(8,128)}, u32[]{:S(2)}) copy-start(f32[512,1024]{1,0:T(8,128)} %x_ref.3) | copy-start | bytes 6291460
  0.0 6.0 %copy-start.1 = (f32[512,1,128]{2,1,0:T(1,128)S(1)}, f32[512,1,128]{2,1,0:T(1,128)}, u32[]{:S(2)}) copy-start(f32[512,1,128]{2,1,0:T(1,128)} %param.13) | copy-start | bytes 786436
  0.0 18.4 %copy-start.7 = (f32[16]{0:T(128)S(1)}, f32[16]{0:T(128)}, u32[]{:S(2)}) copy-start(f32[16]{0:T(128)} %param.15) | copy-start | bytes 196
  2.9 15.5 %copy-start.2 = (f32[512,1,128]{2,1,0:T(1,128)S(1)}, f32[512,1,128]{2,1,0:T(1,128)}, u32[]{:S(2)}) copy-start(f32[512,1,128]{2,1,0:T(1,128)} %param.14) | copy-start | bytes 786436
  2.9 5.7 %collective-permute-start.3 = (bf16[272,128]{1,0:T(8,128)(2,1)}, bf16[272,128]{1,0:T(8,128)(2,1)S(1)}, u32[]{:S(2)}, u32[]{:S(2)}) collective-permute-start(bf16[272,128]{1,0:T(8,128)(2,1)} %get-tuple-element.49), channel_id=1, source_target_pairs={{0,4},{4,0},{8,12},{12,8},{16,20},{20,16},{24,28},{28,24},{1,5},{5... | collective-permute-start | bytes 208904 | tf_op jit(solution)/shard_map/ppermute | solution.py:280
  5.9 5.4 %collective-permute-start = (bf16[272,128]{1,0:T(8,128)(2,1)}, bf16[272,128]{1,0:T(8,128)(2,1)S(1)}, u32[]{:S(2)}, u32[]{:S(2)}) collective-permute-start(bf16[272,128]{1,0:T(8,128)(2,1)} %get-tuple-element.43), channel_id=1, source_target_pairs={{0,4},{4,0},{8,12},{12,8},{16,20},{20,16},{24,28},{28,24},{1,5},{5... | collective-permute-start | bytes 208904 | tf_op jit(solution)/shard_map/ppermute | solution.py:280
  6.0 0.8 %copy-start.3 = (bf16[32,640]{1,0:T(8,128)(2,1)S(1)}, bf16[32,640]{1,0:T(8,128)(2,1)}, u32[]{:S(2)}) copy-start(bf16[32,640]{1,0:T(8,128)(2,1)} %get-tuple-element.41.wk) | copy-start | bytes 122884
  6.8 11.6 %copy-start.5 = (bf16[512,1024]{1,0:T(8,128)(2,1)S(1)}, bf16[512,1024]{1,0:T(8,128)(2,1)}, u32[]{:S(2)}) copy-start(bf16[512,1024]{1,0:T(8,128)(2,1)} %gate_ref.3) | copy-start | bytes 3145732
  6.8 11.6 %copy-start.6 = (f32[4,48,128]{2,1,0:T(8,128)S(1)}, f32[4,48,128]{2,1,0:T(8,128)}, u32[]{:S(2)}) copy-start(f32[4,48,128]{2,1,0:T(8,128)} %get-tuple-element.59.aux) | copy-start | bytes 294916
  8.6 5.1 %collective-permute-start.4 = (bf16[272,128]{1,0:T(8,128)(2,1)S(1)}, bf16[272,128]{1,0:T(8,128)(2,1)S(1)}, u32[]{:S(2)}, u32[]{:S(2)}) collective-permute-start(bf16[272,128]{1,0:T(8,128)(2,1)S(1)} %run.6.own), channel_id=1, source_target_pairs={{0,8},{4,12},{8,0},{12,4},{16,24},{20,28},{24,16},{28,20},{1,9},{5... | collective-permute-start | bytes 208904 | tf_op jit(solution)/shard_map/ppermute | solution.py:280
  11.3 5.9 %collective-permute-start.1 = (bf16[272,128]{1,0:T(8,128)(2,1)S(1)}, bf16[272,128]{1,0:T(8,128)(2,1)S(1)}, u32[]{:S(2)}, u32[]{:S(2)}) collective-permute-start(bf16[272,128]{1,0:T(8,128)(2,1)S(1)} %run.4.own), channel_id=1, source_target_pairs={{0,8},{4,12},{8,0},{12,4},{16,24},{20,28},{24,16},{28,20},{1,9},{5... | collective-permute-start | bytes 208904 | tf_op jit(solution)/shard_map/ppermute | solution.py:280
  13.8 7.9 %collective-permute-start.5 = (bf16[272,128]{1,0:T(8,128)(2,1)S(1)}, bf16[272,128]{1,0:T(8,128)(2,1)S(1)}, u32[]{:S(2)}, u32[]{:S(2)}) collective-permute-start(bf16[272,128]{1,0:T(8,128)(2,1)S(1)} %run.7), channel_id=1, source_target_pairs={{0,16},{4,20},{8,24},{12,28},{16,0},{20,4},{24,8},{28,12},{1,17},{... | collective-permute-start | bytes 208904 | tf_op jit(solution)/shard_map/ppermute | solution.py:280
  17.3 6.0 %collective-permute-start.2 = (bf16[272,128]{1,0:T(8,128)(2,1)S(1)}, bf16[272,128]{1,0:T(8,128)(2,1)S(1)}, u32[]{:S(2)}, u32[]{:S(2)}) collective-permute-start(bf16[272,128]{1,0:T(8,128)(2,1)S(1)} %run.5), channel_id=1, source_target_pairs={{0,16},{4,20},{8,24},{12,28},{16,0},{20,4},{24,8},{28,12},{1,17},{... | collective-permute-start | bytes 208904 | tf_op jit(solution)/shard_map/ppermute | solution.py:280
  18.4 9.5 %slice-start = ((s8[8388608]{0:T(1024)(128)(4,1)}), s8[4194304]{0:T(1024)(128)(4,1)S(1)}, s32[]{:S(2)}) async-start(s8[8388608]{0:T(1024)(128)(4,1)} %bitcast.6), calls=%async_computation | async-start | bytes 8388608
  18.4 9.5 %slice-start.1 = ((s8[8388608]{0:T(1024)(128)(4,1)}), s8[4194304]{0:T(1024)(128)(4,1)S(1)}, s32[]{:S(2)}) async-start(s8[8388608]{0:T(1024)(128)(4,1)} %bitcast.6), calls=%async_computation.1 | async-start | bytes 8388608
  18.4 9.5 %copy-start.4 = (f32[1024]{0:T(1024)S(1)}, f32[1024]{0:T(1024)}, u32[]{:S(2)}) copy-start(f32[1024]{0:T(1024)} %param.16) | copy-start | bytes 12292
  21.8 4.3 %collective-permute-start.7 = (bf16[256,128]{1,0:T(8,128)(2,1)S(1)}, bf16[256,128]{1,0:T(8,128)(2,1)S(1)}, u32[]{:S(2)}, u32[]{:S(2)}) collective-permute-start(bf16[256,128]{1,0:T(8,128)(2,1)S(1)} %get-tuple-element.52), channel_id=1, source_target_pairs={{0,4},{4,0},{8,12},{12,8},{16,20},{20,16},{24,28},{28,24},{1,5},{5... | collective-permute-start | bytes 196616 | tf_op jit(solution)/shard_map/ppermute | solution.py:280
  23.6 4.3 %collective-permute-start.6 = (bf16[256,128]{1,0:T(8,128)(2,1)S(1)}, bf16[256,128]{1,0:T(8,128)(2,1)S(1)}, u32[]{:S(2)}, u32[]{:S(2)}) collective-permute-start(bf16[256,128]{1,0:T(8,128)(2,1)S(1)} %get-tuple-element.51), channel_id=1, source_target_pairs={{0,4},{4,0},{8,12},{12,8},{16,20},{20,16},{24,28},{28,24},{1,5},{5... | collective-permute-start | bytes 196616 | tf_op jit(solution)/shard_map/ppermute | solution.py:280
  29.0 1.6 %collective-permute-start.9 = (bf16[128,1024]{1,0:T(8,128)(2,1)S(1)}, bf16[128,1024]{1,0:T(8,128)(2,1)S(1)}, u32[]{:S(2)}, u32[]{:S(2)}) collective-permute-start(bf16[128,1024]{1,0:T(8,128)(2,1)S(1)} %get-tuple-element.58), channel_id=1, source_target_pairs={{0,1},{1,0},{2,3},{3,2},{4,5},{5,4},{6,7},{7,6},{8,9},{9,8},{10,11... | collective-permute-start | bytes 786440 | tf_op jit(solution)/shard_map/ppermute | solution.py:606
  30.1 5.4 %collective-permute-start.8 = (bf16[128,1536]{1,0:T(8,128)(2,1)S(1)}, bf16[128,1536]{1,0:T(8,128)(2,1)S(1)}, u32[]{:S(2)}, u32[]{:S(2)}) collective-permute-start(bf16[128,1536]{1,0:T(8,128)(2,1)S(1)} %get-tuple-element.55), channel_id=1, source_target_pairs={{0,1},{1,0},{2,3},{3,2},{4,5},{5,4},{6,7},{7,6},{8,9},{9,8},{10,11... | collective-permute-start | bytes 1179656 | tf_op jit(solution)/shard_map/ppermute | solution.py:606
  30.7 9.2 %collective-permute-start.13 = (bf16[128,1024]{1,0:T(8,128)(2,1)S(1)}, bf16[128,1024]{1,0:T(8,128)(2,1)S(1)}, u32[]{:S(2)}, u32[]{:S(2)}) collective-permute-start(bf16[128,1024]{1,0:T(8,128)(2,1)S(1)} %add_pair.4), channel_id=1, source_target_pairs={{0,2},{1,3},{2,0},{3,1},{4,6},{5,7},{6,4},{7,5},{8,10},{9,11},{10,... | collective-permute-start | bytes 786440 | tf_op jit(solution)/shard_map/ppermute | solution.py:645
  35.6 12.8 %collective-permute-start.12 = (bf16[128,1536]{1,0:T(8,128)(2,1)S(1)}, bf16[128,1536]{1,0:T(8,128)(2,1)S(1)}, u32[]{:S(2)}, u32[]{:S(2)}) collective-permute-start(bf16[128,1536]{1,0:T(8,128)(2,1)S(1)} %add_pair.3), channel_id=1, source_target_pairs={{0,2},{1,3},{2,0},{3,1},{4,6},{5,7},{6,4},{7,5},{8,10},{9,11},{10,... | collective-permute-start | bytes 1179656 | tf_op jit(solution)/shard_map/ppermute | solution.py:646
  38.6 3.3 %collective-permute-start.10 = (bf16[128,5632]{1,0:T(8,128)(2,1)S(1)}, bf16[128,5632]{1,0:T(8,128)(2,1)S(1)}, u32[]{:S(2)}, u32[]{:S(2)}) collective-permute-start(bf16[128,5632]{1,0:T(8,128)(2,1)S(1)} %get-tuple-element.63), channel_id=1, source_target_pairs={{0,1},{1,0},{2,3},{3,2},{4,5},{5,4},{6,7},{7,6},{8,9},{9,8},{10,11... | collective-permute-start | bytes 4325384 | tf_op jit(solution)/shard_map/ppermute | solution.py:606
  42.0 14.0 %collective-permute-start.11 = (bf16[128,1536]{1,0:T(8,128)(2,1)S(1)}, bf16[128,1536]{1,0:T(8,128)(2,1)S(1)}, u32[]{:S(2)}, u32[]{:S(2)}) collective-permute-start(bf16[128,1536]{1,0:T(8,128)(2,1)S(1)} %add_pair.5), channel_id=1, source_target_pairs={{0,2},{1,3},{2,0},{3,1},{4,6},{5,7},{6,4},{7,5},{8,10},{9,11},{10,... | collective-permute-start | bytes 1179656 | tf_op jit(solution)/shard_map/ppermute | solution.py:648

commit v4 on v2

--- a/solution.py
+++ b/solution.py
@@ -96,55 +96,53 @@
     return [tail[2 * k:2 * k + 1] + tail[2 * k + 1:2 * k + 2] for k in range(blocks)]
 
 
-def half_message(x_ref, b, wk, first_head, msg):
-    tok, lanes = x_ref.shape
+def quarter_message(x, b, wk, first_head, msg):
+    tok, width = x.shape
     heads2 = wk.shape[0]
-    width = 256
+    spread = dot(wk[...], pick(heads2, width, heads2 // 2, P_SIZE, first_head), ((0,), (0,)))
+    state = dot(b, (x * spread[:tok]).astype(BF), ((0,), (0,)))
     decays = []
-    for g in range(lanes // width):
-        chosen = pick(heads2, width, heads2 // 2, P_SIZE, first_head + g * (width // P_SIZE))
-        spread = dot(wk[...], chosen, ((0,), (0,)))
-        weighted = (x_ref[:, g * width:(g + 1) * width] * spread[:tok]).astype(BF)
-        state = dot(b, weighted, ((0,), (0,)))
-        for i in range(width // LANES):
-            k = g * (width // LANES) + i
-            msg[k * N:(k + 1) * N] = state[:, i * LANES:(i + 1) * LANES].astype(BF)
-            decays.append(spread[tok:tok + 1, i * LANES:(i + 1) * LANES])
+    for k in range(width // LANES):
+        msg[k * N:(k + 1) * N] = state[:, k * LANES:(k + 1) * LANES].astype(BF)
+        decays.append(spread[tok:tok + 1, k * LANES:(k + 1) * LANES])
     msg[msg.shape[0] - 16:] = tail_rows(decays)
 
 
-def half_kernel(give, raw, rate, x, b, msg, wk, aux, raw_v, rate_v, x_v, b_v, sems):
-    lanes = x_v.shape[1]
-    mine = lax.axis_index("seq") % 2
-    half = 1 - mine if give else mine
+def load_quarter(x, x_v, quarter, sem):
+    width = x_v.shape[1]
+    return pltpu.make_async_copy(
+        x.at[:, pl.ds(pl.multiple_of(quarter * width, width), width)], x_v, sem
+    )
+
+
+def give_kernel(raw, rate, x, b, msg1, msg2, msg3, wk, aux, raw_v, rate_v, x_v, b_v, sems):
+    mine = lax.axis_index("seq") % 4
     loads = [
-        pltpu.make_async_copy(b, b_v, sems.at[0]),
-        pltpu.make_async_copy(
-            x.at[:, pl.ds(pl.multiple_of(half * lanes, lanes), lanes)], x_v, sems.at[1]
-        ),
-    ]
-    if give:
-        loads += [
-            pltpu.make_async_copy(raw, raw_v, sems.at[2]),
-            pltpu.make_async_copy(rate, rate_v, sems.at[3]),
-        ]
-    for load in reversed(loads):
+        pltpu.make_async_copy(raw, raw_v, sems.at[0]),
+        pltpu.make_async_copy(rate, rate_v, sems.at[1]),
+        pltpu.make_async_copy(b, b_v, sems.at[2]),
+    ] + [load_quarter(x, x_v.at[k - 1], mine ^ k, sems.at[2 + k]) for k in (1, 2, 3)]
+    for load in loads:
         load.start()
-    if give:
-        loads[2].wait()
-        loads[3].wait()
-        step_vectors(raw_v[...], rate_v[...], wk, aux)
     loads[0].wait()
     loads[1].wait()
-    half_message(x_v, b_v[...].astype(BF), wk, half * (lanes // P_SIZE), msg)
-
-
-def give_kernel(raw, rate, x, b, msg, wk, aux, raw_v, rate_v, x_v, b_v, sems):
-    half_kernel(True, raw, rate, x, b, msg, wk, aux, raw_v, rate_v, x_v, b_v, sems)
+    step_vectors(raw_v[...], rate_v[...], wk, aux)
+    for load in loads[2:]:
+        load.wait()
+    b16 = b_v[...].astype(BF)
+    heads = x_v.shape[2] // P_SIZE
+    for k, msg in ((1, msg1), (2, msg2), (3, msg3)):
+        quarter_message(x_v[k - 1], b16, wk, (mine ^ k) * heads, msg)
 
 
 def keep_kernel(wk, x, b, msg, x_v, b_v, sems):
-    half_kernel(False, None, None, x, b, msg, wk, None, None, None, x_v, b_v, sems)
+    mine = lax.axis_index("seq") % 4
+    loads = [load_quarter(x, x_v, mine, sems.at[0]), pltpu.make_async_copy(b, b_v, sems.at[1])]
+    for load in loads:
+        load.start()
+    for load in loads:
+        load.wait()
+    quarter_message(x_v[...], b_v[...].astype(BF), wk, mine * (x_v.shape[1] // P_SIZE), msg)
 
 
 HBM = pl.BlockSpec(memory_space=pltpu.HBM)
@@ -153,21 +151,21 @@
 
 def give_states(raw, rate, x, b):
     heads, tok = raw.shape
-    lanes = x.shape[1] // 2
+    lanes = x.shape[1] // 4
     return pl.pallas_call(
         give_kernel,
         in_specs=[HBM] * 4,
-        out_shape=[
-            jax.ShapeDtypeStruct((lanes + 16, LANES), BF),
+        out_shape=[jax.ShapeDtypeStruct((lanes // LANES * N + 16, LANES), BF)] * 3
+        + [
             jax.ShapeDtypeStruct((2 * heads, tok + CHUNK), BF),
             jax.ShapeDtypeStruct((tok // CHUNK, 3 * heads, CHUNK), F32),
         ],
         scratch_shapes=[
             pltpu.VMEM((heads, tok), F32),
             pltpu.VMEM((1, heads), F32),
-            pltpu.VMEM((tok, lanes), F32),
+            pltpu.VMEM((3, tok, lanes), F32),
             pltpu.VMEM((tok, N), F32),
-            pltpu.SemaphoreType.DMA((4,)),
+            pltpu.SemaphoreType.DMA((6,)),
         ],
         compiler_params=pltpu.CompilerParams(vmem_limit_bytes=WHOLE_VMEM),
         cost_estimate=pl.CostEstimate(flops=200_000_000, bytes_accessed=1_500_000, transcendentals=0),
@@ -177,11 +175,11 @@
 
 def keep_states(wk, x, b):
     tok = x.shape[0]
-    lanes = x.shape[1] // 2
+    lanes = x.shape[1] // 4
     return pl.pallas_call(
         keep_kernel,
-        in_specs=[pl.BlockSpec(memory_space=pltpu.VMEM), HBM, HBM],
-        out_shape=jax.ShapeDtypeStruct((lanes + 16, LANES), BF),
+        in_specs=[VMEM, HBM, HBM],
+        out_shape=jax.ShapeDtypeStruct((lanes // LANES * N + 16, LANES), BF),
         scratch_shapes=[
             pltpu.VMEM((tok, lanes), F32),
             pltpu.VMEM((tok, N), F32),
@@ -243,26 +241,48 @@
         link(ahead, come, out)
 
 
-def end_kernel(distance, ahead, last, own, come, mine, theirs):
-    blocks = mine.shape[0] // N
+def by_section(work):
+    mine = lax.axis_index("seq") % 4
+    for v in range(4):
+        pl.when(mine == v)(functools.partial(work, [j ^ v for j in range(4)]))
+
+
+def join_four_kernel(own, come1, come2, come3, out):
+    messages = (own, come1, come2, come3)
+
+    def work(place):
+        sections = [messages[p] for p in place]
+        decays = [decays_of(section) for section in sections]
+        for k in range(len(decays[0])):
+            rows = slice(k * N, (k + 1) * N)
+            total = sections[0][rows].astype(F32)
+            for section, decay in zip(sections[1:], decays[1:]):
+                total = section[rows].astype(F32) + decay[k] * total
+            out[rows] = total.astype(BF)
+        spans = [p * q * r * t for p, q, r, t in zip(*decays)]
+        out[len(spans) * N:] = tail_rows(spans)
+
+    by_section(work)
+
+
+def end_kernel(distance, ahead, last, own, come1, come2, come3, mine, out1, out2, out3):
+    messages, outs = (own, come1, come2, come3), (mine, out1, out2, out3)
     weight = is_later(distance).astype(F32)
-    odd = is_later(1)
-
-    def fill(even_section, ahead_ref, behind_ref):
-        step, span = decays_of(ahead), decays_of(even_section)
-        for k in range(blocks):
+
+    def work(place):
+        sections, targets = [messages[p] for p in place], [outs[p] for p in place]
+        decays = [decays_of(section) for section in sections]
+        for k in range(len(decays[0])):
             rows = slice(k * N, (k + 1) * N)
-            start = ahead[rows].astype(F32) + (weight * step[k]) * last[rows].astype(F32)
-            ahead_ref[rows] = start.astype(BF)
-            behind_ref[rows] = (even_section[rows].astype(F32) + span[k] * start).astype(BF)
-
-    @pl.when(odd == 0)
-    def _():
-        fill(own, mine, theirs)
-
-    @pl.when(odd == 1)
-    def _():
-        fill(come, theirs, mine)
+            state = weight * last[rows].astype(F32)
+            if ahead is not None:
+                state = ahead[rows].astype(F32) + decays_of(ahead)[k] * state
+            for j in range(4):
+                targets[j][rows] = state.astype(BF)
+                if j < 3:
+                    state = sections[j][rows].astype(F32) + decays[j][k] * state
+
+    by_section(work)
 
 
 def scan_call(kernel, operands, shapes, name):
@@ -275,29 +295,33 @@
     )(*operands)
 
 
-def incoming_states(give, keep, count, hold):
+def incoming_states(gives, keep, count, hold):
     def exchange(value, distance):
         return lax.ppermute(value, "seq", [(s, s ^ distance) for s in range(count)])
 
-    def joined(kernel, distance, *operands):
-        name = kernel.__name__[:-len("_kernel")]
-        return scan_call(functools.partial(kernel, distance), operands, [keep.shape], name)[0]
-
-    come = exchange(give, 1)
-    run, distance = joined(run_kernel, 1, keep, come), 2
+    def joined(kernel, *operands):
+        return scan_call(kernel, operands, [keep.shape], "join_states")[0]
+
+    parts = [keep] + [exchange(give, k) for k, give in zip((1, 2, 3), gives)]
+    run, ahead, distance = joined(join_four_kernel, *parts), None, 4
     got = exchange(run, distance)
-    ahead = joined(first_ahead_kernel, distance, got)
     while distance * 2 < count:
-        run, distance = joined(run_kernel, distance, run, got), distance * 2
+        if ahead is None:
+            ahead = joined(functools.partial(first_ahead_kernel, distance), got)
+        else:
+            ahead = joined(functools.partial(ahead_kernel, distance), ahead, got)
+        run = joined(functools.partial(run_kernel, distance), run, got)
+        distance *= 2
         got = exchange(run, distance)
-        if distance * 2 < count:
-            ahead = joined(ahead_kernel, distance, ahead, got)
-    hold, got = hold(got)
-    half = (keep.shape[0] - 16, LANES)
-    mine, theirs = scan_call(
-        functools.partial(end_kernel, distance), (ahead, got, keep, come), [half, half], "join_end"
-    )
-    return hold, mine, exchange(theirs, 1)
+    hold, got = lax.optimization_barrier((hold, got))
+    operands = [got] + parts
+    if ahead is None:
+        kernel = functools.partial(end_kernel, distance, None)
+    else:
+        kernel, operands = functools.partial(end_kernel, distance), [ahead] + operands
+    shape = (keep.shape[0] - 16, LANES)
+    outs = scan_call(kernel, operands, [shape] * 4, "join_end")
+    return hold, [outs[0]] + [exchange(out, k) for k, out in zip((1, 2, 3), outs[1:])]
 
 
 def rows_of(ref, block):
@@ -408,7 +432,7 @@
     c = c.astype(BF)
     blocks = incoming.shape[1] // N
     carried = jnp.concatenate(
-        [dot(c, incoming[h, k * N:(k + 1) * N]) for h in range(2) for k in range(blocks)], axis=1
+        [dot(c, incoming[q, k * N:(k + 1) * N]) for q in range(4) for k in range(blocks)], axis=1
     )
     gated = own + lead * carried
     mean = jnp.mean(gated * gated, axis=1, keepdims=True)
@@ -421,10 +445,10 @@
     )
 
 
-def fill_incoming(here, there, incoming):
-    odd = lax.axis_index("seq") % 2
-    incoming[odd] = here[...]
-    incoming[1 - odd] = there[...]
+def fill_incoming(quarters, incoming):
+    mine = lax.axis_index("seq") % 4
+    for k, quarter in enumerate(quarters):
+        incoming[mine ^ k] = quarter[...]
 
 
 def project_both(normed, w, start, columns, theirs, mine, at=0):
@@ -435,9 +459,11 @@
         mine[:, k:k + wide] = out[CHUNK:]
 
 
-def far_kernel(columns, own, lead, c, here, there, gain, w, theirs, mine, normed, incoming):
+def far_kernel(
+    columns, own, lead, c, q0, q1, q2, q3, gain, w, theirs, mine, normed, incoming
+):
     me = lax.axis_index("head")
-    fill_incoming(here, there, incoming)
+    fill_incoming((q0, q1, q2, q3), incoming)
     normed[:CHUNK] = finish_block(me ^ 3, own, lead, c, incoming, gain)
     normed[CHUNK:] = finish_block(me ^ 2, own, lead, c, incoming, gain)
     project_both(normed, w, 0, columns, theirs, mine)
@@ -448,11 +474,12 @@
 
 
 def mixed_kernel(
-    start, columns, normed, own, lead, c, here, there, gain, w, theirs, mine, kept, incoming, given
+    start, columns, normed, own, lead, c, q0, q1, q2, q3, gain, w,
+    theirs, mine, kept, incoming, given,
 ):
     me = lax.axis_index("head")
     project_both(normed, w, start, columns, theirs, mine)
-    fill_incoming(here, there, incoming)
+    fill_incoming((q0, q1, q2, q3), incoming)
     given[...] = finish_block(me ^ 1, own, lead, c, incoming, gain)
     kept[...] = finish_block(me, own, lead, c, incoming, gain)
     wide = 512
@@ -576,21 +603,19 @@
     heads = decay_log.shape[0]
     b = state_in.reshape(tok, N)
     c = state_out.reshape(tok, N)
-    give, wk, aux = give_states(step_raw.T, decay_log.reshape(1, heads), ssm_input, b)
+    *gives, wk, aux = give_states(step_raw.T, decay_log.reshape(1, heads), ssm_input, b)
     keep = keep_states(wk, ssm_input, b)
     inputs = (ssm_input, b, c, gate_input, skip_gain.reshape(1, heads))
     local = within(True, aux, *inputs)
-    (own, lead), here, there = incoming_states(
-        give, keep, seq_count, lambda got: lax.optimization_barrier((local, got))
-    )
+    (own, lead), quarters = incoming_states(gives, keep, seq_count, local)
 
     near = [(h, h ^ 1) for h in range(4)]
     far = [(h, h ^ 2) for h in range(4)]
     gain = norm_gain.reshape(1, -1)
     channels, dout = out_weight.shape
     rows = CHUNK
-    states = pltpu.VMEM((2,) + here.shape, BF)
-    finish = (own, lead, c, here, there, gain, out_weight)
+    states = pltpu.VMEM((4,) + quarters[0].shape, BF)
+    finish = (own, lead, c, *quarters, gain, out_weight)
     (_, one), (start2, two), (start3, three) = PIECES
 
     def piece_outs(columns, extra=0):

time: 56.9 us -> 55.4 us (0.974)
  waiting for transfers between devices: 22.9 us -> 20.4 us
  starting transfers between devices: 14.2 us -> 15.2 us
    ppermute x4 -> x7, waiting for transfers between devices: 9.76 us -> 7.08 us  [exchange(): return lax.ppermute(value, 'seq', [(s, s ^ distance) for s in range(count)])]
    ppermute x4 -> x7, starting transfers between devices: 9.54 us -> 10.8 us  [exchange(): return lax.ppermute(value, 'seq', [(s, s ^ distance) for s in range(count)])]
  transfers between devices with their start and end apart: 10 -> 13, of which waited for: 8 -> 9; matrix products, arithmetic and copies ran while one was open for 0% -> 0% of each run, Pallas kernels for 24% -> 23%
where the time goes in v4:
time: 55.4 us; the launch traced here: 55.3 us
  waiting for transfers between devices  20.4 us (37%)
  Pallas kernels  18.5 us (33%)
  starting transfers between devices  15.2 us (27%)
  local copies, waits for them, and re-layouts  0.81 us (1%)
    ppermute x7, starting transfers between devices, exchange(): return lax.ppermute(value, 'seq', [(s, s ^ distance) for s in range(count)])  10.8 us
    ppermute x7, waiting for transfers between devices, exchange(): return lax.ppermute(value, 'seq', [(s, s ^ distance) for s in range(count)])  7.08 us
    pallas_call x2, Pallas kernels, within(): pl.pallas_call(functools.partial(within_kernel, far), in_specs=[VMEM] * 6...  6.38 us
    pallas_call x7, Pallas kernels, local_call(): pl.pallas_call(kernel, in_specs=[VMEM] * len(operands), out_specs=[VMEM]...  6.1 us
    ppermute x1, waiting for transfers between devices, per_device(): third, filled = await_piece(lax.ppermute(third, 'head', far), filled)  5.29 us
    ppermute x1, waiting for transfers between devices, per_device(): second, first = await_piece(lax.ppermute(second, 'head', far), first)  4.79 us
    pallas_call x1, Pallas kernels, give_states(): pl.pallas_call(give_kernel, in_specs=[HBM] * 4, out_shape=[jax.ShapeDtype...  3.33 us
    ppermute x3, waiting for transfers between devices, add(): come = lax.ppermute(theirs, 'head', near)  2.01 us
  transfers between devices with their start and end apart: 13, of which 9 were waited for; matrix products, arithmetic and copies ran while one was open for 0% of the time, Pallas kernels for 23%

profile of v4, /device:TPU:0, one launch (start us, length us, event | category | flops | bytes accessed | tf_op | source)
XLA Modules:
  0.0 55.3 jit_solution(8544140872260070109)
XLA Ops:
  0.0 3.3 %give_states.1 = (bf16[272,128]{1,0:T(8,128)(2,1)}, bf16[272,128]{1,0:T(8,128)(2,1)}, bf16[272,128]{1,0:T(8,128)(2,1)}, bf16[32,640]{1,0:T(8,128)(2,1)}, f32[4,48,128]{2,1,0:T(8,128)}) custom-call(f32[16,512]{1,0:T(8,128)} %bitcast.20, f32[1,16]{1,0:T(1,128)} %bitcast.21, f32[512,1024]{1,0:T(8,128)} %x_ref.3, f32[512,128]{1,0:T(8,128)} %bitcast.8), custom_call_target="tpu_custom_call" | custom-call | flops 200000000 | bytes 1500000 | tf_op jit(solution)/shard_map/give_states/pallas_call | solution.py:155
  3.4 3.0 %collective-permute-start = (bf16[272,128]{1,0:T(8,128)(2,1)}, bf16[272,128]{1,0:T(8,128)(2,1)S(1)}, u32[]{:S(2)}, u32[]{:S(2)}) collective-permute-start(bf16[272,128]{1,0:T(8,128)(2,1)} %get-tuple-element.41), channel_id=1, source_target_pairs={{0,4},{4,0},{8,12},{12,8},{16,20},{20,16},{24,28},{28,24},{1,5},{5... | collective-permute-start | bytes 208904 | tf_op jit(solution)/shard_map/ppermute | solution.py:300
  6.4 1.6 %collective-permute-start.1 = (bf16[272,128]{1,0:T(8,128)(2,1)}, bf16[272,128]{1,0:T(8,128)(2,1)S(1)}, u32[]{:S(2)}, u32[]{:S(2)}) collective-permute-start(bf16[272,128]{1,0:T(8,128)(2,1)} %get-tuple-element.42), channel_id=1, source_target_pairs={{0,8},{4,12},{8,0},{12,4},{16,24},{20,28},{24,16},{28,20},{1,9},{5... | collective-permute-start | bytes 208904 | tf_op jit(solution)/shard_map/ppermute | solution.py:300
  8.0 0.8 %copy-done.3 = bf16[32,640]{1,0:T(8,128)(2,1)S(1)} copy-done((bf16[32,640]{1,0:T(8,128)(2,1)S(1)}, bf16[32,640]{1,0:T(8,128)(2,1)}, u32[]{:S(2)}) %copy-start.3) | copy-done | bytes 40984
  9.3 2.2 %collective-permute-done.1.come2 = bf16[272,128]{1,0:T(8,128)(2,1)S(1)} collective-permute-done((bf16[272,128]{1,0:T(8,128)(2,1)}, bf16[272,128]{1,0:T(8,128)(2,1)S(1)}, u32[]{:S(2)}, u32[]{:S(2)}) %collective-permute-start.1) | collective-permute-done | bytes 69664 | tf_op jit(solution)/shard_map/ppermute | solution.py:300
  11.5 1.9 %collective-permute-done.2.come3 = bf16[272,128]{1,0:T(8,128)(2,1)S(1)} collective-permute-done((bf16[272,128]{1,0:T(8,128)(2,1)}, bf16[272,128]{1,0:T(8,128)(2,1)S(1)}, u32[]{:S(2)}, u32[]{:S(2)}) %collective-permute-start.2) | collective-permute-done | bytes 69664 | tf_op jit(solution)/shard_map/ppermute | solution.py:300
  13.4 2.7 %collective-permute-start.3 = (bf16[272,128]{1,0:T(8,128)(2,1)S(1)}, bf16[272,128]{1,0:T(8,128)(2,1)S(1)}, u32[]{:S(2)}, u32[]{:S(2)}) collective-permute-start(bf16[272,128]{1,0:T(8,128)(2,1)S(1)} %join_states.1), channel_id=1, source_target_pairs={{0,16},{4,20},{8,24},{12,28},{16,0},{20,4},{24,8},{28,12},{1,17},{... | collective-permute-start | bytes 208904 | tf_op jit(solution)/shard_map/ppermute | solution.py:300
  16.1 3.2 %within_far.1 = (f32[256,1024]{1,0:T(8,128)S(1)}, f32[256,1024]{1,0:T(8,128)S(1)}) custom-call(f32[4,48,128]{2,1,0:T(8,128)S(1)} %copy-done.6, f32[512,1024]{1,0:T(8,128)S(1)} %copy-done, f32[512,128]{1,0:T(8,128)S(1)} %bitcast.10, f32[512,128]{1,0:T(8,128)S(1)} %bitcast.12, bf16[512,1024]{1,0:T(8,128)(2,1)S(1)} %copy-done.5, f32[1,16]{1,0:T(1,128)S(1)} %bitcast.18), custom_call_target="tpu_custom_call" | custom-call | flops 4000000000 | bytes 3000000 | tf_op jit(solution)/shard_map/within_far/pallas_call | solution.py:418
  21.1 2.1 %collective-permute-start.6 = (bf16[256,128]{1,0:T(8,128)(2,1)S(1)}, bf16[256,128]{1,0:T(8,128)(2,1)S(1)}, u32[]{:S(2)}, u32[]{:S(2)}) collective-permute-start(bf16[256,128]{1,0:T(8,128)(2,1)S(1)} %get-tuple-element.50), channel_id=1, source_target_pairs={{0,12},{4,8},{8,4},{12,0},{16,28},{20,24},{24,20},{28,16},{1,13},{... | collective-permute-start | bytes 196616 | tf_op jit(solution)/shard_map/ppermute | solution.py:300
  23.2 0.8 %collective-permute-done.4.q1 = bf16[256,128]{1,0:T(8,128)(2,1)S(1)} collective-permute-done((bf16[256,128]{1,0:T(8,128)(2,1)S(1)}, bf16[256,128]{1,0:T(8,128)(2,1)S(1)}, u32[]{:S(2)}, u32[]{:S(2)}) %collective-permute-start.4) | collective-permute-done | bytes 65568 | tf_op jit(solution)/shard_map/ppermute | solution.py:300
  24.6 1.7 %collective-permute-done.6.q3 = bf16[256,128]{1,0:T(8,128)(2,1)S(1)} collective-permute-done((bf16[256,128]{1,0:T(8,128)(2,1)S(1)}, bf16[256,128]{1,0:T(8,128)(2,1)S(1)}, u32[]{:S(2)}, u32[]{:S(2)}) %collective-permute-start.6) | collective-permute-done | bytes 65568 | tf_op jit(solution)/shard_map/ppermute | solution.py:300
  26.3 1.1 %finish_far.1 = (bf16[128,1024]{1,0:T(8,128)(2,1)S(1)}, f32[128,1024]{1,0:T(8,128)S(1)}, bf16[256,1024]{1,0:T(8,128)(2,1)S(1)}) custom-call(f32[256,1024]{1,0:T(8,128)S(1)} %get-tuple-element.44.own, f32[256,1024]{1,0:T(8,128)S(1)} %get-tuple-element.45.lead, f32[512,128]{1,0:T(8,128)S(1)} %bitcast.13, bf16[256,128]{1,0:T(8,128)(2,1)S(1)} %get-tuple-element.47.q0, ...), custom_call_target="tpu_custom_call" | custom-call | flops 536870912 | tf_op jit(solution)/shard_map/finish_far/pallas_call | solution.py:503
  27.4 1.0 %project_more.1 = (bf16[128,1536]{1,0:T(8,128)(2,1)S(1)}, f32[128,1536]{1,0:T(8,128)S(1)}) custom-call(bf16[256,1024]{1,0:T(8,128)(2,1)S(1)} %get-tuple-element.54.normed, bf16[1024,4096]{1,0:T(8,128)(2,1)S(1)} %bitcast.7), custom_call_target="tpu_custom_call" | custom-call | flops 805306368 | tf_op jit(solution)/shard_map/project_more/pallas_call | solution.py:503
  29.1 1.6 %collective-permute-start.12 = (bf16[128,1024]{1,0:T(8,128)(2,1)S(1)}, bf16[128,1024]{1,0:T(8,128)(2,1)S(1)}, u32[]{:S(2)}, u32[]{:S(2)}) collective-permute-start(bf16[128,1024]{1,0:T(8,128)(2,1)S(1)} %add_pair.4), channel_id=1, source_target_pairs={{0,2},{1,3},{2,0},{3,1},{4,6},{5,7},{6,4},{7,5},{8,10},{9,11},{10,... | collective-permute-start | bytes 786440 | tf_op jit(solution)/shard_map/ppermute | solution.py:664
  30.6 3.2 %within_near.1 = (f32[256,1024]{1,0:T(8,128)S(1)}, f32[256,1024]{1,0:T(8,128)S(1)}) custom-call(f32[4,48,128]{2,1,0:T(8,128)S(1)} %copy-done.6, f32[512,1024]{1,0:T(8,128)S(1)} %copy-done, f32[512,128]{1,0:T(8,128)S(1)} %bitcast.11, f32[512,128]{1,0:T(8,128)S(1)} %bitcast.14, bf16[512,1024]{1,0:T(8,128)(2,1)S(1)} %copy-done.5, f32[1,16]{1,0:T(1,128)S(1)} %bitcast.19), custom_call_target="tpu_custom_call" | custom-call | flops 4000000000 | bytes 3000000 | tf_op jit(solution)/shard_map/within_near/pallas_call | solution.py:418
  34.5 2.5 %finish_near.1 = (bf16[128,5632]{1,0:T(8,128)(2,1)S(1)}, f32[128,1536]{1,0:T(8,128)S(1)}, bf16[128,1024]{1,0:T(8,128)(2,1)S(1)}) custom-call(bf16[256,1024]{1,0:T(8,128)(2,1)S(1)} %get-tuple-element.54.normed, f32[256,1024]{1,0:T(8,128)S(1)} %get-tuple-element.58.own, f32[256,1024]{1,0:T(8,128)S(1)} %get-tuple-element.59.lead, f32[512,128]{1,0:T(8,128)S(1)} %bitcast.15, ...), custom_call_target="tpu_custom_call" | custom-call | flops 1879048192 | tf_op jit(solution)/shard_map/finish_near/pallas_call | solution.py:503
  37.1 1.2 %collective-permute-done.12.refs_0_ = bf16[128,1024]{1,0:T(8,128)(2,1)S(1)} collective-permute-done((bf16[128,1024]{1,0:T(8,128)(2,1)S(1)}, bf16[128,1024]{1,0:T(8,128)(2,1)S(1)}, u32[]{:S(2)}, u32[]{:S(2)}) %collective-permute-start.12) | collective-permute-done | bytes 262176 | tf_op jit(solution)/shard_map/ppermute | solution.py:664
  38.3 2.0 %collective-permute-done.9.come = bf16[128,5632]{1,0:T(8,128)(2,1)S(1)} collective-permute-done((bf16[128,5632]{1,0:T(8,128)(2,1)S(1)}, bf16[128,5632]{1,0:T(8,128)(2,1)S(1)}, u32[]{:S(2)}, u32[]{:S(2)}) %collective-permute-start.9) | collective-permute-done | bytes 1441824 | tf_op jit(solution)/shard_map/ppermute | solution.py:625
  40.3 1.6 %collective-permute-start.10 = (bf16[128,1536]{1,0:T(8,128)(2,1)S(1)}, bf16[128,1536]{1,0:T(8,128)(2,1)S(1)}, u32[]{:S(2)}, u32[]{:S(2)}) collective-permute-start(bf16[128,1536]{1,0:T(8,128)(2,1)S(1)} %add_pair.5), channel_id=1, source_target_pairs={{0,2},{1,3},{2,0},{3,1},{4,6},{5,7},{6,4},{7,5},{8,10},{9,11},{10,... | collective-permute-start | bytes 1179656 | tf_op jit(solution)/shard_map/ppermute | solution.py:667
  41.9 4.8 %collective-permute-done.11.refs_0_ = bf16[128,1536]{1,0:T(8,128)(2,1)S(1)} collective-permute-done((bf16[128,1536]{1,0:T(8,128)(2,1)S(1)}, bf16[128,1536]{1,0:T(8,128)(2,1)S(1)}, u32[]{:S(2)}, u32[]{:S(2)}) %collective-permute-start.11) | collective-permute-done | bytes 393248 | tf_op jit(solution)/shard_map/ppermute | solution.py:665
  46.7 1.3 %project_kept.1.kept = f32[128,4096]{1,0:T(8,128)S(1)} custom-call(bf16[128,1024]{1,0:T(8,128)(2,1)S(1)} %get-tuple-element.60.kept, bf16[128,5632]{1,0:T(8,128)(2,1)S(1)} %collective-permute-done.9.come, bf16[1024,4096]{1,0:T(8,128)(2,1)S(1)} %bitcast.7), custom_call_target="tpu_custom_call" | custom-call | flops 1073741824 | tf_op jit(solution)/shard_map/project_kept/pallas_call | solution.py:503
  48.0 1.0 %early_sums.1.refs_1_ = bf16[128,4096]{1,0:T(8,128)(2,1)} custom-call(f32[128,4096]{1,0:T(8,128)S(1)} %project_kept.1.kept, bf16[128,1024]{1,0:T(8,128)(2,1)S(1)} %get-tuple-element.65.first, bf16[128,1536]{1,0:T(8,128)(2,1)S(1)} %get-tuple-element.66.second), custom_call_target="tpu_custom_call" | custom-call | tf_op jit(solution)/shard_map/early_sums/pallas_call | solution.py:546
  49.0 5.3 %collective-permute-done.10.refs_0_ = bf16[128,1536]{1,0:T(8,128)(2,1)S(1)} collective-permute-done((bf16[128,1536]{1,0:T(8,128)(2,1)S(1)}, bf16[128,1536]{1,0:T(8,128)(2,1)S(1)}, u32[]{:S(2)}, u32[]{:S(2)}) %collective-permute-start.10) | collective-permute-done | bytes 393248 | tf_op jit(solution)/shard_map/ppermute | solution.py:667
  54.3 0.8 %last_sums.1 = bf16[128,4096]{1,0:T(8,128)(2,1)} custom-call(f32[128,4096]{1,0:T(8,128)S(1)} %project_kept.1.kept, bf16[128,1536]{1,0:T(8,128)(2,1)S(1)} %get-tuple-element.67.third, bf16[128,4096]{1,0:T(8,128)(2,1)} %get-tuple-element.68.filled), custom_call_target="tpu_custom_call", output_to_operand_aliasing={{}: (2, {})} | custom-call | tf_op jit(solution)/shard_map/last_sums/pallas_call | solution.py:578
  (41 shorter events, 4.5 us)
Async XLA Ops:
  0.0 8.0 %copy-start = (f32[512,1024]{1,0:T(8,128)S(1)}, f32[512,1024]{1,0:T(8,128)}, u32[]{:S(2)}) copy-start(f32[512,1024]{1,0:T(8,128)} %x_ref.3) | copy-start | bytes 6291460
  0.0 8.0 %copy-start.1 = (f32[512,1,128]{2,1,0:T(1,128)S(1)}, f32[512,1,128]{2,1,0:T(1,128)}, u32[]{:S(2)}) copy-start(f32[512,1,128]{2,1,0:T(1,128)} %param.13) | copy-start | bytes 786436
  0.0 16.1 %copy-start.7 = (f32[16]{0:T(128)S(1)}, f32[16]{0:T(128)}, u32[]{:S(2)}) copy-start(f32[16]{0:T(128)} %param.15) | copy-start | bytes 196
  3.3 12.8 %copy-start.2 = (f32[512,1,128]{2,1,0:T(1,128)S(1)}, f32[512,1,128]{2,1,0:T(1,128)}, u32[]{:S(2)}) copy-start(f32[512,1,128]{2,1,0:T(1,128)} %param.14) | copy-start | bytes 786436
  3.4 6.0 %collective-permute-start = (bf16[272,128]{1,0:T(8,128)(2,1)}, bf16[272,128]{1,0:T(8,128)(2,1)S(1)}, u32[]{:S(2)}, u32[]{:S(2)}) collective-permute-start(bf16[272,128]{1,0:T(8,128)(2,1)} %get-tuple-element.41), channel_id=1, source_target_pairs={{0,4},{4,0},{8,12},{12,8},{16,20},{20,16},{24,28},{28,24},{1,5},{5... | collective-permute-start | bytes 208904 | tf_op jit(solution)/shard_map/ppermute | solution.py:300
  6.4 5.1 %collective-permute-start.1 = (bf16[272,128]{1,0:T(8,128)(2,1)}, bf16[272,128]{1,0:T(8,128)(2,1)S(1)}, u32[]{:S(2)}, u32[]{:S(2)}) collective-permute-start(bf16[272,128]{1,0:T(8,128)(2,1)} %get-tuple-element.42), channel_id=1, source_target_pairs={{0,8},{4,12},{8,0},{12,4},{16,24},{20,28},{24,16},{28,20},{1,9},{5... | collective-permute-start | bytes 208904 | tf_op jit(solution)/shard_map/ppermute | solution.py:300
  7.9 5.4 %collective-permute-start.2 = (bf16[272,128]{1,0:T(8,128)(2,1)}, bf16[272,128]{1,0:T(8,128)(2,1)S(1)}, u32[]{:S(2)}, u32[]{:S(2)}) collective-permute-start(bf16[272,128]{1,0:T(8,128)(2,1)} %get-tuple-element.43), channel_id=1, source_target_pairs={{0,12},{4,8},{8,4},{12,0},{16,28},{20,24},{24,20},{28,16},{1,13},{... | collective-permute-start | bytes 208904 | tf_op jit(solution)/shard_map/ppermute | solution.py:300
  8.0 0.8 %copy-start.3 = (bf16[32,640]{1,0:T(8,128)(2,1)S(1)}, bf16[32,640]{1,0:T(8,128)(2,1)}, u32[]{:S(2)}) copy-start(bf16[32,640]{1,0:T(8,128)(2,1)} %get-tuple-element.40.wk) | copy-start | bytes 122884
  8.7 7.4 %copy-start.5 = (bf16[512,1024]{1,0:T(8,128)(2,1)S(1)}, bf16[512,1024]{1,0:T(8,128)(2,1)}, u32[]{:S(2)}) copy-start(bf16[512,1024]{1,0:T(8,128)(2,1)} %gate_ref.3) | copy-start | bytes 3145732
  8.7 7.4 %copy-start.6 = (f32[4,48,128]{2,1,0:T(8,128)S(1)}, f32[4,48,128]{2,1,0:T(8,128)}, u32[]{:S(2)}) copy-start(f32[4,48,128]{2,1,0:T(8,128)} %get-tuple-element.57.aux) | copy-start | bytes 294916
  13.4 5.9 %collective-permute-start.3 = (bf16[272,128]{1,0:T(8,128)(2,1)S(1)}, bf16[272,128]{1,0:T(8,128)(2,1)S(1)}, u32[]{:S(2)}, u32[]{:S(2)}) collective-permute-start(bf16[272,128]{1,0:T(8,128)(2,1)S(1)} %join_states.1), channel_id=1, source_target_pairs={{0,16},{4,20},{8,24},{12,28},{16,0},{20,4},{24,8},{28,12},{1,17},{... | collective-permute-start | bytes 208904 | tf_op jit(solution)/shard_map/ppermute | solution.py:300
  16.1 10.1 %slice-start = ((s8[8388608]{0:T(1024)(128)(4,1)}), s8[4194304]{0:T(1024)(128)(4,1)S(1)}, s32[]{:S(2)}) async-start(s8[8388608]{0:T(1024)(128)(4,1)} %bitcast.6), calls=%async_computation | async-start | bytes 8388608
  16.1 10.1 %slice-start.1 = ((s8[8388608]{0:T(1024)(128)(4,1)}), s8[4194304]{0:T(1024)(128)(4,1)S(1)}, s32[]{:S(2)}) async-start(s8[8388608]{0:T(1024)(128)(4,1)} %bitcast.6), calls=%async_computation.1 | async-start | bytes 8388608
  16.1 10.1 %copy-start.4 = (f32[1024]{0:T(1024)S(1)}, f32[1024]{0:T(1024)}, u32[]{:S(2)}) copy-start(f32[1024]{0:T(1024)} %param.16) | copy-start | bytes 12292
  19.6 4.3 %collective-permute-start.4 = (bf16[256,128]{1,0:T(8,128)(2,1)S(1)}, bf16[256,128]{1,0:T(8,128)(2,1)S(1)}, u32[]{:S(2)}, u32[]{:S(2)}) collective-permute-start(bf16[256,128]{1,0:T(8,128)(2,1)S(1)} %get-tuple-element.48), channel_id=1, source_target_pairs={{0,4},{4,0},{8,12},{12,8},{16,20},{20,16},{24,28},{28,24},{1,5},{5... | collective-permute-start | bytes 196616 | tf_op jit(solution)/shard_map/ppermute | solution.py:300
  20.3 4.3 %collective-permute-start.5 = (bf16[256,128]{1,0:T(8,128)(2,1)S(1)}, bf16[256,128]{1,0:T(8,128)(2,1)S(1)}, u32[]{:S(2)}, u32[]{:S(2)}) collective-permute-start(bf16[256,128]{1,0:T(8,128)(2,1)S(1)} %get-tuple-element.49), channel_id=1, source_target_pairs={{0,8},{4,12},{8,0},{12,4},{16,24},{20,28},{24,16},{28,20},{1,9},{5... | collective-permute-start | bytes 196616 | tf_op jit(solution)/shard_map/ppermute | solution.py:300
  21.1 5.2 %collective-permute-start.6 = (bf16[256,128]{1,0:T(8,128)(2,1)S(1)}, bf16[256,128]{1,0:T(8,128)(2,1)S(1)}, u32[]{:S(2)}, u32[]{:S(2)}) collective-permute-start(bf16[256,128]{1,0:T(8,128)(2,1)S(1)} %get-tuple-element.50), channel_id=1, source_target_pairs={{0,12},{4,8},{8,4},{12,0},{16,28},{20,24},{24,20},{28,16},{1,13},{... | collective-permute-start | bytes 196616 | tf_op jit(solution)/shard_map/ppermute | solution.py:300
  27.4 1.6 %collective-permute-start.8 = (bf16[128,1024]{1,0:T(8,128)(2,1)S(1)}, bf16[128,1024]{1,0:T(8,128)(2,1)S(1)}, u32[]{:S(2)}, u32[]{:S(2)}) collective-permute-start(bf16[128,1024]{1,0:T(8,128)(2,1)S(1)} %get-tuple-element.56), channel_id=1, source_target_pairs={{0,1},{1,0},{2,3},{3,2},{4,5},{5,4},{6,7},{7,6},{8,9},{9,8},{10,11... | collective-permute-start | bytes 786440 | tf_op jit(solution)/shard_map/ppermute | solution.py:625
  28.4 5.4 %collective-permute-start.7 = (bf16[128,1536]{1,0:T(8,128)(2,1)S(1)}, bf16[128,1536]{1,0:T(8,128)(2,1)S(1)}, u32[]{:S(2)}, u32[]{:S(2)}) collective-permute-start(bf16[128,1536]{1,0:T(8,128)(2,1)S(1)} %get-tuple-element.53), channel_id=1, source_target_pairs={{0,1},{1,0},{2,3},{3,2},{4,5},{5,4},{6,7},{7,6},{8,9},{9,8},{10,11... | collective-permute-start | bytes 1179656 | tf_op jit(solution)/shard_map/ppermute | solution.py:625
  29.1 9.2 %collective-permute-start.12 = (bf16[128,1024]{1,0:T(8,128)(2,1)S(1)}, bf16[128,1024]{1,0:T(8,128)(2,1)S(1)}, u32[]{:S(2)}, u32[]{:S(2)}) collective-permute-start(bf16[128,1024]{1,0:T(8,128)(2,1)S(1)} %add_pair.4), channel_id=1, source_target_pairs={{0,2},{1,3},{2,0},{3,1},{4,6},{5,7},{6,4},{7,5},{8,10},{9,11},{10,... | collective-permute-start | bytes 786440 | tf_op jit(solution)/shard_map/ppermute | solution.py:664
  33.9 12.8 %collective-permute-start.11 = (bf16[128,1536]{1,0:T(8,128)(2,1)S(1)}, bf16[128,1536]{1,0:T(8,128)(2,1)S(1)}, u32[]{:S(2)}, u32[]{:S(2)}) collective-permute-start(bf16[128,1536]{1,0:T(8,128)(2,1)S(1)} %add_pair.3), channel_id=1, source_target_pairs={{0,2},{1,3},{2,0},{3,1},{4,6},{5,7},{6,4},{7,5},{8,10},{9,11},{10,... | collective-permute-start | bytes 1179656 | tf_op jit(solution)/shard_map/ppermute | solution.py:665
  37.0 3.3 %collective-permute-start.9 = (bf16[128,5632]{1,0:T(8,128)(2,1)S(1)}, bf16[128,5632]{1,0:T(8,128)(2,1)S(1)}, u32[]{:S(2)}, u32[]{:S(2)}) collective-permute-start(bf16[128,5632]{1,0:T(8,128)(2,1)S(1)} %get-tuple-element.61), channel_id=1, source_target_pairs={{0,1},{1,0},{2,3},{3,2},{4,5},{5,4},{6,7},{7,6},{8,9},{9,8},{10,11... | collective-permute-start | bytes 4325384 | tf_op jit(solution)/shard_map/ppermute | solution.py:625
  40.3 14.0 %collective-permute-start.10 = (bf16[128,1536]{1,0:T(8,128)(2,1)S(1)}, bf16[128,1536]{1,0:T(8,128)(2,1)S(1)}, u32[]{:S(2)}, u32[]{:S(2)}) collective-permute-start(bf16[128,1536]{1,0:T(8,128)(2,1)S(1)} %add_pair.5), channel_id=1, source_target_pairs={{0,2},{1,3},{2,0},{3,1},{4,6},{5,7},{6,4},{7,5},{8,10},{9,11},{10,... | collective-permute-start | bytes 1179656 | tf_op jit(solution)/shard_map/ppermute | solution.py:667

commit v5 on v4

--- a/solution.py
+++ b/solution.py
@@ -302,7 +302,9 @@
     def joined(kernel, *operands):
         return scan_call(kernel, operands, [keep.shape], "join_states")[0]
 
-    parts = [keep] + [exchange(give, k) for k, give in zip((1, 2, 3), gives)]
+    come = {k: exchange(gives[k - 1], k) for k in (3, 2, 1)}
+    parts = [keep] + [come[k] for k in (1, 2, 3)]
+    hold, parts = lax.optimization_barrier((hold, parts))
     run, ahead, distance = joined(join_four_kernel, *parts), None, 4
     got = exchange(run, distance)
     while distance * 2 < count:
@@ -313,7 +315,6 @@
         run = joined(functools.partial(run_kernel, distance), run, got)
         distance *= 2
         got = exchange(run, distance)
-    hold, got = lax.optimization_barrier((hold, got))
     operands = [got] + parts
     if ahead is None:
         kernel = functools.partial(end_kernel, distance, None)
@@ -321,7 +322,8 @@
         kernel, operands = functools.partial(end_kernel, distance), [ahead] + operands
     shape = (keep.shape[0] - 16, LANES)
     outs = scan_call(kernel, operands, [shape] * 4, "join_end")
-    return hold, [outs[0]] + [exchange(out, k) for k, out in zip((1, 2, 3), outs[1:])]
+    back = {k: exchange(outs[k], k) for k in (3, 2, 1)}
+    return hold, [outs[0]] + [back[k] for k in (1, 2, 3)]
 
 
 def rows_of(ref, block):

time: 55.4 us -> 58.8 us (1.061)
  local copies, waits for them, and re-layouts: 0.81 us -> 3.47 us
    unnamed x20 -> x24, local copies, waits for them, and re-layouts: 0.81 us -> 3.47 us
  transfers between devices with their start and end apart: 13 -> 13, of which waited for: 9 -> 8; matrix products, arithmetic and copies ran while one was open for 0% -> 0% of each run, Pallas kernels for 23% -> 22%
where the time goes in v5:
time: 58.8 us; the launch traced here: 58.6 us
  waiting for transfers between devices  20.6 us (35%)
  Pallas kernels  18.5 us (31%)
  starting transfers between devices  15.7 us (27%)
  local copies, waits for them, and re-layouts  3.47 us (6%)
    ppermute x7, starting transfers between devices, exchange(): return lax.ppermute(value, 'seq', [(s, s ^ distance) for s in range(count)])  11.2 us
    ppermute x7, waiting for transfers between devices, exchange(): return lax.ppermute(value, 'seq', [(s, s ^ distance) for s in range(count)])  7.35 us
    pallas_call x2, Pallas kernels, within(): pl.pallas_call(functools.partial(within_kernel, far), in_specs=[VMEM] * 6...  6.36 us
    pallas_call x7, Pallas kernels, local_call(): pl.pallas_call(kernel, in_specs=[VMEM] * len(operands), out_specs=[VMEM]...  6.09 us
    ppermute x1, waiting for transfers between devices, per_device(): third, filled = await_piece(lax.ppermute(third, 'head', far), filled)  5.28 us
    ppermute x1, waiting for transfers between devices, per_device(): second, first = await_piece(lax.ppermute(second, 'head', far), first)  4.79 us
    unnamed x24, local copies, waits for them, and re-layouts  3.47 us
    pallas_call x1, Pallas kernels, give_states(): pl.pallas_call(give_kernel, in_specs=[HBM] * 4, out_shape=[jax.ShapeDtype...  3.33 us
  transfers between devices with their start and end apart: 13, of which 8 were waited for; matrix products, arithmetic and copies ran while one was open for 0% of the time, Pallas kernels for 22%

profile of v5, /device:TPU:0, one launch (start us, length us, event | category | flops | bytes accessed | tf_op | source)
XLA Modules:
  0.0 58.6 jit_solution(4139767007551992948)
XLA Ops:
  0.0 3.3 %give_states.1 = (bf16[272,128]{1,0:T(8,128)(2,1)}, bf16[272,128]{1,0:T(8,128)(2,1)}, bf16[272,128]{1,0:T(8,128)(2,1)}, bf16[32,640]{1,0:T(8,128)(2,1)}, f32[4,48,128]{2,1,0:T(8,128)}) custom-call(f32[16,512]{1,0:T(8,128)} %bitcast.20, f32[1,16]{1,0:T(1,128)} %bitcast.21, f32[512,1024]{1,0:T(8,128)} %x_ref.3, f32[512,128]{1,0:T(8,128)} %bitcast.8), custom_call_target="tpu_custom_call" | custom-call | flops 200000000 | bytes 1500000 | tf_op jit(solution)/shard_map/give_states/pallas_call | solution.py:155
  3.3 3.0 %collective-permute-start = (bf16[272,128]{1,0:T(8,128)(2,1)}, bf16[272,128]{1,0:T(8,128)(2,1)S(1)}, u32[]{:S(2)}, u32[]{:S(2)}) collective-permute-start(bf16[272,128]{1,0:T(8,128)(2,1)} %get-tuple-element.44), channel_id=1, source_target_pairs={{0,4},{4,0},{8,12},{12,8},{16,20},{20,16},{24,28},{28,24},{1,5},{5... | collective-permute-start | bytes 208904 | tf_op jit(solution)/shard_map/ppermute | solution.py:300
  6.4 1.6 %collective-permute-start.1 = (bf16[272,128]{1,0:T(8,128)(2,1)}, bf16[272,128]{1,0:T(8,128)(2,1)S(1)}, u32[]{:S(2)}, u32[]{:S(2)}) collective-permute-start(bf16[272,128]{1,0:T(8,128)(2,1)} %get-tuple-element.45), channel_id=1, source_target_pairs={{0,8},{4,12},{8,0},{12,4},{16,24},{20,28},{24,16},{28,20},{1,9},{5... | collective-permute-start | bytes 208904 | tf_op jit(solution)/shard_map/ppermute | solution.py:300
  8.0 1.1 %copy-done.2 = f32[512,1,128]{2,1,0:T(1,128)S(1)} copy-done((f32[512,1,128]{2,1,0:T(1,128)S(1)}, f32[512,1,128]{2,1,0:T(1,128)}, u32[]{:S(2)}) %copy-start.2) | copy-done | bytes 262168
  9.1 1.4 %copy-done.6 = bf16[512,1024]{1,0:T(8,128)(2,1)S(1)} copy-done((bf16[512,1024]{1,0:T(8,128)(2,1)S(1)}, bf16[512,1024]{1,0:T(8,128)(2,1)}, u32[]{:S(2)}) %copy-start.6) | copy-done | bytes 1048600
  11.4 3.2 %within_far.1 = (f32[256,1024]{1,0:T(8,128)S(1)}, f32[256,1024]{1,0:T(8,128)S(1)}) custom-call(f32[4,48,128]{2,1,0:T(8,128)S(1)} %copy-done.7, f32[512,1024]{1,0:T(8,128)S(1)} %copy-done, f32[512,128]{1,0:T(8,128)S(1)} %bitcast.9, f32[512,128]{1,0:T(8,128)S(1)} %bitcast.12, bf16[512,1024]{1,0:T(8,128)(2,1)S(1)} %copy-done.6, f32[1,16]{1,0:T(1,128)S(1)} %bitcast.18), custom_call_target="tpu_custom_call" | custom-call | flops 4000000000 | bytes 3000000 | tf_op jit(solution)/shard_map/within_far/pallas_call | solution.py:420
  15.4 3.1 %collective-permute-start.3 = (bf16[272,128]{1,0:T(8,128)(2,1)S(1)}, bf16[272,128]{1,0:T(8,128)(2,1)S(1)}, u32[]{:S(2)}, u32[]{:S(2)}) collective-permute-start(bf16[272,128]{1,0:T(8,128)(2,1)S(1)} %join_states.1), channel_id=1, source_target_pairs={{0,16},{4,20},{8,24},{12,28},{16,0},{20,4},{24,8},{28,12},{1,17},{... | collective-permute-start | bytes 208904 | tf_op jit(solution)/shard_map/ppermute | solution.py:300
  18.4 2.4 %collective-permute-done.3.last = bf16[272,128]{1,0:T(8,128)(2,1)S(1)} collective-permute-done((bf16[272,128]{1,0:T(8,128)(2,1)S(1)}, bf16[272,128]{1,0:T(8,128)(2,1)S(1)}, u32[]{:S(2)}, u32[]{:S(2)}) %collective-permute-start.3) | collective-permute-done | bytes 69664 | tf_op jit(solution)/shard_map/ppermute | solution.py:300
  21.1 1.8 %collective-permute-start.4 = (bf16[256,128]{1,0:T(8,128)(2,1)S(1)}, bf16[256,128]{1,0:T(8,128)(2,1)S(1)}, u32[]{:S(2)}, u32[]{:S(2)}) collective-permute-start(bf16[256,128]{1,0:T(8,128)(2,1)S(1)} %get-tuple-element.54), channel_id=1, source_target_pairs={{0,4},{4,0},{8,12},{12,8},{16,20},{20,16},{24,28},{28,24},{1,5},{5... | collective-permute-start | bytes 196616 | tf_op jit(solution)/shard_map/ppermute | solution.py:300
  22.9 1.6 %collective-permute-start.5 = (bf16[256,128]{1,0:T(8,128)(2,1)S(1)}, bf16[256,128]{1,0:T(8,128)(2,1)S(1)}, u32[]{:S(2)}, u32[]{:S(2)}) collective-permute-start(bf16[256,128]{1,0:T(8,128)(2,1)S(1)} %get-tuple-element.55), channel_id=1, source_target_pairs={{0,8},{4,12},{8,0},{12,4},{16,24},{20,28},{24,16},{28,20},{1,9},{5... | collective-permute-start | bytes 196616 | tf_op jit(solution)/shard_map/ppermute | solution.py:300
  25.4 1.7 %collective-permute-done.5.q2 = bf16[256,128]{1,0:T(8,128)(2,1)S(1)} collective-permute-done((bf16[256,128]{1,0:T(8,128)(2,1)S(1)}, bf16[256,128]{1,0:T(8,128)(2,1)S(1)}, u32[]{:S(2)}, u32[]{:S(2)}) %collective-permute-start.5) | collective-permute-done | bytes 65568 | tf_op jit(solution)/shard_map/ppermute | solution.py:300
  27.1 2.5 %collective-permute-done.6.q3 = bf16[256,128]{1,0:T(8,128)(2,1)S(1)} collective-permute-done((bf16[256,128]{1,0:T(8,128)(2,1)S(1)}, bf16[256,128]{1,0:T(8,128)(2,1)S(1)}, u32[]{:S(2)}, u32[]{:S(2)}) %collective-permute-start.6) | collective-permute-done | bytes 65568 | tf_op jit(solution)/shard_map/ppermute | solution.py:300
  29.6 1.1 %finish_far.1 = (bf16[128,1024]{1,0:T(8,128)(2,1)S(1)}, f32[128,1024]{1,0:T(8,128)S(1)}, bf16[256,1024]{1,0:T(8,128)(2,1)S(1)}) custom-call(f32[256,1024]{1,0:T(8,128)S(1)} %get-tuple-element.47.own, f32[256,1024]{1,0:T(8,128)S(1)} %get-tuple-element.48.lead, f32[512,128]{1,0:T(8,128)S(1)} %bitcast.13, bf16[256,128]{1,0:T(8,128)(2,1)S(1)} %get-tuple-element.53.q0, ...), custom_call_target="tpu_custom_call" | custom-call | flops 536870912 | tf_op jit(solution)/shard_map/finish_far/pallas_call | solution.py:505
  30.8 1.0 %project_more.1 = (bf16[128,1536]{1,0:T(8,128)(2,1)S(1)}, f32[128,1536]{1,0:T(8,128)S(1)}) custom-call(bf16[256,1024]{1,0:T(8,128)(2,1)S(1)} %get-tuple-element.60.normed, bf16[1024,4096]{1,0:T(8,128)(2,1)S(1)} %bitcast.7), custom_call_target="tpu_custom_call" | custom-call | flops 805306368 | tf_op jit(solution)/shard_map/project_more/pallas_call | solution.py:505
  32.4 1.6 %collective-permute-start.12 = (bf16[128,1024]{1,0:T(8,128)(2,1)S(1)}, bf16[128,1024]{1,0:T(8,128)(2,1)S(1)}, u32[]{:S(2)}, u32[]{:S(2)}) collective-permute-start(bf16[128,1024]{1,0:T(8,128)(2,1)S(1)} %add_pair.4), channel_id=1, source_target_pairs={{0,2},{1,3},{2,0},{3,1},{4,6},{5,7},{6,4},{7,5},{8,10},{9,11},{10,... | collective-permute-start | bytes 786440 | tf_op jit(solution)/shard_map/ppermute | solution.py:666
  34.0 3.2 %within_near.1 = (f32[256,1024]{1,0:T(8,128)S(1)}, f32[256,1024]{1,0:T(8,128)S(1)}) custom-call(f32[4,48,128]{2,1,0:T(8,128)S(1)} %copy-done.8, f32[512,1024]{1,0:T(8,128)S(1)} %copy-done, f32[512,128]{1,0:T(8,128)S(1)} %bitcast.11, f32[512,128]{1,0:T(8,128)S(1)} %bitcast.14, bf16[512,1024]{1,0:T(8,128)(2,1)S(1)} %copy-done.6, f32[1,16]{1,0:T(1,128)S(1)} %bitcast.19), custom_call_target="tpu_custom_call" | custom-call | flops 4000000000 | bytes 3000000 | tf_op jit(solution)/shard_map/within_near/pallas_call | solution.py:420
  37.8 2.5 %finish_near.1 = (bf16[128,5632]{1,0:T(8,128)(2,1)S(1)}, f32[128,1536]{1,0:T(8,128)S(1)}, bf16[128,1024]{1,0:T(8,128)(2,1)S(1)}) custom-call(bf16[256,1024]{1,0:T(8,128)(2,1)S(1)} %get-tuple-element.60.normed, f32[256,1024]{1,0:T(8,128)S(1)} %get-tuple-element.64.own, f32[256,1024]{1,0:T(8,128)S(1)} %get-tuple-element.65.lead, f32[512,128]{1,0:T(8,128)S(1)} %bitcast.15, ...), custom_call_target="tpu_custom_call" | custom-call | flops 1879048192 | tf_op jit(solution)/shard_map/finish_near/pallas_call | solution.py:505
  40.4 1.2 %collective-permute-done.12.refs_0_ = bf16[128,1024]{1,0:T(8,128)(2,1)S(1)} collective-permute-done((bf16[128,1024]{1,0:T(8,128)(2,1)S(1)}, bf16[128,1024]{1,0:T(8,128)(2,1)S(1)}, u32[]{:S(2)}, u32[]{:S(2)}) %collective-permute-start.12) | collective-permute-done | bytes 262176 | tf_op jit(solution)/shard_map/ppermute | solution.py:666
  41.6 2.0 %collective-permute-done.9.come = bf16[128,5632]{1,0:T(8,128)(2,1)S(1)} collective-permute-done((bf16[128,5632]{1,0:T(8,128)(2,1)S(1)}, bf16[128,5632]{1,0:T(8,128)(2,1)S(1)}, u32[]{:S(2)}, u32[]{:S(2)}) %collective-permute-start.9) | collective-permute-done | bytes 1441824 | tf_op jit(solution)/shard_map/ppermute | solution.py:627
  43.7 1.6 %collective-permute-start.10 = (bf16[128,1536]{1,0:T(8,128)(2,1)S(1)}, bf16[128,1536]{1,0:T(8,128)(2,1)S(1)}, u32[]{:S(2)}, u32[]{:S(2)}) collective-permute-start(bf16[128,1536]{1,0:T(8,128)(2,1)S(1)} %add_pair.5), channel_id=1, source_target_pairs={{0,2},{1,3},{2,0},{3,1},{4,6},{5,7},{6,4},{7,5},{8,10},{9,11},{10,... | collective-permute-start | bytes 1179656 | tf_op jit(solution)/shard_map/ppermute | solution.py:669
  45.3 4.8 %collective-permute-done.11.refs_0_ = bf16[128,1536]{1,0:T(8,128)(2,1)S(1)} collective-permute-done((bf16[128,1536]{1,0:T(8,128)(2,1)S(1)}, bf16[128,1536]{1,0:T(8,128)(2,1)S(1)}, u32[]{:S(2)}, u32[]{:S(2)}) %collective-permute-start.11) | collective-permute-done | bytes 393248 | tf_op jit(solution)/shard_map/ppermute | solution.py:667
  50.1 1.3 %project_kept.1.kept = f32[128,4096]{1,0:T(8,128)S(1)} custom-call(bf16[128,1024]{1,0:T(8,128)(2,1)S(1)} %get-tuple-element.66.kept, bf16[128,5632]{1,0:T(8,128)(2,1)S(1)} %collective-permute-done.9.come, bf16[1024,4096]{1,0:T(8,128)(2,1)S(1)} %bitcast.7), custom_call_target="tpu_custom_call" | custom-call | flops 1073741824 | tf_op jit(solution)/shard_map/project_kept/pallas_call | solution.py:505
  51.4 1.0 %early_sums.1.refs_1_ = bf16[128,4096]{1,0:T(8,128)(2,1)} custom-call(f32[128,4096]{1,0:T(8,128)S(1)} %project_kept.1.kept, bf16[128,1024]{1,0:T(8,128)(2,1)S(1)} %get-tuple-element.71.first, bf16[128,1536]{1,0:T(8,128)(2,1)S(1)} %get-tuple-element.72.second), custom_call_target="tpu_custom_call" | custom-call | tf_op jit(solution)/shard_map/early_sums/pallas_call | solution.py:548
  52.4 5.3 %collective-permute-done.10.refs_0_ = bf16[128,1536]{1,0:T(8,128)(2,1)S(1)} collective-permute-done((bf16[128,1536]{1,0:T(8,128)(2,1)S(1)}, bf16[128,1536]{1,0:T(8,128)(2,1)S(1)}, u32[]{:S(2)}, u32[]{:S(2)}) %collective-permute-start.10) | collective-permute-done | bytes 393248 | tf_op jit(solution)/shard_map/ppermute | solution.py:669
  (45 shorter events, 5.2 us)
Async XLA Ops:
  0.0 7.9 %copy-start = (f32[512,1024]{1,0:T(8,128)S(1)}, f32[512,1024]{1,0:T(8,128)}, u32[]{:S(2)}) copy-start(f32[512,1024]{1,0:T(8,128)} %x_ref.3) | copy-start | bytes 6291460
  0.0 7.9 %copy-start.1 = (f32[512,1,128]{2,1,0:T(1,128)S(1)}, f32[512,1,128]{2,1,0:T(1,128)}, u32[]{:S(2)}) copy-start(f32[512,1,128]{2,1,0:T(1,128)} %param.13) | copy-start | bytes 786436
  0.0 7.9 %copy-start.9 = (f32[16]{0:T(128)S(1)}, f32[16]{0:T(128)}, u32[]{:S(2)}) copy-start(f32[16]{0:T(128)} %param.15) | copy-start | bytes 196
  3.3 11.9 %collective-permute-start = (bf16[272,128]{1,0:T(8,128)(2,1)}, bf16[272,128]{1,0:T(8,128)(2,1)S(1)}, u32[]{:S(2)}, u32[]{:S(2)}) collective-permute-start(bf16[272,128]{1,0:T(8,128)(2,1)} %get-tuple-element.44), channel_id=1, source_target_pairs={{0,4},{4,0},{8,12},{12,8},{16,20},{20,16},{24,28},{28,24},{1,5},{5... | collective-permute-start | bytes 208904 | tf_op jit(solution)/shard_map/ppermute | solution.py:300
  6.4 8.9 %collective-permute-start.1 = (bf16[272,128]{1,0:T(8,128)(2,1)}, bf16[272,128]{1,0:T(8,128)(2,1)S(1)}, u32[]{:S(2)}, u32[]{:S(2)}) collective-permute-start(bf16[272,128]{1,0:T(8,128)(2,1)} %get-tuple-element.45), channel_id=1, source_target_pairs={{0,8},{4,12},{8,0},{12,4},{16,24},{20,28},{24,16},{28,20},{1,9},{5... | collective-permute-start | bytes 208904 | tf_op jit(solution)/shard_map/ppermute | solution.py:300
  7.9 7.3 %collective-permute-start.2 = (bf16[272,128]{1,0:T(8,128)(2,1)}, bf16[272,128]{1,0:T(8,128)(2,1)S(1)}, u32[]{:S(2)}, u32[]{:S(2)}) collective-permute-start(bf16[272,128]{1,0:T(8,128)(2,1)} %get-tuple-element.46), channel_id=1, source_target_pairs={{0,12},{4,8},{8,4},{12,0},{16,28},{20,24},{24,20},{28,16},{1,13},{... | collective-permute-start | bytes 208904 | tf_op jit(solution)/shard_map/ppermute | solution.py:300
  7.9 21.7 %slice-start = ((s8[8388608]{0:T(1024)(128)(4,1)}), s8[4194304]{0:T(1024)(128)(4,1)S(1)}, s32[]{:S(2)}) async-start(s8[8388608]{0:T(1024)(128)(4,1)} %bitcast.6), calls=%async_computation | async-start | bytes 8388608
  8.0 1.1 %copy-start.2 = (f32[512,1,128]{2,1,0:T(1,128)S(1)}, f32[512,1,128]{2,1,0:T(1,128)}, u32[]{:S(2)}) copy-start(f32[512,1,128]{2,1,0:T(1,128)} %param.14) | copy-start | bytes 786436
  9.1 1.4 %copy-start.6 = (bf16[512,1024]{1,0:T(8,128)(2,1)S(1)}, bf16[512,1024]{1,0:T(8,128)(2,1)}, u32[]{:S(2)}) copy-start(bf16[512,1024]{1,0:T(8,128)(2,1)} %gate_ref.3) | copy-start | bytes 3145732
  11.4 3.2 %copy-start.4 = (bf16[32,640]{1,0:T(8,128)(2,1)S(1)}, bf16[32,640]{1,0:T(8,128)(2,1)}, u32[]{:S(2)}) copy-start(bf16[32,640]{1,0:T(8,128)(2,1)} %get-tuple-element.43.wk) | copy-start | bytes 122884
  11.4 18.2 %slice-start.1 = ((s8[8388608]{0:T(1024)(128)(4,1)}), s8[4194304]{0:T(1024)(128)(4,1)S(1)}, s32[]{:S(2)}) async-start(s8[8388608]{0:T(1024)(128)(4,1)} %bitcast.6), calls=%async_computation.1 | async-start | bytes 8388608
  14.6 15.0 %copy-start.3 = (f32[512,1,128]{2,1,0:T(1,128)S(1)}, f32[512,1,128]{2,1,0:T(1,128)}, u32[]{:S(2)}) copy-start(f32[512,1,128]{2,1,0:T(1,128)} %param.14) | copy-start | bytes 786436
  14.6 15.0 %copy-start.5 = (f32[1024]{0:T(1024)S(1)}, f32[1024]{0:T(1024)}, u32[]{:S(2)}) copy-start(f32[1024]{0:T(1024)} %param.16) | copy-start | bytes 12292
  15.4 5.5 %collective-permute-start.3 = (bf16[272,128]{1,0:T(8,128)(2,1)S(1)}, bf16[272,128]{1,0:T(8,128)(2,1)S(1)}, u32[]{:S(2)}, u32[]{:S(2)}) collective-permute-start(bf16[272,128]{1,0:T(8,128)(2,1)S(1)} %join_states.1), channel_id=1, source_target_pairs={{0,16},{4,20},{8,24},{12,28},{16,0},{20,4},{24,8},{28,12},{1,17},{... | collective-permute-start | bytes 208904 | tf_op jit(solution)/shard_map/ppermute | solution.py:300
  21.1 4.3 %collective-permute-start.4 = (bf16[256,128]{1,0:T(8,128)(2,1)S(1)}, bf16[256,128]{1,0:T(8,128)(2,1)S(1)}, u32[]{:S(2)}, u32[]{:S(2)}) collective-permute-start(bf16[256,128]{1,0:T(8,128)(2,1)S(1)} %get-tuple-element.54), channel_id=1, source_target_pairs={{0,4},{4,0},{8,12},{12,8},{16,20},{20,16},{24,28},{28,24},{1,5},{5... | collective-permute-start | bytes 196616 | tf_op jit(solution)/shard_map/ppermute | solution.py:300
  22.9 4.3 %collective-permute-start.5 = (bf16[256,128]{1,0:T(8,128)(2,1)S(1)}, bf16[256,128]{1,0:T(8,128)(2,1)S(1)}, u32[]{:S(2)}, u32[]{:S(2)}) collective-permute-start(bf16[256,128]{1,0:T(8,128)(2,1)S(1)} %get-tuple-element.55), channel_id=1, source_target_pairs={{0,8},{4,12},{8,0},{12,4},{16,24},{20,28},{24,16},{28,20},{1,9},{5... | collective-permute-start | bytes 196616 | tf_op jit(solution)/shard_map/ppermute | solution.py:300
  24.4 5.2 %collective-permute-start.6 = (bf16[256,128]{1,0:T(8,128)(2,1)S(1)}, bf16[256,128]{1,0:T(8,128)(2,1)S(1)}, u32[]{:S(2)}, u32[]{:S(2)}) collective-permute-start(bf16[256,128]{1,0:T(8,128)(2,1)S(1)} %get-tuple-element.56), channel_id=1, source_target_pairs={{0,12},{4,8},{8,4},{12,0},{16,28},{20,24},{24,20},{28,16},{1,13},{... | collective-permute-start | bytes 196616 | tf_op jit(solution)/shard_map/ppermute | solution.py:300
  30.7 1.6 %collective-permute-start.8 = (bf16[128,1024]{1,0:T(8,128)(2,1)S(1)}, bf16[128,1024]{1,0:T(8,128)(2,1)S(1)}, u32[]{:S(2)}, u32[]{:S(2)}) collective-permute-start(bf16[128,1024]{1,0:T(8,128)(2,1)S(1)} %get-tuple-element.62), channel_id=1, source_target_pairs={{0,1},{1,0},{2,3},{3,2},{4,5},{5,4},{6,7},{7,6},{8,9},{9,8},{10,11... | collective-permute-start | bytes 786440 | tf_op jit(solution)/shard_map/ppermute | solution.py:627
  30.8 3.2 %copy-start.8 = (f32[4,48,128]{2,1,0:T(8,128)S(1)}, f32[4,48,128]{2,1,0:T(8,128)}, u32[]{:S(2)}) copy-start(f32[4,48,128]{2,1,0:T(8,128)} %get-tuple-element.63.aux) | copy-start | bytes 294916
  31.8 5.4 %collective-permute-start.7 = (bf16[128,1536]{1,0:T(8,128)(2,1)S(1)}, bf16[128,1536]{1,0:T(8,128)(2,1)S(1)}, u32[]{:S(2)}, u32[]{:S(2)}) collective-permute-start(bf16[128,1536]{1,0:T(8,128)(2,1)S(1)} %get-tuple-element.59), channel_id=1, source_target_pairs={{0,1},{1,0},{2,3},{3,2},{4,5},{5,4},{6,7},{7,6},{8,9},{9,8},{10,11... | collective-permute-start | bytes 1179656 | tf_op jit(solution)/shard_map/ppermute | solution.py:627
  32.4 9.2 %collective-permute-start.12 = (bf16[128,1024]{1,0:T(8,128)(2,1)S(1)}, bf16[128,1024]{1,0:T(8,128)(2,1)S(1)}, u32[]{:S(2)}, u32[]{:S(2)}) collective-permute-start(bf16[128,1024]{1,0:T(8,128)(2,1)S(1)} %add_pair.4), channel_id=1, source_target_pairs={{0,2},{1,3},{2,0},{3,1},{4,6},{5,7},{6,4},{7,5},{8,10},{9,11},{10,... | collective-permute-start | bytes 786440 | tf_op jit(solution)/shard_map/ppermute | solution.py:666
  37.3 12.8 %collective-permute-start.11 = (bf16[128,1536]{1,0:T(8,128)(2,1)S(1)}, bf16[128,1536]{1,0:T(8,128)(2,1)S(1)}, u32[]{:S(2)}, u32[]{:S(2)}) collective-permute-start(bf16[128,1536]{1,0:T(8,128)(2,1)S(1)} %add_pair.3), channel_id=1, source_target_pairs={{0,2},{1,3},{2,0},{3,1},{4,6},{5,7},{6,4},{7,5},{8,10},{9,11},{10,... | collective-permute-start | bytes 1179656 | tf_op jit(solution)/shard_map/ppermute | solution.py:667
  40.3 3.3 %collective-permute-start.9 = (bf16[128,5632]{1,0:T(8,128)(2,1)S(1)}, bf16[128,5632]{1,0:T(8,128)(2,1)S(1)}, u32[]{:S(2)}, u32[]{:S(2)}) collective-permute-start(bf16[128,5632]{1,0:T(8,128)(2,1)S(1)} %get-tuple-element.67), channel_id=1, source_target_pairs={{0,1},{1,0},{2,3},{3,2},{4,5},{5,4},{6,7},{7,6},{8,9},{9,8},{10,11... | collective-permute-start | bytes 4325384 | tf_op jit(solution)/shard_map/ppermute | solution.py:627
  43.7 14.0 %collective-permute-start.10 = (bf16[128,1536]{1,0:T(8,128)(2,1)S(1)}, bf16[128,1536]{1,0:T(8,128)(2,1)S(1)}, u32[]{:S(2)}, u32[]{:S(2)}) collective-permute-start(bf16[128,1536]{1,0:T(8,128)(2,1)S(1)} %add_pair.5), channel_id=1, source_target_pairs={{0,2},{1,3},{2,0},{3,1},{4,6},{5,7},{6,4},{7,5},{8,10},{9,11},{10,... | collective-permute-start | bytes 1179656 | tf_op jit(solution)/shard_map/ppermute | solution.py:669
  (1 other events, 0.9 us)

commit v6 on v5

--- a/solution.py
+++ b/solution.py
@@ -14,7 +14,7 @@
 BF = jnp.bfloat16
 F32 = jnp.float32
 VMEM_LIMIT = 16 * 1024 * 1024
-WHOLE_VMEM = 61 * 1024 * 1024 + 512 * 1024
+WHOLE_VMEM = 58 * 1024 * 1024
 PIECES = ((0, 1024), (1024, 1536), (2560, 1536))
 
 
@@ -168,7 +168,7 @@
             pltpu.SemaphoreType.DMA((6,)),
         ],
         compiler_params=pltpu.CompilerParams(vmem_limit_bytes=WHOLE_VMEM),
-        cost_estimate=pl.CostEstimate(flops=200_000_000, bytes_accessed=1_500_000, transcendentals=0),
+        cost_estimate=pl.CostEstimate(flops=4_000_000_000, bytes_accessed=1_500_000, transcendentals=0),
         name="give_states",
     )(raw, rate, x, b)
 
@@ -186,7 +186,7 @@
             pltpu.SemaphoreType.DMA((2,)),
         ],
         compiler_params=pltpu.CompilerParams(vmem_limit_bytes=VMEM_LIMIT),
-        cost_estimate=pl.CostEstimate(flops=200_000_000, bytes_accessed=1_500_000, transcendentals=0),
+        cost_estimate=pl.CostEstimate(flops=800_000_000, bytes_accessed=1_500_000, transcendentals=0),
         name="keep_states",
     )(wk, x, b)
 
@@ -302,7 +302,7 @@
     def joined(kernel, *operands):
         return scan_call(kernel, operands, [keep.shape], "join_states")[0]
 
-    come = {k: exchange(gives[k - 1], k) for k in (3, 2, 1)}
+    come = {k: exchange(gives[k - 1], k) for k in (1, 2, 3)}
     parts = [keep] + [come[k] for k in (1, 2, 3)]
     hold, parts = lax.optimization_barrier((hold, parts))
     run, ahead, distance = joined(join_four_kernel, *parts), None, 4
@@ -322,7 +322,7 @@
         kernel, operands = functools.partial(end_kernel, distance), [ahead] + operands
     shape = (keep.shape[0] - 16, LANES)
     outs = scan_call(kernel, operands, [shape] * 4, "join_end")
-    back = {k: exchange(outs[k], k) for k in (3, 2, 1)}
+    back = {k: exchange(outs[k], k) for k in (1, 2, 3)}
     return hold, [outs[0]] + [back[k] for k in (1, 2, 3)]
 
 

time: 58.8 us -> 56.4 us (0.959)
  local copies, waits for them, and re-layouts: 3.47 us -> 1.08 us
    unnamed x24 -> x22, local copies, waits for them, and re-layouts: 3.47 us -> 1.08 us
  transfers between devices with their start and end apart: 13 -> 13, of which waited for: 8 -> 9; matrix products, arithmetic and copies ran while one was open for 0% -> 0% of each run, Pallas kernels for 22% -> 23%
where the time goes in v6:
time: 56.4 us; the launch traced here: 56.2 us
  waiting for transfers between devices  21.1 us (37%)
  Pallas kernels  18.5 us (33%)
  starting transfers between devices  15.2 us (27%)
  local copies, waits for them, and re-layouts  1.08 us (2%)
    ppermute x7, starting transfers between devices, exchange(): return lax.ppermute(value, 'seq', [(s, s ^ distance) for s in range(count)])  10.8 us
    ppermute x7, waiting for transfers between devices, exchange(): return lax.ppermute(value, 'seq', [(s, s ^ distance) for s in range(count)])  7.79 us
    pallas_call x2, Pallas kernels, within(): pl.pallas_call(functools.partial(within_kernel, far), in_specs=[VMEM] * 6...  6.36 us
    pallas_call x7, Pallas kernels, local_call(): pl.pallas_call(kernel, in_specs=[VMEM] * len(operands), out_specs=[VMEM]...  6.04 us
    ppermute x1, waiting for transfers between devices, per_device(): third, filled = await_piece(lax.ppermute(third, 'head', far), filled)  5.32 us
    ppermute x1, waiting for transfers between devices, per_device(): second, first = await_piece(lax.ppermute(second, 'head', far), first)  4.77 us
    pallas_call x1, Pallas kernels, give_states(): pl.pallas_call(give_kernel, in_specs=[HBM] * 4, out_shape=[jax.ShapeDtype...  3.34 us
    ppermute x3, waiting for transfers between devices, add(): come = lax.ppermute(theirs, 'head', near)  2 us
  transfers between devices with their start and end apart: 13, of which 9 were waited for; matrix products, arithmetic and copies ran while one was open for 0% of the time, Pallas kernels for 23%

profile of v6, /device:TPU:0, one launch (start us, length us, event | category | flops | bytes accessed | tf_op | source)
XLA Modules:
  0.0 56.2 jit_solution(11645536108656218005)
XLA Ops:
  0.0 3.3 %give_states.1 = (bf16[272,128]{1,0:T(8,128)(2,1)}, bf16[272,128]{1,0:T(8,128)(2,1)}, bf16[272,128]{1,0:T(8,128)(2,1)}, bf16[32,640]{1,0:T(8,128)(2,1)}, f32[4,48,128]{2,1,0:T(8,128)}) custom-call(f32[16,512]{1,0:T(8,128)} %bitcast.20, f32[1,16]{1,0:T(1,128)} %bitcast.21, f32[512,1024]{1,0:T(8,128)} %x_ref.3, f32[512,128]{1,0:T(8,128)} %bitcast.14), custom_call_target="tpu_custom_call" | custom-call | flops 4000000000 | bytes 1500000 | tf_op jit(solution)/shard_map/give_states/pallas_call | solution.py:155
  3.4 3.0 %collective-permute-start = (bf16[272,128]{1,0:T(8,128)(2,1)}, bf16[272,128]{1,0:T(8,128)(2,1)S(1)}, u32[]{:S(2)}, u32[]{:S(2)}) collective-permute-start(bf16[272,128]{1,0:T(8,128)(2,1)} %get-tuple-element.44), channel_id=1, source_target_pairs={{0,4},{4,0},{8,12},{12,8},{16,20},{20,16},{24,28},{28,24},{1,5},{5... | collective-permute-start | bytes 208904 | tf_op jit(solution)/shard_map/ppermute | solution.py:300
  6.4 1.6 %collective-permute-start.1 = (bf16[272,128]{1,0:T(8,128)(2,1)}, bf16[272,128]{1,0:T(8,128)(2,1)S(1)}, u32[]{:S(2)}, u32[]{:S(2)}) collective-permute-start(bf16[272,128]{1,0:T(8,128)(2,1)} %get-tuple-element.45), channel_id=1, source_target_pairs={{0,8},{4,12},{8,0},{12,4},{16,24},{20,28},{24,16},{28,20},{1,9},{5... | collective-permute-start | bytes 208904 | tf_op jit(solution)/shard_map/ppermute | solution.py:300
  8.0 1.0 %copy-done.7 = f32[4,48,128]{2,1,0:T(8,128)S(1)} copy-done((f32[4,48,128]{2,1,0:T(8,128)S(1)}, f32[4,48,128]{2,1,0:T(8,128)}, u32[]{:S(2)}) %copy-start.7) | copy-done | bytes 98328
  9.1 3.2 %within_far.1 = (f32[256,1024]{1,0:T(8,128)S(1)}, f32[256,1024]{1,0:T(8,128)S(1)}) custom-call(f32[4,48,128]{2,1,0:T(8,128)S(1)} %copy-done.7, f32[512,1024]{1,0:T(8,128)S(1)} %copy-done.2, f32[512,128]{1,0:T(8,128)S(1)} %bitcast.15, f32[512,128]{1,0:T(8,128)S(1)} %bitcast.8, bf16[512,1024]{1,0:T(8,128)(2,1)S(1)} %copy-done.3, f32[1,16]{1,0:T(1,128)S(1)} %bitcast.18), custom_call_target="tpu_custom_call" | custom-call | flops 4000000000 | bytes 3000000 | tf_op jit(solution)/shard_map/within_far/pallas_call | solution.py:420
  13.5 2.7 %collective-permute-start.3 = (bf16[272,128]{1,0:T(8,128)(2,1)S(1)}, bf16[272,128]{1,0:T(8,128)(2,1)S(1)}, u32[]{:S(2)}, u32[]{:S(2)}) collective-permute-start(bf16[272,128]{1,0:T(8,128)(2,1)S(1)} %join_states.1), channel_id=1, source_target_pairs={{0,16},{4,20},{8,24},{12,28},{16,0},{20,4},{24,8},{28,12},{1,17},{... | collective-permute-start | bytes 208904 | tf_op jit(solution)/shard_map/ppermute | solution.py:300
  16.1 2.6 %collective-permute-done.3.last = bf16[272,128]{1,0:T(8,128)(2,1)S(1)} collective-permute-done((bf16[272,128]{1,0:T(8,128)(2,1)S(1)}, bf16[272,128]{1,0:T(8,128)(2,1)S(1)}, u32[]{:S(2)}, u32[]{:S(2)}) %collective-permute-start.3) | collective-permute-done | bytes 69664 | tf_op jit(solution)/shard_map/ppermute | solution.py:300
  19.0 1.5 %collective-permute-start.4 = (bf16[256,128]{1,0:T(8,128)(2,1)S(1)}, bf16[256,128]{1,0:T(8,128)(2,1)S(1)}, u32[]{:S(2)}, u32[]{:S(2)}) collective-permute-start(bf16[256,128]{1,0:T(8,128)(2,1)S(1)} %get-tuple-element.54), channel_id=1, source_target_pairs={{0,4},{4,0},{8,12},{12,8},{16,20},{20,16},{24,28},{28,24},{1,5},{5... | collective-permute-start | bytes 196616 | tf_op jit(solution)/shard_map/ppermute | solution.py:300
  20.5 1.6 %collective-permute-start.5 = (bf16[256,128]{1,0:T(8,128)(2,1)S(1)}, bf16[256,128]{1,0:T(8,128)(2,1)S(1)}, u32[]{:S(2)}, u32[]{:S(2)}) collective-permute-start(bf16[256,128]{1,0:T(8,128)(2,1)S(1)} %get-tuple-element.55), channel_id=1, source_target_pairs={{0,8},{4,12},{8,0},{12,4},{16,24},{20,28},{24,16},{28,20},{1,9},{5... | collective-permute-start | bytes 196616 | tf_op jit(solution)/shard_map/ppermute | solution.py:300
  22.6 1.5 %collective-permute-done.4.q1 = bf16[256,128]{1,0:T(8,128)(2,1)S(1)} collective-permute-done((bf16[256,128]{1,0:T(8,128)(2,1)S(1)}, bf16[256,128]{1,0:T(8,128)(2,1)S(1)}, u32[]{:S(2)}, u32[]{:S(2)}) %collective-permute-start.4) | collective-permute-done | bytes 65568 | tf_op jit(solution)/shard_map/ppermute | solution.py:300
  24.8 2.5 %collective-permute-done.6.q3 = bf16[256,128]{1,0:T(8,128)(2,1)S(1)} collective-permute-done((bf16[256,128]{1,0:T(8,128)(2,1)S(1)}, bf16[256,128]{1,0:T(8,128)(2,1)S(1)}, u32[]{:S(2)}, u32[]{:S(2)}) %collective-permute-start.6) | collective-permute-done | bytes 65568 | tf_op jit(solution)/shard_map/ppermute | solution.py:300
  27.2 1.1 %finish_far.1 = (bf16[128,1024]{1,0:T(8,128)(2,1)S(1)}, f32[128,1024]{1,0:T(8,128)S(1)}, bf16[256,1024]{1,0:T(8,128)(2,1)S(1)}) custom-call(f32[256,1024]{1,0:T(8,128)S(1)} %get-tuple-element.47.own, f32[256,1024]{1,0:T(8,128)S(1)} %get-tuple-element.48.lead, f32[512,128]{1,0:T(8,128)S(1)} %bitcast.9, bf16[256,128]{1,0:T(8,128)(2,1)S(1)} %get-tuple-element.53.q0, ...), custom_call_target="tpu_custom_call" | custom-call | flops 536870912 | tf_op jit(solution)/shard_map/finish_far/pallas_call | solution.py:505
  28.4 1.0 %project_more.1 = (bf16[128,1536]{1,0:T(8,128)(2,1)S(1)}, f32[128,1536]{1,0:T(8,128)S(1)}) custom-call(bf16[256,1024]{1,0:T(8,128)(2,1)S(1)} %get-tuple-element.60.normed, bf16[1024,4096]{1,0:T(8,128)(2,1)S(1)} %bitcast.7), custom_call_target="tpu_custom_call" | custom-call | flops 805306368 | tf_op jit(solution)/shard_map/project_more/pallas_call | solution.py:505
  30.0 1.6 %collective-permute-start.12 = (bf16[128,1024]{1,0:T(8,128)(2,1)S(1)}, bf16[128,1024]{1,0:T(8,128)(2,1)S(1)}, u32[]{:S(2)}, u32[]{:S(2)}) collective-permute-start(bf16[128,1024]{1,0:T(8,128)(2,1)S(1)} %add_pair.4), channel_id=1, source_target_pairs={{0,2},{1,3},{2,0},{3,1},{4,6},{5,7},{6,4},{7,5},{8,10},{9,11},{10,... | collective-permute-start | bytes 786440 | tf_op jit(solution)/shard_map/ppermute | solution.py:666
  31.6 3.2 %within_near.1 = (f32[256,1024]{1,0:T(8,128)S(1)}, f32[256,1024]{1,0:T(8,128)S(1)}) custom-call(f32[4,48,128]{2,1,0:T(8,128)S(1)} %copy-done.8, f32[512,1024]{1,0:T(8,128)S(1)} %copy-done.2, f32[512,128]{1,0:T(8,128)S(1)} %bitcast.17, f32[512,128]{1,0:T(8,128)S(1)} %bitcast.10, bf16[512,1024]{1,0:T(8,128)(2,1)S(1)} %copy-done.3, f32[1,16]{1,0:T(1,128)S(1)} %bitcast.19), custom_call_target="tpu_custom_call" | custom-call | flops 4000000000 | bytes 3000000 | tf_op jit(solution)/shard_map/within_near/pallas_call | solution.py:420
  35.5 2.5 %finish_near.1 = (bf16[128,5632]{1,0:T(8,128)(2,1)S(1)}, f32[128,1536]{1,0:T(8,128)S(1)}, bf16[128,1024]{1,0:T(8,128)(2,1)S(1)}) custom-call(bf16[256,1024]{1,0:T(8,128)(2,1)S(1)} %get-tuple-element.60.normed, f32[256,1024]{1,0:T(8,128)S(1)} %get-tuple-element.64.own, f32[256,1024]{1,0:T(8,128)S(1)} %get-tuple-element.65.lead, f32[512,128]{1,0:T(8,128)S(1)} %bitcast.11, ...), custom_call_target="tpu_custom_call" | custom-call | flops 1879048192 | tf_op jit(solution)/shard_map/finish_near/pallas_call | solution.py:505
  38.0 1.2 %collective-permute-done.12.refs_0_ = bf16[128,1024]{1,0:T(8,128)(2,1)S(1)} collective-permute-done((bf16[128,1024]{1,0:T(8,128)(2,1)S(1)}, bf16[128,1024]{1,0:T(8,128)(2,1)S(1)}, u32[]{:S(2)}, u32[]{:S(2)}) %collective-permute-start.12) | collective-permute-done | bytes 262176 | tf_op jit(solution)/shard_map/ppermute | solution.py:666
  39.2 2.0 %collective-permute-done.9.come = bf16[128,5632]{1,0:T(8,128)(2,1)S(1)} collective-permute-done((bf16[128,5632]{1,0:T(8,128)(2,1)S(1)}, bf16[128,5632]{1,0:T(8,128)(2,1)S(1)}, u32[]{:S(2)}, u32[]{:S(2)}) %collective-permute-start.9) | collective-permute-done | bytes 1441824 | tf_op jit(solution)/shard_map/ppermute | solution.py:627
  41.3 1.6 %collective-permute-start.10 = (bf16[128,1536]{1,0:T(8,128)(2,1)S(1)}, bf16[128,1536]{1,0:T(8,128)(2,1)S(1)}, u32[]{:S(2)}, u32[]{:S(2)}) collective-permute-start(bf16[128,1536]{1,0:T(8,128)(2,1)S(1)} %add_pair.5), channel_id=1, source_target_pairs={{0,2},{1,3},{2,0},{3,1},{4,6},{5,7},{6,4},{7,5},{8,10},{9,11},{10,... | collective-permute-start | bytes 1179656 | tf_op jit(solution)/shard_map/ppermute | solution.py:669
  42.9 4.8 %collective-permute-done.11.refs_0_ = bf16[128,1536]{1,0:T(8,128)(2,1)S(1)} collective-permute-done((bf16[128,1536]{1,0:T(8,128)(2,1)S(1)}, bf16[128,1536]{1,0:T(8,128)(2,1)S(1)}, u32[]{:S(2)}, u32[]{:S(2)}) %collective-permute-start.11) | collective-permute-done | bytes 393248 | tf_op jit(solution)/shard_map/ppermute | solution.py:667
  47.7 1.3 %project_kept.1.kept = f32[128,4096]{1,0:T(8,128)S(1)} custom-call(bf16[128,1024]{1,0:T(8,128)(2,1)S(1)} %get-tuple-element.66.kept, bf16[128,5632]{1,0:T(8,128)(2,1)S(1)} %collective-permute-done.9.come, bf16[1024,4096]{1,0:T(8,128)(2,1)S(1)} %bitcast.7), custom_call_target="tpu_custom_call" | custom-call | flops 1073741824 | tf_op jit(solution)/shard_map/project_kept/pallas_call | solution.py:505
  49.0 1.0 %early_sums.1.refs_1_ = bf16[128,4096]{1,0:T(8,128)(2,1)} custom-call(f32[128,4096]{1,0:T(8,128)S(1)} %project_kept.1.kept, bf16[128,1024]{1,0:T(8,128)(2,1)S(1)} %get-tuple-element.71.first, bf16[128,1536]{1,0:T(8,128)(2,1)S(1)} %get-tuple-element.72.second), custom_call_target="tpu_custom_call" | custom-call | tf_op jit(solution)/shard_map/early_sums/pallas_call | solution.py:548
  49.9 5.3 %collective-permute-done.10.refs_0_ = bf16[128,1536]{1,0:T(8,128)(2,1)S(1)} collective-permute-done((bf16[128,1536]{1,0:T(8,128)(2,1)S(1)}, bf16[128,1536]{1,0:T(8,128)(2,1)S(1)}, u32[]{:S(2)}, u32[]{:S(2)}) %collective-permute-start.10) | collective-permute-done | bytes 393248 | tf_op jit(solution)/shard_map/ppermute | solution.py:669
  55.3 0.8 %last_sums.1 = bf16[128,4096]{1,0:T(8,128)(2,1)} custom-call(f32[128,4096]{1,0:T(8,128)S(1)} %project_kept.1.kept, bf16[128,1536]{1,0:T(8,128)(2,1)S(1)} %get-tuple-element.73.third, bf16[128,4096]{1,0:T(8,128)(2,1)} %get-tuple-element.74.filled), custom_call_target="tpu_custom_call", output_to_operand_aliasing={{}: (2, {})} | custom-call | tf_op jit(solution)/shard_map/last_sums/pallas_call | solution.py:580
  (43 shorter events, 4.2 us)
Async XLA Ops:
  0.0 8.0 %copy-start = (f32[512,1,128]{2,1,0:T(1,128)S(1)}, f32[512,1,128]{2,1,0:T(1,128)}, u32[]{:S(2)}) copy-start(f32[512,1,128]{2,1,0:T(1,128)} %param.14) | copy-start | bytes 786436
  0.0 8.0 %copy-start.2 = (f32[512,1024]{1,0:T(8,128)S(1)}, f32[512,1024]{1,0:T(8,128)}, u32[]{:S(2)}) copy-start(f32[512,1024]{1,0:T(8,128)} %x_ref.3) | copy-start | bytes 6291460
  0.0 8.0 %copy-start.3 = (bf16[512,1024]{1,0:T(8,128)(2,1)S(1)}, bf16[512,1024]{1,0:T(8,128)(2,1)}, u32[]{:S(2)}) copy-start(bf16[512,1024]{1,0:T(8,128)(2,1)} %gate_ref.3) | copy-start | bytes 3145732
  0.0 8.0 %copy-start.4 = (f32[512,1,128]{2,1,0:T(1,128)S(1)}, f32[512,1,128]{2,1,0:T(1,128)}, u32[]{:S(2)}) copy-start(f32[512,1,128]{2,1,0:T(1,128)} %param.13) | copy-start | bytes 786436
  0.0 8.0 %copy-start.5 = (f32[16]{0:T(128)S(1)}, f32[16]{0:T(128)}, u32[]{:S(2)}) copy-start(f32[16]{0:T(128)} %param.15) | copy-start | bytes 196
  3.4 9.5 %collective-permute-start = (bf16[272,128]{1,0:T(8,128)(2,1)}, bf16[272,128]{1,0:T(8,128)(2,1)S(1)}, u32[]{:S(2)}, u32[]{:S(2)}) collective-permute-start(bf16[272,128]{1,0:T(8,128)(2,1)} %get-tuple-element.44), channel_id=1, source_target_pairs={{0,4},{4,0},{8,12},{12,8},{16,20},{20,16},{24,28},{28,24},{1,5},{5... | collective-permute-start | bytes 208904 | tf_op jit(solution)/shard_map/ppermute | solution.py:300
  6.4 6.5 %collective-permute-start.1 = (bf16[272,128]{1,0:T(8,128)(2,1)}, bf16[272,128]{1,0:T(8,128)(2,1)S(1)}, u32[]{:S(2)}, u32[]{:S(2)}) collective-permute-start(bf16[272,128]{1,0:T(8,128)(2,1)} %get-tuple-element.45), channel_id=1, source_target_pairs={{0,8},{4,12},{8,0},{12,4},{16,24},{20,28},{24,16},{28,20},{1,9},{5... | collective-permute-start | bytes 208904 | tf_op jit(solution)/shard_map/ppermute | solution.py:300
  8.0 5.4 %collective-permute-start.2 = (bf16[272,128]{1,0:T(8,128)(2,1)}, bf16[272,128]{1,0:T(8,128)(2,1)S(1)}, u32[]{:S(2)}, u32[]{:S(2)}) collective-permute-start(bf16[272,128]{1,0:T(8,128)(2,1)} %get-tuple-element.46), channel_id=1, source_target_pairs={{0,12},{4,8},{8,4},{12,0},{16,28},{20,24},{24,20},{28,16},{1,13},{... | collective-permute-start | bytes 208904 | tf_op jit(solution)/shard_map/ppermute | solution.py:300
  8.0 19.3 %slice-start = ((s8[8388608]{0:T(1024)(128)(4,1)}), s8[4194304]{0:T(1024)(128)(4,1)S(1)}, s32[]{:S(2)}) async-start(s8[8388608]{0:T(1024)(128)(4,1)} %bitcast.6), calls=%async_computation | async-start | bytes 8388608
  8.0 1.0 %copy-start.7 = (f32[4,48,128]{2,1,0:T(8,128)S(1)}, f32[4,48,128]{2,1,0:T(8,128)}, u32[]{:S(2)}) copy-start(f32[4,48,128]{2,1,0:T(8,128)} %get-tuple-element.63.aux) | copy-start | bytes 294916
  9.1 3.2 %copy-start.6 = (bf16[32,640]{1,0:T(8,128)(2,1)S(1)}, bf16[32,640]{1,0:T(8,128)(2,1)}, u32[]{:S(2)}) copy-start(bf16[32,640]{1,0:T(8,128)(2,1)} %get-tuple-element.43.wk) | copy-start | bytes 122884
  9.1 18.2 %slice-start.1 = ((s8[8388608]{0:T(1024)(128)(4,1)}), s8[4194304]{0:T(1024)(128)(4,1)S(1)}, s32[]{:S(2)}) async-start(s8[8388608]{0:T(1024)(128)(4,1)} %bitcast.6), calls=%async_computation.1 | async-start | bytes 8388608
  12.2 15.0 %copy-start.1 = (f32[1024]{0:T(1024)S(1)}, f32[1024]{0:T(1024)}, u32[]{:S(2)}) copy-start(f32[1024]{0:T(1024)} %param.16) | copy-start | bytes 12292
  13.5 5.3 %collective-permute-start.3 = (bf16[272,128]{1,0:T(8,128)(2,1)S(1)}, bf16[272,128]{1,0:T(8,128)(2,1)S(1)}, u32[]{:S(2)}, u32[]{:S(2)}) collective-permute-start(bf16[272,128]{1,0:T(8,128)(2,1)S(1)} %join_states.1), channel_id=1, source_target_pairs={{0,16},{4,20},{8,24},{12,28},{16,0},{20,4},{24,8},{28,12},{1,17},{... | collective-permute-start | bytes 208904 | tf_op jit(solution)/shard_map/ppermute | solution.py:300
  19.0 5.0 %collective-permute-start.4 = (bf16[256,128]{1,0:T(8,128)(2,1)S(1)}, bf16[256,128]{1,0:T(8,128)(2,1)S(1)}, u32[]{:S(2)}, u32[]{:S(2)}) collective-permute-start(bf16[256,128]{1,0:T(8,128)(2,1)S(1)} %get-tuple-element.54), channel_id=1, source_target_pairs={{0,4},{4,0},{8,12},{12,8},{16,20},{20,16},{24,28},{28,24},{1,5},{5... | collective-permute-start | bytes 196616 | tf_op jit(solution)/shard_map/ppermute | solution.py:300
  20.5 4.3 %collective-permute-start.5 = (bf16[256,128]{1,0:T(8,128)(2,1)S(1)}, bf16[256,128]{1,0:T(8,128)(2,1)S(1)}, u32[]{:S(2)}, u32[]{:S(2)}) collective-permute-start(bf16[256,128]{1,0:T(8,128)(2,1)S(1)} %get-tuple-element.55), channel_id=1, source_target_pairs={{0,8},{4,12},{8,0},{12,4},{16,24},{20,28},{24,16},{28,20},{1,9},{5... | collective-permute-start | bytes 196616 | tf_op jit(solution)/shard_map/ppermute | solution.py:300
  22.1 5.2 %collective-permute-start.6 = (bf16[256,128]{1,0:T(8,128)(2,1)S(1)}, bf16[256,128]{1,0:T(8,128)(2,1)S(1)}, u32[]{:S(2)}, u32[]{:S(2)}) collective-permute-start(bf16[256,128]{1,0:T(8,128)(2,1)S(1)} %get-tuple-element.56), channel_id=1, source_target_pairs={{0,12},{4,8},{8,4},{12,0},{16,28},{20,24},{24,20},{28,16},{1,13},{... | collective-permute-start | bytes 196616 | tf_op jit(solution)/shard_map/ppermute | solution.py:300
  28.3 1.6 %collective-permute-start.8 = (bf16[128,1024]{1,0:T(8,128)(2,1)S(1)}, bf16[128,1024]{1,0:T(8,128)(2,1)S(1)}, u32[]{:S(2)}, u32[]{:S(2)}) collective-permute-start(bf16[128,1024]{1,0:T(8,128)(2,1)S(1)} %get-tuple-element.62), channel_id=1, source_target_pairs={{0,1},{1,0},{2,3},{3,2},{4,5},{5,4},{6,7},{7,6},{8,9},{9,8},{10,11... | collective-permute-start | bytes 786440 | tf_op jit(solution)/shard_map/ppermute | solution.py:627
  28.4 3.2 %copy-start.8 = (f32[4,48,128]{2,1,0:T(8,128)S(1)}, f32[4,48,128]{2,1,0:T(8,128)}, u32[]{:S(2)}) copy-start(f32[4,48,128]{2,1,0:T(8,128)} %get-tuple-element.63.aux) | copy-start | bytes 294916
  29.4 5.4 %collective-permute-start.7 = (bf16[128,1536]{1,0:T(8,128)(2,1)S(1)}, bf16[128,1536]{1,0:T(8,128)(2,1)S(1)}, u32[]{:S(2)}, u32[]{:S(2)}) collective-permute-start(bf16[128,1536]{1,0:T(8,128)(2,1)S(1)} %get-tuple-element.59), channel_id=1, source_target_pairs={{0,1},{1,0},{2,3},{3,2},{4,5},{5,4},{6,7},{7,6},{8,9},{9,8},{10,11... | collective-permute-start | bytes 1179656 | tf_op jit(solution)/shard_map/ppermute | solution.py:627
  30.0 9.2 %collective-permute-start.12 = (bf16[128,1024]{1,0:T(8,128)(2,1)S(1)}, bf16[128,1024]{1,0:T(8,128)(2,1)S(1)}, u32[]{:S(2)}, u32[]{:S(2)}) collective-permute-start(bf16[128,1024]{1,0:T(8,128)(2,1)S(1)} %add_pair.4), channel_id=1, source_target_pairs={{0,2},{1,3},{2,0},{3,1},{4,6},{5,7},{6,4},{7,5},{8,10},{9,11},{10,... | collective-permute-start | bytes 786440 | tf_op jit(solution)/shard_map/ppermute | solution.py:666
  34.9 12.8 %collective-permute-start.11 = (bf16[128,1536]{1,0:T(8,128)(2,1)S(1)}, bf16[128,1536]{1,0:T(8,128)(2,1)S(1)}, u32[]{:S(2)}, u32[]{:S(2)}) collective-permute-start(bf16[128,1536]{1,0:T(8,128)(2,1)S(1)} %add_pair.3), channel_id=1, source_target_pairs={{0,2},{1,3},{2,0},{3,1},{4,6},{5,7},{6,4},{7,5},{8,10},{9,11},{10,... | collective-permute-start | bytes 1179656 | tf_op jit(solution)/shard_map/ppermute | solution.py:667
  38.0 3.3 %collective-permute-start.9 = (bf16[128,5632]{1,0:T(8,128)(2,1)S(1)}, bf16[128,5632]{1,0:T(8,128)(2,1)S(1)}, u32[]{:S(2)}, u32[]{:S(2)}) collective-permute-start(bf16[128,5632]{1,0:T(8,128)(2,1)S(1)} %get-tuple-element.67), channel_id=1, source_target_pairs={{0,1},{1,0},{2,3},{3,2},{4,5},{5,4},{6,7},{7,6},{8,9},{9,8},{10,11... | collective-permute-start | bytes 4325384 | tf_op jit(solution)/shard_map/ppermute | solution.py:627
  41.3 13.9 %collective-permute-start.10 = (bf16[128,1536]{1,0:T(8,128)(2,1)S(1)}, bf16[128,1536]{1,0:T(8,128)(2,1)S(1)}, u32[]{:S(2)}, u32[]{:S(2)}) collective-permute-start(bf16[128,1536]{1,0:T(8,128)(2,1)S(1)} %add_pair.5), channel_id=1, source_target_pairs={{0,2},{1,3},{2,0},{3,1},{4,6},{5,7},{6,4},{7,5},{8,10},{9,11},{10,... | collective-permute-start | bytes 1179656 | tf_op jit(solution)/shard_map/ppermute | solution.py:669

commit v7 on v4

--- a/solution.py
+++ b/solution.py
@@ -15,7 +15,7 @@
 F32 = jnp.float32
 VMEM_LIMIT = 16 * 1024 * 1024
 WHOLE_VMEM = 61 * 1024 * 1024 + 512 * 1024
-PIECES = ((0, 1024), (1024, 1536), (2560, 1536))
+PIECES = ((0, 768), (768, 2304), (3072, 1024))
 
 
 def dot(a, b, contract=((1,), (0,)), precision=None):
@@ -452,7 +452,7 @@
 
 
 def project_both(normed, w, start, columns, theirs, mine, at=0):
-    wide = 512
+    wide = 256
     for k in range(0, columns, wide):
         out = dot(normed[...], w[:, start + k:start + k + wide])
         theirs[:, at + k:at + k + wide] = out[:CHUNK].astype(BF)

time: 55.4 us -> 57.8 us (1.043)
  waiting for transfers between devices: 20.4 us -> 22.7 us
    ppermute x1, waiting for transfers between devices: 4.79 us -> 8.75 us  [per_device(): second, first = await_piece(lax.ppermute(second, 'head', far), first)]
    ppermute x1, waiting for transfers between devices: 5.29 us -> 2.07 us  [per_device(): third, filled = await_piece(lax.ppermute(third, 'head', far), filled)]
    ppermute x3, waiting for transfers between devices: 2.01 us -> 4.78 us  [add(): come = lax.ppermute(theirs, 'head', near)]
    ppermute x1, waiting for transfers between devices: 1.21 us -> 0.01 us  [per_device(): first = await_piece(lax.ppermute(first, 'head', far))[0]]
  transfers between devices with their start and end apart: 13 -> 13, of which waited for: 9 -> 9; matrix products, arithmetic and copies ran while one was open for 0% -> 0% of each run, Pallas kernels for 23% -> 20%
where the time goes in v7:
time: 57.8 us; the launch traced here: 57.7 us
  waiting for transfers between devices  22.7 us (39%)
  Pallas kernels  18.6 us (32%)
  starting transfers between devices  15.2 us (26%)
  local copies, waits for them, and re-layouts  0.81 us (1%)
    ppermute x7, starting transfers between devices, exchange(): return lax.ppermute(value, 'seq', [(s, s ^ distance) for s in range(count)])  10.8 us
    ppermute x1, waiting for transfers between devices, per_device(): second, first = await_piece(lax.ppermute(second, 'head', far), first)  8.75 us
    ppermute x7, waiting for transfers between devices, exchange(): return lax.ppermute(value, 'seq', [(s, s ^ distance) for s in range(count)])  7.08 us
    pallas_call x2, Pallas kernels, within(): pl.pallas_call(functools.partial(within_kernel, far), in_specs=[VMEM] * 6...  6.37 us
    pallas_call x7, Pallas kernels, local_call(): pl.pallas_call(kernel, in_specs=[VMEM] * len(operands), out_specs=[VMEM]...  6.18 us
    ppermute x3, waiting for transfers between devices, add(): come = lax.ppermute(theirs, 'head', near)  4.78 us
    pallas_call x1, Pallas kernels, give_states(): pl.pallas_call(give_kernel, in_specs=[HBM] * 4, out_shape=[jax.ShapeDtype...  3.33 us
    ppermute x1, waiting for transfers between devices, per_device(): third, filled = await_piece(lax.ppermute(third, 'head', far), filled)  2.07 us
  transfers between devices with their start and end apart: 13, of which 9 were waited for; matrix products, arithmetic and copies ran while one was open for 0% of the time, Pallas kernels for 20%

profile of v7, /device:TPU:0, one launch (start us, length us, event | category | flops | bytes accessed | tf_op | source)
XLA Modules:
  0.0 57.7 jit_solution(15198009440001800920)
XLA Ops:
  0.0 3.3 %give_states.1 = (bf16[272,128]{1,0:T(8,128)(2,1)}, bf16[272,128]{1,0:T(8,128)(2,1)}, bf16[272,128]{1,0:T(8,128)(2,1)}, bf16[32,640]{1,0:T(8,128)(2,1)}, f32[4,48,128]{2,1,0:T(8,128)}) custom-call(f32[16,512]{1,0:T(8,128)} %bitcast.20, f32[1,16]{1,0:T(1,128)} %bitcast.21, f32[512,1024]{1,0:T(8,128)} %x_ref.3, f32[512,128]{1,0:T(8,128)} %bitcast.8), custom_call_target="tpu_custom_call" | custom-call | flops 200000000 | bytes 1500000 | tf_op jit(solution)/shard_map/give_states/pallas_call | solution.py:155
  3.4 3.0 %collective-permute-start = (bf16[272,128]{1,0:T(8,128)(2,1)}, bf16[272,128]{1,0:T(8,128)(2,1)S(1)}, u32[]{:S(2)}, u32[]{:S(2)}) collective-permute-start(bf16[272,128]{1,0:T(8,128)(2,1)} %get-tuple-element.41), channel_id=1, source_target_pairs={{0,4},{4,0},{8,12},{12,8},{16,20},{20,16},{24,28},{28,24},{1,5},{5... | collective-permute-start | bytes 208904 | tf_op jit(solution)/shard_map/ppermute | solution.py:300
  6.4 1.6 %collective-permute-start.1 = (bf16[272,128]{1,0:T(8,128)(2,1)}, bf16[272,128]{1,0:T(8,128)(2,1)S(1)}, u32[]{:S(2)}, u32[]{:S(2)}) collective-permute-start(bf16[272,128]{1,0:T(8,128)(2,1)} %get-tuple-element.42), channel_id=1, source_target_pairs={{0,8},{4,12},{8,0},{12,4},{16,24},{20,28},{24,16},{28,20},{1,9},{5... | collective-permute-start | bytes 208904 | tf_op jit(solution)/shard_map/ppermute | solution.py:300
  8.0 0.8 %copy-done.3 = bf16[32,640]{1,0:T(8,128)(2,1)S(1)} copy-done((bf16[32,640]{1,0:T(8,128)(2,1)S(1)}, bf16[32,640]{1,0:T(8,128)(2,1)}, u32[]{:S(2)}) %copy-start.3) | copy-done | bytes 40984
  9.3 2.2 %collective-permute-done.1.come2 = bf16[272,128]{1,0:T(8,128)(2,1)S(1)} collective-permute-done((bf16[272,128]{1,0:T(8,128)(2,1)}, bf16[272,128]{1,0:T(8,128)(2,1)S(1)}, u32[]{:S(2)}, u32[]{:S(2)}) %collective-permute-start.1) | collective-permute-done | bytes 69664 | tf_op jit(solution)/shard_map/ppermute | solution.py:300
  11.5 1.9 %collective-permute-done.2.come3 = bf16[272,128]{1,0:T(8,128)(2,1)S(1)} collective-permute-done((bf16[272,128]{1,0:T(8,128)(2,1)}, bf16[272,128]{1,0:T(8,128)(2,1)S(1)}, u32[]{:S(2)}, u32[]{:S(2)}) %collective-permute-start.2) | collective-permute-done | bytes 69664 | tf_op jit(solution)/shard_map/ppermute | solution.py:300
  13.4 2.7 %collective-permute-start.3 = (bf16[272,128]{1,0:T(8,128)(2,1)S(1)}, bf16[272,128]{1,0:T(8,128)(2,1)S(1)}, u32[]{:S(2)}, u32[]{:S(2)}) collective-permute-start(bf16[272,128]{1,0:T(8,128)(2,1)S(1)} %join_states.1), channel_id=1, source_target_pairs={{0,16},{4,20},{8,24},{12,28},{16,0},{20,4},{24,8},{28,12},{1,17},{... | collective-permute-start | bytes 208904 | tf_op jit(solution)/shard_map/ppermute | solution.py:300
  16.1 3.2 %within_far.1 = (f32[256,1024]{1,0:T(8,128)S(1)}, f32[256,1024]{1,0:T(8,128)S(1)}) custom-call(f32[4,48,128]{2,1,0:T(8,128)S(1)} %copy-done.6, f32[512,1024]{1,0:T(8,128)S(1)} %copy-done, f32[512,128]{1,0:T(8,128)S(1)} %bitcast.10, f32[512,128]{1,0:T(8,128)S(1)} %bitcast.12, bf16[512,1024]{1,0:T(8,128)(2,1)S(1)} %copy-done.5, f32[1,16]{1,0:T(1,128)S(1)} %bitcast.18), custom_call_target="tpu_custom_call" | custom-call | flops 4000000000 | bytes 3000000 | tf_op jit(solution)/shard_map/within_far/pallas_call | solution.py:418
  20.3 0.8 %collective-permute-start.5 = (bf16[256,128]{1,0:T(8,128)(2,1)S(1)}, bf16[256,128]{1,0:T(8,128)(2,1)S(1)}, u32[]{:S(2)}, u32[]{:S(2)}) collective-permute-start(bf16[256,128]{1,0:T(8,128)(2,1)S(1)} %get-tuple-element.49), channel_id=1, source_target_pairs={{0,8},{4,12},{8,0},{12,4},{16,24},{20,28},{24,16},{28,20},{1,9},{5... | collective-permute-start | bytes 196616 | tf_op jit(solution)/shard_map/ppermute | solution.py:300
  21.1 2.1 %collective-permute-start.6 = (bf16[256,128]{1,0:T(8,128)(2,1)S(1)}, bf16[256,128]{1,0:T(8,128)(2,1)S(1)}, u32[]{:S(2)}, u32[]{:S(2)}) collective-permute-start(bf16[256,128]{1,0:T(8,128)(2,1)S(1)} %get-tuple-element.50), channel_id=1, source_target_pairs={{0,12},{4,8},{8,4},{12,0},{16,28},{20,24},{24,20},{28,16},{1,13},{... | collective-permute-start | bytes 196616 | tf_op jit(solution)/shard_map/ppermute | solution.py:300
  23.2 0.8 %collective-permute-done.4.q1 = bf16[256,128]{1,0:T(8,128)(2,1)S(1)} collective-permute-done((bf16[256,128]{1,0:T(8,128)(2,1)S(1)}, bf16[256,128]{1,0:T(8,128)(2,1)S(1)}, u32[]{:S(2)}, u32[]{:S(2)}) %collective-permute-start.4) | collective-permute-done | bytes 65568 | tf_op jit(solution)/shard_map/ppermute | solution.py:300
  24.6 1.7 %collective-permute-done.6.q3 = bf16[256,128]{1,0:T(8,128)(2,1)S(1)} collective-permute-done((bf16[256,128]{1,0:T(8,128)(2,1)S(1)}, bf16[256,128]{1,0:T(8,128)(2,1)S(1)}, u32[]{:S(2)}, u32[]{:S(2)}) %collective-permute-start.6) | collective-permute-done | bytes 65568 | tf_op jit(solution)/shard_map/ppermute | solution.py:300
  26.3 1.0 %finish_far.1 = (bf16[128,768]{1,0:T(8,128)(2,1)S(1)}, f32[128,768]{1,0:T(8,128)S(1)}, bf16[256,1024]{1,0:T(8,128)(2,1)S(1)}) custom-call(f32[256,1024]{1,0:T(8,128)S(1)} %get-tuple-element.44.own, f32[256,1024]{1,0:T(8,128)S(1)} %get-tuple-element.45.lead, f32[512,128]{1,0:T(8,128)S(1)} %bitcast.13, bf16[256,128]{1,0:T(8,128)(2,1)S(1)} %get-tuple-element.47.q0, ...), custom_call_target="tpu_custom_call" | custom-call | flops 402653184 | tf_op jit(solution)/shard_map/finish_far/pallas_call | solution.py:503
  27.2 1.4 %project_more.1 = (bf16[128,2304]{1,0:T(8,128)(2,1)S(1)}, f32[128,2304]{1,0:T(8,128)S(1)}) custom-call(bf16[256,1024]{1,0:T(8,128)(2,1)S(1)} %get-tuple-element.54.normed, bf16[1024,4096]{1,0:T(8,128)(2,1)S(1)} %bitcast.7), custom_call_target="tpu_custom_call" | custom-call | flops 1207959552 | tf_op jit(solution)/shard_map/project_more/pallas_call | solution.py:503
  29.2 1.8 %collective-permute-done.8.come = bf16[128,768]{1,0:T(8,128)(2,1)S(1)} collective-permute-done((bf16[128,768]{1,0:T(8,128)(2,1)S(1)}, bf16[128,768]{1,0:T(8,128)(2,1)S(1)}, u32[]{:S(2)}, u32[]{:S(2)}) %collective-permute-start.8) | collective-permute-done | bytes 196640 | tf_op jit(solution)/shard_map/ppermute | solution.py:625
  31.0 1.6 %collective-permute-start.12 = (bf16[128,768]{1,0:T(8,128)(2,1)S(1)}, bf16[128,768]{1,0:T(8,128)(2,1)S(1)}, u32[]{:S(2)}, u32[]{:S(2)}) collective-permute-start(bf16[128,768]{1,0:T(8,128)(2,1)S(1)} %add_pair.4), channel_id=1, source_target_pairs={{0,2},{1,3},{2,0},{3,1},{4,6},{5,7},{6,4},{7,5},{8,10},{9,11},{10,... | collective-permute-start | bytes 589832 | tf_op jit(solution)/shard_map/ppermute | solution.py:664
  32.6 3.2 %within_near.1 = (f32[256,1024]{1,0:T(8,128)S(1)}, f32[256,1024]{1,0:T(8,128)S(1)}) custom-call(f32[4,48,128]{2,1,0:T(8,128)S(1)} %copy-done.6, f32[512,1024]{1,0:T(8,128)S(1)} %copy-done, f32[512,128]{1,0:T(8,128)S(1)} %bitcast.11, f32[512,128]{1,0:T(8,128)S(1)} %bitcast.14, bf16[512,1024]{1,0:T(8,128)(2,1)S(1)} %copy-done.5, f32[1,16]{1,0:T(1,128)S(1)} %bitcast.19), custom_call_target="tpu_custom_call" | custom-call | flops 4000000000 | bytes 3000000 | tf_op jit(solution)/shard_map/within_near/pallas_call | solution.py:418
  36.5 2.2 %finish_near.1 = (bf16[128,5120]{1,0:T(8,128)(2,1)S(1)}, f32[128,1024]{1,0:T(8,128)S(1)}, bf16[128,1024]{1,0:T(8,128)(2,1)S(1)}) custom-call(bf16[256,1024]{1,0:T(8,128)(2,1)S(1)} %get-tuple-element.54.normed, f32[256,1024]{1,0:T(8,128)S(1)} %get-tuple-element.58.own, f32[256,1024]{1,0:T(8,128)S(1)} %get-tuple-element.59.lead, f32[512,128]{1,0:T(8,128)S(1)} %bitcast.15, ...), custom_call_target="tpu_custom_call" | custom-call | flops 1610612736 | tf_op jit(solution)/shard_map/finish_near/pallas_call | solution.py:503
  38.9 3.0 %collective-permute-done.9.come = bf16[128,5120]{1,0:T(8,128)(2,1)S(1)} collective-permute-done((bf16[128,5120]{1,0:T(8,128)(2,1)S(1)}, bf16[128,5120]{1,0:T(8,128)(2,1)S(1)}, u32[]{:S(2)}, u32[]{:S(2)}) %collective-permute-start.9) | collective-permute-done | bytes 1310752 | tf_op jit(solution)/shard_map/ppermute | solution.py:625
  41.9 1.6 %collective-permute-start.10 = (bf16[128,1024]{1,0:T(8,128)(2,1)S(1)}, bf16[128,1024]{1,0:T(8,128)(2,1)S(1)}, u32[]{:S(2)}, u32[]{:S(2)}) collective-permute-start(bf16[128,1024]{1,0:T(8,128)(2,1)S(1)} %add_pair.5), channel_id=1, source_target_pairs={{0,2},{1,3},{2,0},{3,1},{4,6},{5,7},{6,4},{7,5},{8,10},{9,11},{10,... | collective-permute-start | bytes 786440 | tf_op jit(solution)/shard_map/ppermute | solution.py:667
  43.5 8.7 %collective-permute-done.11.refs_0_ = bf16[128,2304]{1,0:T(8,128)(2,1)S(1)} collective-permute-done((bf16[128,2304]{1,0:T(8,128)(2,1)S(1)}, bf16[128,2304]{1,0:T(8,128)(2,1)S(1)}, u32[]{:S(2)}, u32[]{:S(2)}) %collective-permute-start.11) | collective-permute-done | bytes 589856 | tf_op jit(solution)/shard_map/ppermute | solution.py:665
  52.3 1.3 %project_kept.1.kept = f32[128,4096]{1,0:T(8,128)S(1)} custom-call(bf16[128,1024]{1,0:T(8,128)(2,1)S(1)} %get-tuple-element.60.kept, bf16[128,5120]{1,0:T(8,128)(2,1)S(1)} %collective-permute-done.9.come, bf16[1024,4096]{1,0:T(8,128)(2,1)S(1)} %bitcast.7), custom_call_target="tpu_custom_call" | custom-call | flops 1073741824 | tf_op jit(solution)/shard_map/project_kept/pallas_call | solution.py:503
  53.6 1.1 %early_sums.1.refs_1_ = bf16[128,4096]{1,0:T(8,128)(2,1)} custom-call(f32[128,4096]{1,0:T(8,128)S(1)} %project_kept.1.kept, bf16[128,768]{1,0:T(8,128)(2,1)S(1)} %get-tuple-element.65.first, bf16[128,2304]{1,0:T(8,128)(2,1)S(1)} %get-tuple-element.66.second), custom_call_target="tpu_custom_call" | custom-call | tf_op jit(solution)/shard_map/early_sums/pallas_call | solution.py:546
  54.7 2.1 %collective-permute-done.10.refs_0_ = bf16[128,1024]{1,0:T(8,128)(2,1)S(1)} collective-permute-done((bf16[128,1024]{1,0:T(8,128)(2,1)S(1)}, bf16[128,1024]{1,0:T(8,128)(2,1)S(1)}, u32[]{:S(2)}, u32[]{:S(2)}) %collective-permute-start.10) | collective-permute-done | bytes 262176 | tf_op jit(solution)/shard_map/ppermute | solution.py:667
  (41 shorter events, 4.5 us)
Async XLA Ops:
  0.0 8.0 %copy-start = (f32[512,1024]{1,0:T(8,128)S(1)}, f32[512,1024]{1,0:T(8,128)}, u32[]{:S(2)}) copy-start(f32[512,1024]{1,0:T(8,128)} %x_ref.3) | copy-start | bytes 6291460
  0.0 8.0 %copy-start.1 = (f32[512,1,128]{2,1,0:T(1,128)S(1)}, f32[512,1,128]{2,1,0:T(1,128)}, u32[]{:S(2)}) copy-start(f32[512,1,128]{2,1,0:T(1,128)} %param.13) | copy-start | bytes 786436
  0.0 16.1 %copy-start.7 = (f32[16]{0:T(128)S(1)}, f32[16]{0:T(128)}, u32[]{:S(2)}) copy-start(f32[16]{0:T(128)} %param.15) | copy-start | bytes 196
  3.3 12.8 %copy-start.2 = (f32[512,1,128]{2,1,0:T(1,128)S(1)}, f32[512,1,128]{2,1,0:T(1,128)}, u32[]{:S(2)}) copy-start(f32[512,1,128]{2,1,0:T(1,128)} %param.14) | copy-start | bytes 786436
  3.4 6.0 %collective-permute-start = (bf16[272,128]{1,0:T(8,128)(2,1)}, bf16[272,128]{1,0:T(8,128)(2,1)S(1)}, u32[]{:S(2)}, u32[]{:S(2)}) collective-permute-start(bf16[272,128]{1,0:T(8,128)(2,1)} %get-tuple-element.41), channel_id=1, source_target_pairs={{0,4},{4,0},{8,12},{12,8},{16,20},{20,16},{24,28},{28,24},{1,5},{5... | collective-permute-start | bytes 208904 | tf_op jit(solution)/shard_map/ppermute | solution.py:300
  6.4 5.1 %collective-permute-start.1 = (bf16[272,128]{1,0:T(8,128)(2,1)}, bf16[272,128]{1,0:T(8,128)(2,1)S(1)}, u32[]{:S(2)}, u32[]{:S(2)}) collective-permute-start(bf16[272,128]{1,0:T(8,128)(2,1)} %get-tuple-element.42), channel_id=1, source_target_pairs={{0,8},{4,12},{8,0},{12,4},{16,24},{20,28},{24,16},{28,20},{1,9},{5... | collective-permute-start | bytes 208904 | tf_op jit(solution)/shard_map/ppermute | solution.py:300
  7.9 5.4 %collective-permute-start.2 = (bf16[272,128]{1,0:T(8,128)(2,1)}, bf16[272,128]{1,0:T(8,128)(2,1)S(1)}, u32[]{:S(2)}, u32[]{:S(2)}) collective-permute-start(bf16[272,128]{1,0:T(8,128)(2,1)} %get-tuple-element.43), channel_id=1, source_target_pairs={{0,12},{4,8},{8,4},{12,0},{16,28},{20,24},{24,20},{28,16},{1,13},{... | collective-permute-start | bytes 208904 | tf_op jit(solution)/shard_map/ppermute | solution.py:300
  8.0 0.8 %copy-start.3 = (bf16[32,640]{1,0:T(8,128)(2,1)S(1)}, bf16[32,640]{1,0:T(8,128)(2,1)}, u32[]{:S(2)}) copy-start(bf16[32,640]{1,0:T(8,128)(2,1)} %get-tuple-element.40.wk) | copy-start | bytes 122884
  8.7 7.4 %copy-start.5 = (bf16[512,1024]{1,0:T(8,128)(2,1)S(1)}, bf16[512,1024]{1,0:T(8,128)(2,1)}, u32[]{:S(2)}) copy-start(bf16[512,1024]{1,0:T(8,128)(2,1)} %gate_ref.3) | copy-start | bytes 3145732
  8.7 7.4 %copy-start.6 = (f32[4,48,128]{2,1,0:T(8,128)S(1)}, f32[4,48,128]{2,1,0:T(8,128)}, u32[]{:S(2)}) copy-start(f32[4,48,128]{2,1,0:T(8,128)} %get-tuple-element.57.aux) | copy-start | bytes 294916
  13.4 5.9 %collective-permute-start.3 = (bf16[272,128]{1,0:T(8,128)(2,1)S(1)}, bf16[272,128]{1,0:T(8,128)(2,1)S(1)}, u32[]{:S(2)}, u32[]{:S(2)}) collective-permute-start(bf16[272,128]{1,0:T(8,128)(2,1)S(1)} %join_states.1), channel_id=1, source_target_pairs={{0,16},{4,20},{8,24},{12,28},{16,0},{20,4},{24,8},{28,12},{1,17},{... | collective-permute-start | bytes 208904 | tf_op jit(solution)/shard_map/ppermute | solution.py:300
  16.1 10.1 %slice-start = ((s8[8388608]{0:T(1024)(128)(4,1)}), s8[4194304]{0:T(1024)(128)(4,1)S(1)}, s32[]{:S(2)}) async-start(s8[8388608]{0:T(1024)(128)(4,1)} %bitcast.6), calls=%async_computation | async-start | bytes 8388608
  16.1 10.1 %slice-start.1 = ((s8[8388608]{0:T(1024)(128)(4,1)}), s8[4194304]{0:T(1024)(128)(4,1)S(1)}, s32[]{:S(2)}) async-start(s8[8388608]{0:T(1024)(128)(4,1)} %bitcast.6), calls=%async_computation.1 | async-start | bytes 8388608
  16.1 10.1 %copy-start.4 = (f32[1024]{0:T(1024)S(1)}, f32[1024]{0:T(1024)}, u32[]{:S(2)}) copy-start(f32[1024]{0:T(1024)} %param.16) | copy-start | bytes 12292
  19.6 4.3 %collective-permute-start.4 = (bf16[256,128]{1,0:T(8,128)(2,1)S(1)}, bf16[256,128]{1,0:T(8,128)(2,1)S(1)}, u32[]{:S(2)}, u32[]{:S(2)}) collective-permute-start(bf16[256,128]{1,0:T(8,128)(2,1)S(1)} %get-tuple-element.48), channel_id=1, source_target_pairs={{0,4},{4,0},{8,12},{12,8},{16,20},{20,16},{24,28},{28,24},{1,5},{5... | collective-permute-start | bytes 196616 | tf_op jit(solution)/shard_map/ppermute | solution.py:300
  20.3 4.3 %collective-permute-start.5 = (bf16[256,128]{1,0:T(8,128)(2,1)S(1)}, bf16[256,128]{1,0:T(8,128)(2,1)S(1)}, u32[]{:S(2)}, u32[]{:S(2)}) collective-permute-start(bf16[256,128]{1,0:T(8,128)(2,1)S(1)} %get-tuple-element.49), channel_id=1, source_target_pairs={{0,8},{4,12},{8,0},{12,4},{16,24},{20,28},{24,16},{28,20},{1,9},{5... | collective-permute-start | bytes 196616 | tf_op jit(solution)/shard_map/ppermute | solution.py:300
  21.1 5.2 %collective-permute-start.6 = (bf16[256,128]{1,0:T(8,128)(2,1)S(1)}, bf16[256,128]{1,0:T(8,128)(2,1)S(1)}, u32[]{:S(2)}, u32[]{:S(2)}) collective-permute-start(bf16[256,128]{1,0:T(8,128)(2,1)S(1)} %get-tuple-element.50), channel_id=1, source_target_pairs={{0,12},{4,8},{8,4},{12,0},{16,28},{20,24},{24,20},{28,16},{1,13},{... | collective-permute-start | bytes 196616 | tf_op jit(solution)/shard_map/ppermute | solution.py:300
  28.6 7.2 %collective-permute-start.7 = (bf16[128,2304]{1,0:T(8,128)(2,1)S(1)}, bf16[128,2304]{1,0:T(8,128)(2,1)S(1)}, u32[]{:S(2)}, u32[]{:S(2)}) collective-permute-start(bf16[128,2304]{1,0:T(8,128)(2,1)S(1)} %get-tuple-element.53), channel_id=1, source_target_pairs={{0,1},{1,0},{2,3},{3,2},{4,5},{5,4},{6,7},{7,6},{8,9},{9,8},{10,11... | collective-permute-start | bytes 1769480 | tf_op jit(solution)/shard_map/ppermute | solution.py:625
  28.7 2.3 %collective-permute-start.8 = (bf16[128,768]{1,0:T(8,128)(2,1)S(1)}, bf16[128,768]{1,0:T(8,128)(2,1)S(1)}, u32[]{:S(2)}, u32[]{:S(2)}) collective-permute-start(bf16[128,768]{1,0:T(8,128)(2,1)S(1)} %get-tuple-element.56), channel_id=1, source_target_pairs={{0,1},{1,0},{2,3},{3,2},{4,5},{5,4},{6,7},{7,6},{8,9},{9,8},{10,11... | collective-permute-start | bytes 589832 | tf_op jit(solution)/shard_map/ppermute | solution.py:625
  31.0 7.8 %collective-permute-start.12 = (bf16[128,768]{1,0:T(8,128)(2,1)S(1)}, bf16[128,768]{1,0:T(8,128)(2,1)S(1)}, u32[]{:S(2)}, u32[]{:S(2)}) collective-permute-start(bf16[128,768]{1,0:T(8,128)(2,1)S(1)} %add_pair.4), channel_id=1, source_target_pairs={{0,2},{1,3},{2,0},{3,1},{4,6},{5,7},{6,4},{7,5},{8,10},{9,11},{10,... | collective-permute-start | bytes 589832 | tf_op jit(solution)/shard_map/ppermute | solution.py:664
  36.0 16.3 %collective-permute-start.11 = (bf16[128,2304]{1,0:T(8,128)(2,1)S(1)}, bf16[128,2304]{1,0:T(8,128)(2,1)S(1)}, u32[]{:S(2)}, u32[]{:S(2)}) collective-permute-start(bf16[128,2304]{1,0:T(8,128)(2,1)S(1)} %add_pair.3), channel_id=1, source_target_pairs={{0,2},{1,3},{2,0},{3,1},{4,6},{5,7},{6,4},{7,5},{8,10},{9,11},{10,... | collective-permute-start | bytes 1769480 | tf_op jit(solution)/shard_map/ppermute | solution.py:665
  38.8 3.1 %collective-permute-start.9 = (bf16[128,5120]{1,0:T(8,128)(2,1)S(1)}, bf16[128,5120]{1,0:T(8,128)(2,1)S(1)}, u32[]{:S(2)}, u32[]{:S(2)}) collective-permute-start(bf16[128,5120]{1,0:T(8,128)(2,1)S(1)} %get-tuple-element.61), channel_id=1, source_target_pairs={{0,1},{1,0},{2,3},{3,2},{4,5},{5,4},{6,7},{7,6},{8,9},{9,8},{10,11... | collective-permute-start | bytes 3932168 | tf_op jit(solution)/shard_map/ppermute | solution.py:625
  41.9 14.8 %collective-permute-start.10 = (bf16[128,1024]{1,0:T(8,128)(2,1)S(1)}, bf16[128,1024]{1,0:T(8,128)(2,1)S(1)}, u32[]{:S(2)}, u32[]{:S(2)}) collective-permute-start(bf16[128,1024]{1,0:T(8,128)(2,1)S(1)} %add_pair.5), channel_id=1, source_target_pairs={{0,2},{1,3},{2,0},{3,1},{4,6},{5,7},{6,4},{7,5},{8,10},{9,11},{10,... | collective-permute-start | bytes 786440 | tf_op jit(solution)/shard_map/ppermute | solution.py:667

commit v8 on v4

--- a/solution.py
+++ b/solution.py
@@ -15,7 +15,7 @@
 F32 = jnp.float32
 VMEM_LIMIT = 16 * 1024 * 1024
 WHOLE_VMEM = 61 * 1024 * 1024 + 512 * 1024
-PIECES = ((0, 1024), (1024, 1536), (2560, 1536))
+PIECES = ((0, 1024), (1024, 2048), (3072, 1024))
 
 
 def dot(a, b, contract=((1,), (0,)), precision=None):

time: 55.4 us -> 55.5 us (level)
    ppermute x1, waiting for transfers between devices: 4.79 us -> 8.01 us  [per_device(): second, first = await_piece(lax.ppermute(second, 'head', far), first)]
    ppermute x1, waiting for transfers between devices: 5.29 us -> 2.3 us  [per_device(): third, filled = await_piece(lax.ppermute(third, 'head', far), filled)]
  transfers between devices with their start and end apart: 13 -> 13, of which waited for: 9 -> 9; matrix products, arithmetic and copies ran while one was open for 0% -> 0% of each run, Pallas kernels for 23% -> 24%
where the time goes in v8:
time: 55.5 us; the launch traced here: 55.4 us
  waiting for transfers between devices  20.4 us (37%)
  Pallas kernels  18.6 us (34%)
  starting transfers between devices  15.2 us (27%)
  local copies, waits for them, and re-layouts  0.81 us (1%)
    ppermute x7, starting transfers between devices, exchange(): return lax.ppermute(value, 'seq', [(s, s ^ distance) for s in range(count)])  10.8 us
    ppermute x1, waiting for transfers between devices, per_device(): second, first = await_piece(lax.ppermute(second, 'head', far), first)  8.01 us
    ppermute x7, waiting for transfers between devices, exchange(): return lax.ppermute(value, 'seq', [(s, s ^ distance) for s in range(count)])  7.08 us
    pallas_call x2, Pallas kernels, within(): pl.pallas_call(functools.partial(within_kernel, far), in_specs=[VMEM] * 6...  6.39 us
    pallas_call x7, Pallas kernels, local_call(): pl.pallas_call(kernel, in_specs=[VMEM] * len(operands), out_specs=[VMEM]...  6.15 us
    pallas_call x1, Pallas kernels, give_states(): pl.pallas_call(give_kernel, in_specs=[HBM] * 4, out_shape=[jax.ShapeDtype...  3.33 us
    ppermute x1, waiting for transfers between devices, per_device(): third, filled = await_piece(lax.ppermute(third, 'head', far), filled)  2.3 us
    ppermute x3, waiting for transfers between devices, add(): come = lax.ppermute(theirs, 'head', near)  1.59 us
  transfers between devices with their start and end apart: 13, of which 9 were waited for; matrix products, arithmetic and copies ran while one was open for 0% of the time, Pallas kernels for 24%

profile of v8, /device:TPU:0, one launch (start us, length us, event | category | flops | bytes accessed | tf_op | source)
XLA Modules:
  0.0 55.4 jit_solution(6960691364109871779)
XLA Ops:
  0.0 3.3 %give_states.1 = (bf16[272,128]{1,0:T(8,128)(2,1)}, bf16[272,128]{1,0:T(8,128)(2,1)}, bf16[272,128]{1,0:T(8,128)(2,1)}, bf16[32,640]{1,0:T(8,128)(2,1)}, f32[4,48,128]{2,1,0:T(8,128)}) custom-call(f32[16,512]{1,0:T(8,128)} %bitcast.20, f32[1,16]{1,0:T(1,128)} %bitcast.21, f32[512,1024]{1,0:T(8,128)} %x_ref.3, f32[512,128]{1,0:T(8,128)} %bitcast.8), custom_call_target="tpu_custom_call" | custom-call | flops 200000000 | bytes 1500000 | tf_op jit(solution)/shard_map/give_states/pallas_call | solution.py:155
  3.4 3.0 %collective-permute-start = (bf16[272,128]{1,0:T(8,128)(2,1)}, bf16[272,128]{1,0:T(8,128)(2,1)S(1)}, u32[]{:S(2)}, u32[]{:S(2)}) collective-permute-start(bf16[272,128]{1,0:T(8,128)(2,1)} %get-tuple-element.41), channel_id=1, source_target_pairs={{0,4},{4,0},{8,12},{12,8},{16,20},{20,16},{24,28},{28,24},{1,5},{5... | collective-permute-start | bytes 208904 | tf_op jit(solution)/shard_map/ppermute | solution.py:300
  6.4 1.6 %collective-permute-start.1 = (bf16[272,128]{1,0:T(8,128)(2,1)}, bf16[272,128]{1,0:T(8,128)(2,1)S(1)}, u32[]{:S(2)}, u32[]{:S(2)}) collective-permute-start(bf16[272,128]{1,0:T(8,128)(2,1)} %get-tuple-element.42), channel_id=1, source_target_pairs={{0,8},{4,12},{8,0},{12,4},{16,24},{20,28},{24,16},{28,20},{1,9},{5... | collective-permute-start | bytes 208904 | tf_op jit(solution)/shard_map/ppermute | solution.py:300
  8.0 0.8 %copy-done.3 = bf16[32,640]{1,0:T(8,128)(2,1)S(1)} copy-done((bf16[32,640]{1,0:T(8,128)(2,1)S(1)}, bf16[32,640]{1,0:T(8,128)(2,1)}, u32[]{:S(2)}) %copy-start.3) | copy-done | bytes 40984
  9.3 2.2 %collective-permute-done.1.come2 = bf16[272,128]{1,0:T(8,128)(2,1)S(1)} collective-permute-done((bf16[272,128]{1,0:T(8,128)(2,1)}, bf16[272,128]{1,0:T(8,128)(2,1)S(1)}, u32[]{:S(2)}, u32[]{:S(2)}) %collective-permute-start.1) | collective-permute-done | bytes 69664 | tf_op jit(solution)/shard_map/ppermute | solution.py:300
  11.5 1.9 %collective-permute-done.2.come3 = bf16[272,128]{1,0:T(8,128)(2,1)S(1)} collective-permute-done((bf16[272,128]{1,0:T(8,128)(2,1)}, bf16[272,128]{1,0:T(8,128)(2,1)S(1)}, u32[]{:S(2)}, u32[]{:S(2)}) %collective-permute-start.2) | collective-permute-done | bytes 69664 | tf_op jit(solution)/shard_map/ppermute | solution.py:300
  13.4 2.7 %collective-permute-start.3 = (bf16[272,128]{1,0:T(8,128)(2,1)S(1)}, bf16[272,128]{1,0:T(8,128)(2,1)S(1)}, u32[]{:S(2)}, u32[]{:S(2)}) collective-permute-start(bf16[272,128]{1,0:T(8,128)(2,1)S(1)} %join_states.1), channel_id=1, source_target_pairs={{0,16},{4,20},{8,24},{12,28},{16,0},{20,4},{24,8},{28,12},{1,17},{... | collective-permute-start | bytes 208904 | tf_op jit(solution)/shard_map/ppermute | solution.py:300
  16.1 3.2 %within_far.1 = (f32[256,1024]{1,0:T(8,128)S(1)}, f32[256,1024]{1,0:T(8,128)S(1)}) custom-call(f32[4,48,128]{2,1,0:T(8,128)S(1)} %copy-done.6, f32[512,1024]{1,0:T(8,128)S(1)} %copy-done, f32[512,128]{1,0:T(8,128)S(1)} %bitcast.10, f32[512,128]{1,0:T(8,128)S(1)} %bitcast.12, bf16[512,1024]{1,0:T(8,128)(2,1)S(1)} %copy-done.5, f32[1,16]{1,0:T(1,128)S(1)} %bitcast.18), custom_call_target="tpu_custom_call" | custom-call | flops 4000000000 | bytes 3000000 | tf_op jit(solution)/shard_map/within_far/pallas_call | solution.py:418
  20.3 0.8 %collective-permute-start.5 = (bf16[256,128]{1,0:T(8,128)(2,1)S(1)}, bf16[256,128]{1,0:T(8,128)(2,1)S(1)}, u32[]{:S(2)}, u32[]{:S(2)}) collective-permute-start(bf16[256,128]{1,0:T(8,128)(2,1)S(1)} %get-tuple-element.49), channel_id=1, source_target_pairs={{0,8},{4,12},{8,0},{12,4},{16,24},{20,28},{24,16},{28,20},{1,9},{5... | collective-permute-start | bytes 196616 | tf_op jit(solution)/shard_map/ppermute | solution.py:300
  21.1 2.1 %collective-permute-start.6 = (bf16[256,128]{1,0:T(8,128)(2,1)S(1)}, bf16[256,128]{1,0:T(8,128)(2,1)S(1)}, u32[]{:S(2)}, u32[]{:S(2)}) collective-permute-start(bf16[256,128]{1,0:T(8,128)(2,1)S(1)} %get-tuple-element.50), channel_id=1, source_target_pairs={{0,12},{4,8},{8,4},{12,0},{16,28},{20,24},{24,20},{28,16},{1,13},{... | collective-permute-start | bytes 196616 | tf_op jit(solution)/shard_map/ppermute | solution.py:300
  23.2 0.8 %collective-permute-done.4.q1 = bf16[256,128]{1,0:T(8,128)(2,1)S(1)} collective-permute-done((bf16[256,128]{1,0:T(8,128)(2,1)S(1)}, bf16[256,128]{1,0:T(8,128)(2,1)S(1)}, u32[]{:S(2)}, u32[]{:S(2)}) %collective-permute-start.4) | collective-permute-done | bytes 65568 | tf_op jit(solution)/shard_map/ppermute | solution.py:300
  24.6 1.7 %collective-permute-done.6.q3 = bf16[256,128]{1,0:T(8,128)(2,1)S(1)} collective-permute-done((bf16[256,128]{1,0:T(8,128)(2,1)S(1)}, bf16[256,128]{1,0:T(8,128)(2,1)S(1)}, u32[]{:S(2)}, u32[]{:S(2)}) %collective-permute-start.6) | collective-permute-done | bytes 65568 | tf_op jit(solution)/shard_map/ppermute | solution.py:300
  26.3 1.1 %finish_far.1 = (bf16[128,1024]{1,0:T(8,128)(2,1)S(1)}, f32[128,1024]{1,0:T(8,128)S(1)}, bf16[256,1024]{1,0:T(8,128)(2,1)S(1)}) custom-call(f32[256,1024]{1,0:T(8,128)S(1)} %get-tuple-element.44.own, f32[256,1024]{1,0:T(8,128)S(1)} %get-tuple-element.45.lead, f32[512,128]{1,0:T(8,128)S(1)} %bitcast.13, bf16[256,128]{1,0:T(8,128)(2,1)S(1)} %get-tuple-element.47.q0, ...), custom_call_target="tpu_custom_call" | custom-call | flops 536870912 | tf_op jit(solution)/shard_map/finish_far/pallas_call | solution.py:503
  27.4 1.2 %project_more.1 = (bf16[128,2048]{1,0:T(8,128)(2,1)S(1)}, f32[128,2048]{1,0:T(8,128)S(1)}) custom-call(bf16[256,1024]{1,0:T(8,128)(2,1)S(1)} %get-tuple-element.54.normed, bf16[1024,4096]{1,0:T(8,128)(2,1)S(1)} %bitcast.7), custom_call_target="tpu_custom_call" | custom-call | flops 1073741824 | tf_op jit(solution)/shard_map/project_more/pallas_call | solution.py:503
  29.3 1.6 %collective-permute-start.12 = (bf16[128,1024]{1,0:T(8,128)(2,1)S(1)}, bf16[128,1024]{1,0:T(8,128)(2,1)S(1)}, u32[]{:S(2)}, u32[]{:S(2)}) collective-permute-start(bf16[128,1024]{1,0:T(8,128)(2,1)S(1)} %add_pair.4), channel_id=1, source_target_pairs={{0,2},{1,3},{2,0},{3,1},{4,6},{5,7},{6,4},{7,5},{8,10},{9,11},{10,... | collective-permute-start | bytes 786440 | tf_op jit(solution)/shard_map/ppermute | solution.py:664
  30.9 3.2 %within_near.1 = (f32[256,1024]{1,0:T(8,128)S(1)}, f32[256,1024]{1,0:T(8,128)S(1)}) custom-call(f32[4,48,128]{2,1,0:T(8,128)S(1)} %copy-done.6, f32[512,1024]{1,0:T(8,128)S(1)} %copy-done, f32[512,128]{1,0:T(8,128)S(1)} %bitcast.11, f32[512,128]{1,0:T(8,128)S(1)} %bitcast.14, bf16[512,1024]{1,0:T(8,128)(2,1)S(1)} %copy-done.5, f32[1,16]{1,0:T(1,128)S(1)} %bitcast.19), custom_call_target="tpu_custom_call" | custom-call | flops 4000000000 | bytes 3000000 | tf_op jit(solution)/shard_map/within_near/pallas_call | solution.py:418
  34.8 2.2 %finish_near.1 = (bf16[128,5120]{1,0:T(8,128)(2,1)S(1)}, f32[128,1024]{1,0:T(8,128)S(1)}, bf16[128,1024]{1,0:T(8,128)(2,1)S(1)}) custom-call(bf16[256,1024]{1,0:T(8,128)(2,1)S(1)} %get-tuple-element.54.normed, f32[256,1024]{1,0:T(8,128)S(1)} %get-tuple-element.58.own, f32[256,1024]{1,0:T(8,128)S(1)} %get-tuple-element.59.lead, f32[512,128]{1,0:T(8,128)S(1)} %bitcast.15, ...), custom_call_target="tpu_custom_call" | custom-call | flops 1610612736 | tf_op jit(solution)/shard_map/finish_near/pallas_call | solution.py:503
  37.1 1.4 %collective-permute-done.12.refs_0_ = bf16[128,1024]{1,0:T(8,128)(2,1)S(1)} collective-permute-done((bf16[128,1024]{1,0:T(8,128)(2,1)S(1)}, bf16[128,1024]{1,0:T(8,128)(2,1)S(1)}, u32[]{:S(2)}, u32[]{:S(2)}) %collective-permute-start.12) | collective-permute-done | bytes 262176 | tf_op jit(solution)/shard_map/ppermute | solution.py:664
  38.6 1.6 %collective-permute-done.9.come = bf16[128,5120]{1,0:T(8,128)(2,1)S(1)} collective-permute-done((bf16[128,5120]{1,0:T(8,128)(2,1)S(1)}, bf16[128,5120]{1,0:T(8,128)(2,1)S(1)}, u32[]{:S(2)}, u32[]{:S(2)}) %collective-permute-start.9) | collective-permute-done | bytes 1310752 | tf_op jit(solution)/shard_map/ppermute | solution.py:625
  40.2 1.6 %collective-permute-start.10 = (bf16[128,1024]{1,0:T(8,128)(2,1)S(1)}, bf16[128,1024]{1,0:T(8,128)(2,1)S(1)}, u32[]{:S(2)}, u32[]{:S(2)}) collective-permute-start(bf16[128,1024]{1,0:T(8,128)(2,1)S(1)} %add_pair.5), channel_id=1, source_target_pairs={{0,2},{1,3},{2,0},{3,1},{4,6},{5,7},{6,4},{7,5},{8,10},{9,11},{10,... | collective-permute-start | bytes 786440 | tf_op jit(solution)/shard_map/ppermute | solution.py:667
  41.8 8.0 %collective-permute-done.11.refs_0_ = bf16[128,2048]{1,0:T(8,128)(2,1)S(1)} collective-permute-done((bf16[128,2048]{1,0:T(8,128)(2,1)S(1)}, bf16[128,2048]{1,0:T(8,128)(2,1)S(1)}, u32[]{:S(2)}, u32[]{:S(2)}) %collective-permute-start.11) | collective-permute-done | bytes 524320 | tf_op jit(solution)/shard_map/ppermute | solution.py:665
  49.8 1.3 %project_kept.1.kept = f32[128,4096]{1,0:T(8,128)S(1)} custom-call(bf16[128,1024]{1,0:T(8,128)(2,1)S(1)} %get-tuple-element.60.kept, bf16[128,5120]{1,0:T(8,128)(2,1)S(1)} %collective-permute-done.9.come, bf16[1024,4096]{1,0:T(8,128)(2,1)S(1)} %bitcast.7), custom_call_target="tpu_custom_call" | custom-call | flops 1073741824 | tf_op jit(solution)/shard_map/project_kept/pallas_call | solution.py:503
  51.1 1.0 %early_sums.1.refs_1_ = bf16[128,4096]{1,0:T(8,128)(2,1)} custom-call(f32[128,4096]{1,0:T(8,128)S(1)} %project_kept.1.kept, bf16[128,1024]{1,0:T(8,128)(2,1)S(1)} %get-tuple-element.65.first, bf16[128,2048]{1,0:T(8,128)(2,1)S(1)} %get-tuple-element.66.second), custom_call_target="tpu_custom_call" | custom-call | tf_op jit(solution)/shard_map/early_sums/pallas_call | solution.py:546
  52.2 2.3 %collective-permute-done.10.refs_0_ = bf16[128,1024]{1,0:T(8,128)(2,1)S(1)} collective-permute-done((bf16[128,1024]{1,0:T(8,128)(2,1)S(1)}, bf16[128,1024]{1,0:T(8,128)(2,1)S(1)}, u32[]{:S(2)}, u32[]{:S(2)}) %collective-permute-start.10) | collective-permute-done | bytes 262176 | tf_op jit(solution)/shard_map/ppermute | solution.py:667
  (41 shorter events, 4.5 us)
Async XLA Ops:
  0.0 8.0 %copy-start = (f32[512,1024]{1,0:T(8,128)S(1)}, f32[512,1024]{1,0:T(8,128)}, u32[]{:S(2)}) copy-start(f32[512,1024]{1,0:T(8,128)} %x_ref.3) | copy-start | bytes 6291460
  0.0 8.0 %copy-start.1 = (f32[512,1,128]{2,1,0:T(1,128)S(1)}, f32[512,1,128]{2,1,0:T(1,128)}, u32[]{:S(2)}) copy-start(f32[512,1,128]{2,1,0:T(1,128)} %param.13) | copy-start | bytes 786436
  0.0 16.1 %copy-start.7 = (f32[16]{0:T(128)S(1)}, f32[16]{0:T(128)}, u32[]{:S(2)}) copy-start(f32[16]{0:T(128)} %param.15) | copy-start | bytes 196
  3.3 12.8 %copy-start.2 = (f32[512,1,128]{2,1,0:T(1,128)S(1)}, f32[512,1,128]{2,1,0:T(1,128)}, u32[]{:S(2)}) copy-start(f32[512,1,128]{2,1,0:T(1,128)} %param.14) | copy-start | bytes 786436
  3.4 6.0 %collective-permute-start = (bf16[272,128]{1,0:T(8,128)(2,1)}, bf16[272,128]{1,0:T(8,128)(2,1)S(1)}, u32[]{:S(2)}, u32[]{:S(2)}) collective-permute-start(bf16[272,128]{1,0:T(8,128)(2,1)} %get-tuple-element.41), channel_id=1, source_target_pairs={{0,4},{4,0},{8,12},{12,8},{16,20},{20,16},{24,28},{28,24},{1,5},{5... | collective-permute-start | bytes 208904 | tf_op jit(solution)/shard_map/ppermute | solution.py:300
  6.4 5.1 %collective-permute-start.1 = (bf16[272,128]{1,0:T(8,128)(2,1)}, bf16[272,128]{1,0:T(8,128)(2,1)S(1)}, u32[]{:S(2)}, u32[]{:S(2)}) collective-permute-start(bf16[272,128]{1,0:T(8,128)(2,1)} %get-tuple-element.42), channel_id=1, source_target_pairs={{0,8},{4,12},{8,0},{12,4},{16,24},{20,28},{24,16},{28,20},{1,9},{5... | collective-permute-start | bytes 208904 | tf_op jit(solution)/shard_map/ppermute | solution.py:300
  7.9 5.4 %collective-permute-start.2 = (bf16[272,128]{1,0:T(8,128)(2,1)}, bf16[272,128]{1,0:T(8,128)(2,1)S(1)}, u32[]{:S(2)}, u32[]{:S(2)}) collective-permute-start(bf16[272,128]{1,0:T(8,128)(2,1)} %get-tuple-element.43), channel_id=1, source_target_pairs={{0,12},{4,8},{8,4},{12,0},{16,28},{20,24},{24,20},{28,16},{1,13},{... | collective-permute-start | bytes 208904 | tf_op jit(solution)/shard_map/ppermute | solution.py:300
  8.0 0.8 %copy-start.3 = (bf16[32,640]{1,0:T(8,128)(2,1)S(1)}, bf16[32,640]{1,0:T(8,128)(2,1)}, u32[]{:S(2)}) copy-start(bf16[32,640]{1,0:T(8,128)(2,1)} %get-tuple-element.40.wk) | copy-start | bytes 122884
  8.7 7.4 %copy-start.5 = (bf16[512,1024]{1,0:T(8,128)(2,1)S(1)}, bf16[512,1024]{1,0:T(8,128)(2,1)}, u32[]{:S(2)}) copy-start(bf16[512,1024]{1,0:T(8,128)(2,1)} %gate_ref.3) | copy-start | bytes 3145732
  8.7 7.4 %copy-start.6 = (f32[4,48,128]{2,1,0:T(8,128)S(1)}, f32[4,48,128]{2,1,0:T(8,128)}, u32[]{:S(2)}) copy-start(f32[4,48,128]{2,1,0:T(8,128)} %get-tuple-element.57.aux) | copy-start | bytes 294916
  13.4 5.9 %collective-permute-start.3 = (bf16[272,128]{1,0:T(8,128)(2,1)S(1)}, bf16[272,128]{1,0:T(8,128)(2,1)S(1)}, u32[]{:S(2)}, u32[]{:S(2)}) collective-permute-start(bf16[272,128]{1,0:T(8,128)(2,1)S(1)} %join_states.1), channel_id=1, source_target_pairs={{0,16},{4,20},{8,24},{12,28},{16,0},{20,4},{24,8},{28,12},{1,17},{... | collective-permute-start | bytes 208904 | tf_op jit(solution)/shard_map/ppermute | solution.py:300
  16.1 10.1 %slice-start = ((s8[8388608]{0:T(1024)(128)(4,1)}), s8[4194304]{0:T(1024)(128)(4,1)S(1)}, s32[]{:S(2)}) async-start(s8[8388608]{0:T(1024)(128)(4,1)} %bitcast.6), calls=%async_computation | async-start | bytes 8388608
  16.1 10.1 %slice-start.1 = ((s8[8388608]{0:T(1024)(128)(4,1)}), s8[4194304]{0:T(1024)(128)(4,1)S(1)}, s32[]{:S(2)}) async-start(s8[8388608]{0:T(1024)(128)(4,1)} %bitcast.6), calls=%async_computation.1 | async-start | bytes 8388608
  16.1 10.1 %copy-start.4 = (f32[1024]{0:T(1024)S(1)}, f32[1024]{0:T(1024)}, u32[]{:S(2)}) copy-start(f32[1024]{0:T(1024)} %param.16) | copy-start | bytes 12292
  19.6 4.3 %collective-permute-start.4 = (bf16[256,128]{1,0:T(8,128)(2,1)S(1)}, bf16[256,128]{1,0:T(8,128)(2,1)S(1)}, u32[]{:S(2)}, u32[]{:S(2)}) collective-permute-start(bf16[256,128]{1,0:T(8,128)(2,1)S(1)} %get-tuple-element.48), channel_id=1, source_target_pairs={{0,4},{4,0},{8,12},{12,8},{16,20},{20,16},{24,28},{28,24},{1,5},{5... | collective-permute-start | bytes 196616 | tf_op jit(solution)/shard_map/ppermute | solution.py:300
  20.3 4.3 %collective-permute-start.5 = (bf16[256,128]{1,0:T(8,128)(2,1)S(1)}, bf16[256,128]{1,0:T(8,128)(2,1)S(1)}, u32[]{:S(2)}, u32[]{:S(2)}) collective-permute-start(bf16[256,128]{1,0:T(8,128)(2,1)S(1)} %get-tuple-element.49), channel_id=1, source_target_pairs={{0,8},{4,12},{8,0},{12,4},{16,24},{20,28},{24,16},{28,20},{1,9},{5... | collective-permute-start | bytes 196616 | tf_op jit(solution)/shard_map/ppermute | solution.py:300
  21.1 5.2 %collective-permute-start.6 = (bf16[256,128]{1,0:T(8,128)(2,1)S(1)}, bf16[256,128]{1,0:T(8,128)(2,1)S(1)}, u32[]{:S(2)}, u32[]{:S(2)}) collective-permute-start(bf16[256,128]{1,0:T(8,128)(2,1)S(1)} %get-tuple-element.50), channel_id=1, source_target_pairs={{0,12},{4,8},{8,4},{12,0},{16,28},{20,24},{24,20},{28,16},{1,13},{... | collective-permute-start | bytes 196616 | tf_op jit(solution)/shard_map/ppermute | solution.py:300
  27.4 1.9 %collective-permute-start.8 = (bf16[128,1024]{1,0:T(8,128)(2,1)S(1)}, bf16[128,1024]{1,0:T(8,128)(2,1)S(1)}, u32[]{:S(2)}, u32[]{:S(2)}) collective-permute-start(bf16[128,1024]{1,0:T(8,128)(2,1)S(1)} %get-tuple-element.56), channel_id=1, source_target_pairs={{0,1},{1,0},{2,3},{3,2},{4,5},{5,4},{6,7},{7,6},{8,9},{9,8},{10,11... | collective-permute-start | bytes 786440 | tf_op jit(solution)/shard_map/ppermute | solution.py:625
  28.7 5.4 %collective-permute-start.7 = (bf16[128,2048]{1,0:T(8,128)(2,1)S(1)}, bf16[128,2048]{1,0:T(8,128)(2,1)S(1)}, u32[]{:S(2)}, u32[]{:S(2)}) collective-permute-start(bf16[128,2048]{1,0:T(8,128)(2,1)S(1)} %get-tuple-element.53), channel_id=1, source_target_pairs={{0,1},{1,0},{2,3},{3,2},{4,5},{5,4},{6,7},{7,6},{8,9},{9,8},{10,11... | collective-permute-start | bytes 1572872 | tf_op jit(solution)/shard_map/ppermute | solution.py:625
  29.3 9.2 %collective-permute-start.12 = (bf16[128,1024]{1,0:T(8,128)(2,1)S(1)}, bf16[128,1024]{1,0:T(8,128)(2,1)S(1)}, u32[]{:S(2)}, u32[]{:S(2)}) collective-permute-start(bf16[128,1024]{1,0:T(8,128)(2,1)S(1)} %add_pair.4), channel_id=1, source_target_pairs={{0,2},{1,3},{2,0},{3,1},{4,6},{5,7},{6,4},{7,5},{8,10},{9,11},{10,... | collective-permute-start | bytes 786440 | tf_op jit(solution)/shard_map/ppermute | solution.py:664
  34.3 15.5 %collective-permute-start.11 = (bf16[128,2048]{1,0:T(8,128)(2,1)S(1)}, bf16[128,2048]{1,0:T(8,128)(2,1)S(1)}, u32[]{:S(2)}, u32[]{:S(2)}) collective-permute-start(bf16[128,2048]{1,0:T(8,128)(2,1)S(1)} %add_pair.3), channel_id=1, source_target_pairs={{0,2},{1,3},{2,0},{3,1},{4,6},{5,7},{6,4},{7,5},{8,10},{9,11},{10,... | collective-permute-start | bytes 1572872 | tf_op jit(solution)/shard_map/ppermute | solution.py:665
  37.0 3.1 %collective-permute-start.9 = (bf16[128,5120]{1,0:T(8,128)(2,1)S(1)}, bf16[128,5120]{1,0:T(8,128)(2,1)S(1)}, u32[]{:S(2)}, u32[]{:S(2)}) collective-permute-start(bf16[128,5120]{1,0:T(8,128)(2,1)S(1)} %get-tuple-element.61), channel_id=1, source_target_pairs={{0,1},{1,0},{2,3},{3,2},{4,5},{5,4},{6,7},{7,6},{8,9},{9,8},{10,11... | collective-permute-start | bytes 3932168 | tf_op jit(solution)/shard_map/ppermute | solution.py:625
  40.2 14.3 %collective-permute-start.10 = (bf16[128,1024]{1,0:T(8,128)(2,1)S(1)}, bf16[128,1024]{1,0:T(8,128)(2,1)S(1)}, u32[]{:S(2)}, u32[]{:S(2)}) collective-permute-start(bf16[128,1024]{1,0:T(8,128)(2,1)S(1)} %add_pair.5), channel_id=1, source_target_pairs={{0,2},{1,3},{2,0},{3,1},{4,6},{5,7},{6,4},{7,5},{8,10},{9,11},{10,... | collective-permute-start | bytes 786440 | tf_op jit(solution)/shard_map/ppermute | solution.py:667

commit v9 on v4

--- a/solution.py
+++ b/solution.py
@@ -127,11 +127,11 @@
     loads[0].wait()
     loads[1].wait()
     step_vectors(raw_v[...], rate_v[...], wk, aux)
-    for load in loads[2:]:
-        load.wait()
+    loads[2].wait()
     b16 = b_v[...].astype(BF)
     heads = x_v.shape[2] // P_SIZE
     for k, msg in ((1, msg1), (2, msg2), (3, msg3)):
+        loads[2 + k].wait()
         quarter_message(x_v[k - 1], b16, wk, (mine ^ k) * heads, msg)
 
 
@@ -363,7 +363,10 @@
         lines.append(pre)
         before = before + pre[:, CHUNK - 1:]
         b, c = rows_of(b_ref, block), rows_of(c_ref, block)
-        raw = dot(c, b, ((1,), (1,)), lax.Precision.HIGHEST)
+        (ch, cl), (bh, bl) = split2(c), split2(b)
+        raw = dot(
+            jnp.concatenate([ch, ch, cl], axis=1), jnp.concatenate([bh, bl, bh], axis=1), ((1,), (1,))
+        )
         scores.append(jnp.where(r >= l, raw, 0.0))
         rows_b.append(b.astype(BF))
         rows_c.append(c.astype(BF))

time: 55.4 us -> 55.3 us (level)
  transfers between devices with their start and end apart: 13 -> 13, of which waited for: 9 -> 10; matrix products, arithmetic and copies ran while one was open for 0% -> 0% of each run, Pallas kernels for 23% -> 23%
where the time goes in v9:
time: 55.3 us; the launch traced here: 55.1 us
  waiting for transfers between devices  20.6 us (37%)
  Pallas kernels  18.1 us (33%)
  starting transfers between devices  15.2 us (27%)
  local copies, waits for them, and re-layouts  0.81 us (1%)
    ppermute x7, starting transfers between devices, exchange(): return lax.ppermute(value, 'seq', [(s, s ^ distance) for s in range(count)])  10.8 us
    ppermute x7, waiting for transfers between devices, exchange(): return lax.ppermute(value, 'seq', [(s, s ^ distance) for s in range(count)])  7.13 us
    pallas_call x7, Pallas kernels, local_call(): pl.pallas_call(kernel, in_specs=[VMEM] * len(operands), out_specs=[VMEM]...  6.08 us
    pallas_call x2, Pallas kernels, within(): pl.pallas_call(functools.partial(within_kernel, far), in_specs=[VMEM] * 6...  6.03 us
    ppermute x1, waiting for transfers between devices, per_device(): third, filled = await_piece(lax.ppermute(third, 'head', far), filled)  5.29 us
    ppermute x1, waiting for transfers between devices, per_device(): second, first = await_piece(lax.ppermute(second, 'head', far), first)  4.95 us
    pallas_call x1, Pallas kernels, give_states(): pl.pallas_call(give_kernel, in_specs=[HBM] * 4, out_shape=[jax.ShapeDtype...  3.36 us
    ppermute x3, waiting for transfers between devices, add(): come = lax.ppermute(theirs, 'head', near)  1.81 us
  transfers between devices with their start and end apart: 13, of which 10 were waited for; matrix products, arithmetic and copies ran while one was open for 0% of the time, Pallas kernels for 23%

profile of v9, /device:TPU:0, one launch (start us, length us, event | category | flops | bytes accessed | tf_op | source)
XLA Modules:
  0.0 55.1 jit_solution(3867617520189161557)
XLA Ops:
  0.0 3.4 %give_states.1 = (bf16[272,128]{1,0:T(8,128)(2,1)}, bf16[272,128]{1,0:T(8,128)(2,1)}, bf16[272,128]{1,0:T(8,128)(2,1)}, bf16[32,640]{1,0:T(8,128)(2,1)}, f32[4,48,128]{2,1,0:T(8,128)}) custom-call(f32[16,512]{1,0:T(8,128)} %bitcast.20, f32[1,16]{1,0:T(1,128)} %bitcast.21, f32[512,1024]{1,0:T(8,128)} %x_ref.3, f32[512,128]{1,0:T(8,128)} %bitcast.8), custom_call_target="tpu_custom_call" | custom-call | flops 200000000 | bytes 1500000 | tf_op jit(solution)/shard_map/give_states/pallas_call | solution.py:155
  3.4 3.0 %collective-permute-start = (bf16[272,128]{1,0:T(8,128)(2,1)}, bf16[272,128]{1,0:T(8,128)(2,1)S(1)}, u32[]{:S(2)}, u32[]{:S(2)}) collective-permute-start(bf16[272,128]{1,0:T(8,128)(2,1)} %get-tuple-element.41), channel_id=1, source_target_pairs={{0,4},{4,0},{8,12},{12,8},{16,20},{20,16},{24,28},{28,24},{1,5},{5... | collective-permute-start | bytes 208904 | tf_op jit(solution)/shard_map/ppermute | solution.py:300
  6.4 1.6 %collective-permute-start.1 = (bf16[272,128]{1,0:T(8,128)(2,1)}, bf16[272,128]{1,0:T(8,128)(2,1)S(1)}, u32[]{:S(2)}, u32[]{:S(2)}) collective-permute-start(bf16[272,128]{1,0:T(8,128)(2,1)} %get-tuple-element.42), channel_id=1, source_target_pairs={{0,8},{4,12},{8,0},{12,4},{16,24},{20,28},{24,16},{28,20},{1,9},{5... | collective-permute-start | bytes 208904 | tf_op jit(solution)/shard_map/ppermute | solution.py:300
  8.0 0.8 %copy-done.3 = bf16[32,640]{1,0:T(8,128)(2,1)S(1)} copy-done((bf16[32,640]{1,0:T(8,128)(2,1)S(1)}, bf16[32,640]{1,0:T(8,128)(2,1)}, u32[]{:S(2)}) %copy-start.3) | copy-done | bytes 40984
  9.4 2.1 %collective-permute-done.1.come2 = bf16[272,128]{1,0:T(8,128)(2,1)S(1)} collective-permute-done((bf16[272,128]{1,0:T(8,128)(2,1)}, bf16[272,128]{1,0:T(8,128)(2,1)S(1)}, u32[]{:S(2)}, u32[]{:S(2)}) %collective-permute-start.1) | collective-permute-done | bytes 69664 | tf_op jit(solution)/shard_map/ppermute | solution.py:300
  11.5 1.9 %collective-permute-done.2.come3 = bf16[272,128]{1,0:T(8,128)(2,1)S(1)} collective-permute-done((bf16[272,128]{1,0:T(8,128)(2,1)}, bf16[272,128]{1,0:T(8,128)(2,1)S(1)}, u32[]{:S(2)}, u32[]{:S(2)}) %collective-permute-start.2) | collective-permute-done | bytes 69664 | tf_op jit(solution)/shard_map/ppermute | solution.py:300
  13.5 2.7 %collective-permute-start.3 = (bf16[272,128]{1,0:T(8,128)(2,1)S(1)}, bf16[272,128]{1,0:T(8,128)(2,1)S(1)}, u32[]{:S(2)}, u32[]{:S(2)}) collective-permute-start(bf16[272,128]{1,0:T(8,128)(2,1)S(1)} %join_states.1), channel_id=1, source_target_pairs={{0,16},{4,20},{8,24},{12,28},{16,0},{20,4},{24,8},{28,12},{1,17},{... | collective-permute-start | bytes 208904 | tf_op jit(solution)/shard_map/ppermute | solution.py:300
  16.2 3.0 %within_far.1 = (f32[256,1024]{1,0:T(8,128)S(1)}, f32[256,1024]{1,0:T(8,128)S(1)}) custom-call(f32[4,48,128]{2,1,0:T(8,128)S(1)} %copy-done.6, f32[512,1024]{1,0:T(8,128)S(1)} %copy-done, f32[512,128]{1,0:T(8,128)S(1)} %bitcast.10, f32[512,128]{1,0:T(8,128)S(1)} %bitcast.12, bf16[512,1024]{1,0:T(8,128)(2,1)S(1)} %copy-done.5, f32[1,16]{1,0:T(1,128)S(1)} %bitcast.18), custom_call_target="tpu_custom_call" | custom-call | flops 4000000000 | bytes 3000000 | tf_op jit(solution)/shard_map/within_far/pallas_call | solution.py:421
  20.9 2.3 %collective-permute-start.6 = (bf16[256,128]{1,0:T(8,128)(2,1)S(1)}, bf16[256,128]{1,0:T(8,128)(2,1)S(1)}, u32[]{:S(2)}, u32[]{:S(2)}) collective-permute-start(bf16[256,128]{1,0:T(8,128)(2,1)S(1)} %get-tuple-element.50), channel_id=1, source_target_pairs={{0,12},{4,8},{8,4},{12,0},{16,28},{20,24},{24,20},{28,16},{1,13},{... | collective-permute-start | bytes 196616 | tf_op jit(solution)/shard_map/ppermute | solution.py:300
  23.2 0.8 %collective-permute-done.4.q1 = bf16[256,128]{1,0:T(8,128)(2,1)S(1)} collective-permute-done((bf16[256,128]{1,0:T(8,128)(2,1)S(1)}, bf16[256,128]{1,0:T(8,128)(2,1)S(1)}, u32[]{:S(2)}, u32[]{:S(2)}) %collective-permute-start.4) | collective-permute-done | bytes 65568 | tf_op jit(solution)/shard_map/ppermute | solution.py:300
  24.6 1.5 %collective-permute-done.6.q3 = bf16[256,128]{1,0:T(8,128)(2,1)S(1)} collective-permute-done((bf16[256,128]{1,0:T(8,128)(2,1)S(1)}, bf16[256,128]{1,0:T(8,128)(2,1)S(1)}, u32[]{:S(2)}, u32[]{:S(2)}) %collective-permute-start.6) | collective-permute-done | bytes 65568 | tf_op jit(solution)/shard_map/ppermute | solution.py:300
  26.1 1.1 %finish_far.1 = (bf16[128,1024]{1,0:T(8,128)(2,1)S(1)}, f32[128,1024]{1,0:T(8,128)S(1)}, bf16[256,1024]{1,0:T(8,128)(2,1)S(1)}) custom-call(f32[256,1024]{1,0:T(8,128)S(1)} %get-tuple-element.44.own, f32[256,1024]{1,0:T(8,128)S(1)} %get-tuple-element.45.lead, f32[512,128]{1,0:T(8,128)S(1)} %bitcast.13, bf16[256,128]{1,0:T(8,128)(2,1)S(1)} %get-tuple-element.47.q0, ...), custom_call_target="tpu_custom_call" | custom-call | flops 536870912 | tf_op jit(solution)/shard_map/finish_far/pallas_call | solution.py:506
  27.3 1.0 %project_more.1 = (bf16[128,1536]{1,0:T(8,128)(2,1)S(1)}, f32[128,1536]{1,0:T(8,128)S(1)}) custom-call(bf16[256,1024]{1,0:T(8,128)(2,1)S(1)} %get-tuple-element.54.normed, bf16[1024,4096]{1,0:T(8,128)(2,1)S(1)} %bitcast.7), custom_call_target="tpu_custom_call" | custom-call | flops 805306368 | tf_op jit(solution)/shard_map/project_more/pallas_call | solution.py:506
  28.9 1.6 %collective-permute-start.12 = (bf16[128,1024]{1,0:T(8,128)(2,1)S(1)}, bf16[128,1024]{1,0:T(8,128)(2,1)S(1)}, u32[]{:S(2)}, u32[]{:S(2)}) collective-permute-start(bf16[128,1024]{1,0:T(8,128)(2,1)S(1)} %add_pair.4), channel_id=1, source_target_pairs={{0,2},{1,3},{2,0},{3,1},{4,6},{5,7},{6,4},{7,5},{8,10},{9,11},{10,... | collective-permute-start | bytes 786440 | tf_op jit(solution)/shard_map/ppermute | solution.py:667
  30.5 3.0 %within_near.1 = (f32[256,1024]{1,0:T(8,128)S(1)}, f32[256,1024]{1,0:T(8,128)S(1)}) custom-call(f32[4,48,128]{2,1,0:T(8,128)S(1)} %copy-done.6, f32[512,1024]{1,0:T(8,128)S(1)} %copy-done, f32[512,128]{1,0:T(8,128)S(1)} %bitcast.11, f32[512,128]{1,0:T(8,128)S(1)} %bitcast.14, bf16[512,1024]{1,0:T(8,128)(2,1)S(1)} %copy-done.5, f32[1,16]{1,0:T(1,128)S(1)} %bitcast.19), custom_call_target="tpu_custom_call" | custom-call | flops 4000000000 | bytes 3000000 | tf_op jit(solution)/shard_map/within_near/pallas_call | solution.py:421
  34.2 2.5 %finish_near.1 = (bf16[128,5632]{1,0:T(8,128)(2,1)S(1)}, f32[128,1536]{1,0:T(8,128)S(1)}, bf16[128,1024]{1,0:T(8,128)(2,1)S(1)}) custom-call(bf16[256,1024]{1,0:T(8,128)(2,1)S(1)} %get-tuple-element.54.normed, f32[256,1024]{1,0:T(8,128)S(1)} %get-tuple-element.58.own, f32[256,1024]{1,0:T(8,128)S(1)} %get-tuple-element.59.lead, f32[512,128]{1,0:T(8,128)S(1)} %bitcast.15, ...), custom_call_target="tpu_custom_call" | custom-call | flops 1879048192 | tf_op jit(solution)/shard_map/finish_near/pallas_call | solution.py:506
  36.8 1.4 %collective-permute-done.12.refs_0_ = bf16[128,1024]{1,0:T(8,128)(2,1)S(1)} collective-permute-done((bf16[128,1024]{1,0:T(8,128)(2,1)S(1)}, bf16[128,1024]{1,0:T(8,128)(2,1)S(1)}, u32[]{:S(2)}, u32[]{:S(2)}) %collective-permute-start.12) | collective-permute-done | bytes 262176 | tf_op jit(solution)/shard_map/ppermute | solution.py:667
  38.2 1.8 %collective-permute-done.9.come = bf16[128,5632]{1,0:T(8,128)(2,1)S(1)} collective-permute-done((bf16[128,5632]{1,0:T(8,128)(2,1)S(1)}, bf16[128,5632]{1,0:T(8,128)(2,1)S(1)}, u32[]{:S(2)}, u32[]{:S(2)}) %collective-permute-start.9) | collective-permute-done | bytes 1441824 | tf_op jit(solution)/shard_map/ppermute | solution.py:628
  40.0 1.6 %collective-permute-start.10 = (bf16[128,1536]{1,0:T(8,128)(2,1)S(1)}, bf16[128,1536]{1,0:T(8,128)(2,1)S(1)}, u32[]{:S(2)}, u32[]{:S(2)}) collective-permute-start(bf16[128,1536]{1,0:T(8,128)(2,1)S(1)} %add_pair.5), channel_id=1, source_target_pairs={{0,2},{1,3},{2,0},{3,1},{4,6},{5,7},{6,4},{7,5},{8,10},{9,11},{10,... | collective-permute-start | bytes 1179656 | tf_op jit(solution)/shard_map/ppermute | solution.py:670
  41.6 5.0 %collective-permute-done.11.refs_0_ = bf16[128,1536]{1,0:T(8,128)(2,1)S(1)} collective-permute-done((bf16[128,1536]{1,0:T(8,128)(2,1)S(1)}, bf16[128,1536]{1,0:T(8,128)(2,1)S(1)}, u32[]{:S(2)}, u32[]{:S(2)}) %collective-permute-start.11) | collective-permute-done | bytes 393248 | tf_op jit(solution)/shard_map/ppermute | solution.py:668
  46.6 1.3 %project_kept.1.kept = f32[128,4096]{1,0:T(8,128)S(1)} custom-call(bf16[128,1024]{1,0:T(8,128)(2,1)S(1)} %get-tuple-element.60.kept, bf16[128,5632]{1,0:T(8,128)(2,1)S(1)} %collective-permute-done.9.come, bf16[1024,4096]{1,0:T(8,128)(2,1)S(1)} %bitcast.7), custom_call_target="tpu_custom_call" | custom-call | flops 1073741824 | tf_op jit(solution)/shard_map/project_kept/pallas_call | solution.py:506
  47.9 1.0 %early_sums.1.refs_1_ = bf16[128,4096]{1,0:T(8,128)(2,1)} custom-call(f32[128,4096]{1,0:T(8,128)S(1)} %project_kept.1.kept, bf16[128,1024]{1,0:T(8,128)(2,1)S(1)} %get-tuple-element.65.first, bf16[128,1536]{1,0:T(8,128)(2,1)S(1)} %get-tuple-element.66.second), custom_call_target="tpu_custom_call" | custom-call | tf_op jit(solution)/shard_map/early_sums/pallas_call | solution.py:549
  48.9 5.3 %collective-permute-done.10.refs_0_ = bf16[128,1536]{1,0:T(8,128)(2,1)S(1)} collective-permute-done((bf16[128,1536]{1,0:T(8,128)(2,1)S(1)}, bf16[128,1536]{1,0:T(8,128)(2,1)S(1)}, u32[]{:S(2)}, u32[]{:S(2)}) %collective-permute-start.10) | collective-permute-done | bytes 393248 | tf_op jit(solution)/shard_map/ppermute | solution.py:670
  54.2 0.8 %last_sums.1 = bf16[128,4096]{1,0:T(8,128)(2,1)} custom-call(f32[128,4096]{1,0:T(8,128)S(1)} %project_kept.1.kept, bf16[128,1536]{1,0:T(8,128)(2,1)S(1)} %get-tuple-element.67.third, bf16[128,4096]{1,0:T(8,128)(2,1)} %get-tuple-element.68.filled), custom_call_target="tpu_custom_call", output_to_operand_aliasing={{}: (2, {})} | custom-call | tf_op jit(solution)/shard_map/last_sums/pallas_call | solution.py:581
  (41 shorter events, 4.6 us)
Async XLA Ops:
  0.0 8.0 %copy-start = (f32[512,1024]{1,0:T(8,128)S(1)}, f32[512,1024]{1,0:T(8,128)}, u32[]{:S(2)}) copy-start(f32[512,1024]{1,0:T(8,128)} %x_ref.3) | copy-start | bytes 6291460
  0.0 8.0 %copy-start.1 = (f32[512,1,128]{2,1,0:T(1,128)S(1)}, f32[512,1,128]{2,1,0:T(1,128)}, u32[]{:S(2)}) copy-start(f32[512,1,128]{2,1,0:T(1,128)} %param.13) | copy-start | bytes 786436
  0.0 16.1 %copy-start.7 = (f32[16]{0:T(128)S(1)}, f32[16]{0:T(128)}, u32[]{:S(2)}) copy-start(f32[16]{0:T(128)} %param.15) | copy-start | bytes 196
  3.4 12.8 %copy-start.2 = (f32[512,1,128]{2,1,0:T(1,128)S(1)}, f32[512,1,128]{2,1,0:T(1,128)}, u32[]{:S(2)}) copy-start(f32[512,1,128]{2,1,0:T(1,128)} %param.14) | copy-start | bytes 786436
  3.4 6.0 %collective-permute-start = (bf16[272,128]{1,0:T(8,128)(2,1)}, bf16[272,128]{1,0:T(8,128)(2,1)S(1)}, u32[]{:S(2)}, u32[]{:S(2)}) collective-permute-start(bf16[272,128]{1,0:T(8,128)(2,1)} %get-tuple-element.41), channel_id=1, source_target_pairs={{0,4},{4,0},{8,12},{12,8},{16,20},{20,16},{24,28},{28,24},{1,5},{5... | collective-permute-start | bytes 208904 | tf_op jit(solution)/shard_map/ppermute | solution.py:300
  6.4 5.1 %collective-permute-start.1 = (bf16[272,128]{1,0:T(8,128)(2,1)}, bf16[272,128]{1,0:T(8,128)(2,1)S(1)}, u32[]{:S(2)}, u32[]{:S(2)}) collective-permute-start(bf16[272,128]{1,0:T(8,128)(2,1)} %get-tuple-element.42), channel_id=1, source_target_pairs={{0,8},{4,12},{8,0},{12,4},{16,24},{20,28},{24,16},{28,20},{1,9},{5... | collective-permute-start | bytes 208904 | tf_op jit(solution)/shard_map/ppermute | solution.py:300
  8.0 5.4 %collective-permute-start.2 = (bf16[272,128]{1,0:T(8,128)(2,1)}, bf16[272,128]{1,0:T(8,128)(2,1)S(1)}, u32[]{:S(2)}, u32[]{:S(2)}) collective-permute-start(bf16[272,128]{1,0:T(8,128)(2,1)} %get-tuple-element.43), channel_id=1, source_target_pairs={{0,12},{4,8},{8,4},{12,0},{16,28},{20,24},{24,20},{28,16},{1,13},{... | collective-permute-start | bytes 208904 | tf_op jit(solution)/shard_map/ppermute | solution.py:300
  8.0 0.8 %copy-start.3 = (bf16[32,640]{1,0:T(8,128)(2,1)S(1)}, bf16[32,640]{1,0:T(8,128)(2,1)}, u32[]{:S(2)}) copy-start(bf16[32,640]{1,0:T(8,128)(2,1)} %get-tuple-element.40.wk) | copy-start | bytes 122884
  8.8 7.4 %copy-start.5 = (bf16[512,1024]{1,0:T(8,128)(2,1)S(1)}, bf16[512,1024]{1,0:T(8,128)(2,1)}, u32[]{:S(2)}) copy-start(bf16[512,1024]{1,0:T(8,128)(2,1)} %gate_ref.3) | copy-start | bytes 3145732
  8.8 7.4 %copy-start.6 = (f32[4,48,128]{2,1,0:T(8,128)S(1)}, f32[4,48,128]{2,1,0:T(8,128)}, u32[]{:S(2)}) copy-start(f32[4,48,128]{2,1,0:T(8,128)} %get-tuple-element.57.aux) | copy-start | bytes 294916
  13.5 5.9 %collective-permute-start.3 = (bf16[272,128]{1,0:T(8,128)(2,1)S(1)}, bf16[272,128]{1,0:T(8,128)(2,1)S(1)}, u32[]{:S(2)}, u32[]{:S(2)}) collective-permute-start(bf16[272,128]{1,0:T(8,128)(2,1)S(1)} %join_states.1), channel_id=1, source_target_pairs={{0,16},{4,20},{8,24},{12,28},{16,0},{20,4},{24,8},{28,12},{1,17},{... | collective-permute-start | bytes 208904 | tf_op jit(solution)/shard_map/ppermute | solution.py:300
  16.1 10.0 %slice-start = ((s8[8388608]{0:T(1024)(128)(4,1)}), s8[4194304]{0:T(1024)(128)(4,1)S(1)}, s32[]{:S(2)}) async-start(s8[8388608]{0:T(1024)(128)(4,1)} %bitcast.6), calls=%async_computation | async-start | bytes 8388608
  16.1 10.0 %slice-start.1 = ((s8[8388608]{0:T(1024)(128)(4,1)}), s8[4194304]{0:T(1024)(128)(4,1)S(1)}, s32[]{:S(2)}) async-start(s8[8388608]{0:T(1024)(128)(4,1)} %bitcast.6), calls=%async_computation.1 | async-start | bytes 8388608
  16.2 10.0 %copy-start.4 = (f32[1024]{0:T(1024)S(1)}, f32[1024]{0:T(1024)}, u32[]{:S(2)}) copy-start(f32[1024]{0:T(1024)} %param.16) | copy-start | bytes 12292
  19.6 4.3 %collective-permute-start.4 = (bf16[256,128]{1,0:T(8,128)(2,1)S(1)}, bf16[256,128]{1,0:T(8,128)(2,1)S(1)}, u32[]{:S(2)}, u32[]{:S(2)}) collective-permute-start(bf16[256,128]{1,0:T(8,128)(2,1)S(1)} %get-tuple-element.48), channel_id=1, source_target_pairs={{0,4},{4,0},{8,12},{12,8},{16,20},{20,16},{24,28},{28,24},{1,5},{5... | collective-permute-start | bytes 196616 | tf_op jit(solution)/shard_map/ppermute | solution.py:300
  20.3 4.3 %collective-permute-start.5 = (bf16[256,128]{1,0:T(8,128)(2,1)S(1)}, bf16[256,128]{1,0:T(8,128)(2,1)S(1)}, u32[]{:S(2)}, u32[]{:S(2)}) collective-permute-start(bf16[256,128]{1,0:T(8,128)(2,1)S(1)} %get-tuple-element.49), channel_id=1, source_target_pairs={{0,8},{4,12},{8,0},{12,4},{16,24},{20,28},{24,16},{28,20},{1,9},{5... | collective-permute-start | bytes 196616 | tf_op jit(solution)/shard_map/ppermute | solution.py:300
  20.9 5.2 %collective-permute-start.6 = (bf16[256,128]{1,0:T(8,128)(2,1)S(1)}, bf16[256,128]{1,0:T(8,128)(2,1)S(1)}, u32[]{:S(2)}, u32[]{:S(2)}) collective-permute-start(bf16[256,128]{1,0:T(8,128)(2,1)S(1)} %get-tuple-element.50), channel_id=1, source_target_pairs={{0,12},{4,8},{8,4},{12,0},{16,28},{20,24},{24,20},{28,16},{1,13},{... | collective-permute-start | bytes 196616 | tf_op jit(solution)/shard_map/ppermute | solution.py:300
  27.2 1.6 %collective-permute-start.8 = (bf16[128,1024]{1,0:T(8,128)(2,1)S(1)}, bf16[128,1024]{1,0:T(8,128)(2,1)S(1)}, u32[]{:S(2)}, u32[]{:S(2)}) collective-permute-start(bf16[128,1024]{1,0:T(8,128)(2,1)S(1)} %get-tuple-element.56), channel_id=1, source_target_pairs={{0,1},{1,0},{2,3},{3,2},{4,5},{5,4},{6,7},{7,6},{8,9},{9,8},{10,11... | collective-permute-start | bytes 786440 | tf_op jit(solution)/shard_map/ppermute | solution.py:628
  28.3 5.2 %collective-permute-start.7 = (bf16[128,1536]{1,0:T(8,128)(2,1)S(1)}, bf16[128,1536]{1,0:T(8,128)(2,1)S(1)}, u32[]{:S(2)}, u32[]{:S(2)}) collective-permute-start(bf16[128,1536]{1,0:T(8,128)(2,1)S(1)} %get-tuple-element.53), channel_id=1, source_target_pairs={{0,1},{1,0},{2,3},{3,2},{4,5},{5,4},{6,7},{7,6},{8,9},{9,8},{10,11... | collective-permute-start | bytes 1179656 | tf_op jit(solution)/shard_map/ppermute | solution.py:628
  28.9 9.2 %collective-permute-start.12 = (bf16[128,1024]{1,0:T(8,128)(2,1)S(1)}, bf16[128,1024]{1,0:T(8,128)(2,1)S(1)}, u32[]{:S(2)}, u32[]{:S(2)}) collective-permute-start(bf16[128,1024]{1,0:T(8,128)(2,1)S(1)} %add_pair.4), channel_id=1, source_target_pairs={{0,2},{1,3},{2,0},{3,1},{4,6},{5,7},{6,4},{7,5},{8,10},{9,11},{10,... | collective-permute-start | bytes 786440 | tf_op jit(solution)/shard_map/ppermute | solution.py:667
  33.6 13.0 %collective-permute-start.11 = (bf16[128,1536]{1,0:T(8,128)(2,1)S(1)}, bf16[128,1536]{1,0:T(8,128)(2,1)S(1)}, u32[]{:S(2)}, u32[]{:S(2)}) collective-permute-start(bf16[128,1536]{1,0:T(8,128)(2,1)S(1)} %add_pair.3), channel_id=1, source_target_pairs={{0,2},{1,3},{2,0},{3,1},{4,6},{5,7},{6,4},{7,5},{8,10},{9,11},{10,... | collective-permute-start | bytes 1179656 | tf_op jit(solution)/shard_map/ppermute | solution.py:668
  36.7 3.3 %collective-permute-start.9 = (bf16[128,5632]{1,0:T(8,128)(2,1)S(1)}, bf16[128,5632]{1,0:T(8,128)(2,1)S(1)}, u32[]{:S(2)}, u32[]{:S(2)}) collective-permute-start(bf16[128,5632]{1,0:T(8,128)(2,1)S(1)} %get-tuple-element.61), channel_id=1, source_target_pairs={{0,1},{1,0},{2,3},{3,2},{4,5},{5,4},{6,7},{7,6},{8,9},{9,8},{10,11... | collective-permute-start | bytes 4325384 | tf_op jit(solution)/shard_map/ppermute | solution.py:628
  40.0 14.1 %collective-permute-start.10 = (bf16[128,1536]{1,0:T(8,128)(2,1)S(1)}, bf16[128,1536]{1,0:T(8,128)(2,1)S(1)}, u32[]{:S(2)}, u32[]{:S(2)}) collective-permute-start(bf16[128,1536]{1,0:T(8,128)(2,1)S(1)} %add_pair.5), channel_id=1, source_target_pairs={{0,2},{1,3},{2,0},{3,1},{4,6},{5,7},{6,4},{7,5},{8,10},{9,11},{10,... | collective-permute-start | bytes 1179656 | tf_op jit(solution)/shard_map/ppermute | solution.py:670

commit v10 on v9

--- a/solution.py
+++ b/solution.py
@@ -313,7 +313,6 @@
         run = joined(functools.partial(run_kernel, distance), run, got)
         distance *= 2
         got = exchange(run, distance)
-    hold, got = lax.optimization_barrier((hold, got))
     operands = [got] + parts
     if ahead is None:
         kernel = functools.partial(end_kernel, distance, None)

time: 55.3 us -> 55.2 us (level)
  transfers between devices with their start and end apart: 13 -> 13, of which waited for: 10 -> 7; matrix products, arithmetic and copies ran while one was open for 0% -> 0% of each run, Pallas kernels for 23% -> 23%
where the time goes in v10:
time: 55.2 us; the launch traced here: 55 us
  waiting for transfers between devices  20.7 us (38%)
  Pallas kernels  18 us (33%)
  starting transfers between devices  15.3 us (28%)
  local copies, waits for them, and re-layouts  0.81 us (1%)
    ppermute x7, starting transfers between devices, exchange(): return lax.ppermute(value, 'seq', [(s, s ^ distance) for s in range(count)])  10.8 us
    ppermute x7, waiting for transfers between devices, exchange(): return lax.ppermute(value, 'seq', [(s, s ^ distance) for s in range(count)])  7.28 us
    pallas_call x7, Pallas kernels, local_call(): pl.pallas_call(kernel, in_specs=[VMEM] * len(operands), out_specs=[VMEM]...  6.11 us
    pallas_call x2, Pallas kernels, within(): pl.pallas_call(functools.partial(within_kernel, far), in_specs=[VMEM] * 6...  6.02 us
    ppermute x1, waiting for transfers between devices, per_device(): third, filled = await_piece(lax.ppermute(third, 'head', far), filled)  5.29 us
    ppermute x1, waiting for transfers between devices, per_device(): second, first = await_piece(lax.ppermute(second, 'head', far), first)  4.94 us
    pallas_call x1, Pallas kernels, give_states(): pl.pallas_call(give_kernel, in_specs=[HBM] * 4, out_shape=[jax.ShapeDtype...  3.35 us
    ppermute x3, waiting for transfers between devices, add(): come = lax.ppermute(theirs, 'head', near)  1.82 us
  transfers between devices with their start and end apart: 13, of which 7 were waited for; matrix products, arithmetic and copies ran while one was open for 0% of the time, Pallas kernels for 23%

profile of v10, /device:TPU:0, one launch (start us, length us, event | category | flops | bytes accessed | tf_op | source)
XLA Modules:
  0.0 55.0 jit_solution(8196612175478293911)
XLA Ops:
  0.0 3.4 %give_states.1 = (bf16[272,128]{1,0:T(8,128)(2,1)}, bf16[272,128]{1,0:T(8,128)(2,1)}, bf16[272,128]{1,0:T(8,128)(2,1)}, bf16[32,640]{1,0:T(8,128)(2,1)}, f32[4,48,128]{2,1,0:T(8,128)}) custom-call(f32[16,512]{1,0:T(8,128)} %bitcast.20, f32[1,16]{1,0:T(1,128)} %bitcast.21, f32[512,1024]{1,0:T(8,128)} %x_ref.3, f32[512,128]{1,0:T(8,128)} %bitcast.8), custom_call_target="tpu_custom_call" | custom-call | flops 200000000 | bytes 1500000 | tf_op jit(solution)/shard_map/give_states/pallas_call | solution.py:155
  3.4 3.0 %collective-permute-start = (bf16[272,128]{1,0:T(8,128)(2,1)}, bf16[272,128]{1,0:T(8,128)(2,1)S(1)}, u32[]{:S(2)}, u32[]{:S(2)}) collective-permute-start(bf16[272,128]{1,0:T(8,128)(2,1)} %get-tuple-element.38), channel_id=1, source_target_pairs={{0,4},{4,0},{8,12},{12,8},{16,20},{20,16},{24,28},{28,24},{1,5},{5... | collective-permute-start | bytes 208904 | tf_op jit(solution)/shard_map/ppermute | solution.py:300
  6.4 1.6 %collective-permute-start.1 = (bf16[272,128]{1,0:T(8,128)(2,1)}, bf16[272,128]{1,0:T(8,128)(2,1)S(1)}, u32[]{:S(2)}, u32[]{:S(2)}) collective-permute-start(bf16[272,128]{1,0:T(8,128)(2,1)} %get-tuple-element.39), channel_id=1, source_target_pairs={{0,8},{4,12},{8,0},{12,4},{16,24},{20,28},{24,16},{28,20},{1,9},{5... | collective-permute-start | bytes 208904 | tf_op jit(solution)/shard_map/ppermute | solution.py:300
  8.0 0.8 %copy-done.3 = bf16[32,640]{1,0:T(8,128)(2,1)S(1)} copy-done((bf16[32,640]{1,0:T(8,128)(2,1)S(1)}, bf16[32,640]{1,0:T(8,128)(2,1)}, u32[]{:S(2)}) %copy-start.3) | copy-done | bytes 40984
  9.4 2.1 %collective-permute-done.1.come2 = bf16[272,128]{1,0:T(8,128)(2,1)S(1)} collective-permute-done((bf16[272,128]{1,0:T(8,128)(2,1)}, bf16[272,128]{1,0:T(8,128)(2,1)S(1)}, u32[]{:S(2)}, u32[]{:S(2)}) %collective-permute-start.1) | collective-permute-done | bytes 69664 | tf_op jit(solution)/shard_map/ppermute | solution.py:300
  11.5 1.9 %collective-permute-done.2.come3 = bf16[272,128]{1,0:T(8,128)(2,1)S(1)} collective-permute-done((bf16[272,128]{1,0:T(8,128)(2,1)}, bf16[272,128]{1,0:T(8,128)(2,1)S(1)}, u32[]{:S(2)}, u32[]{:S(2)}) %collective-permute-start.2) | collective-permute-done | bytes 69664 | tf_op jit(solution)/shard_map/ppermute | solution.py:300
  13.5 2.7 %collective-permute-start.3 = (bf16[272,128]{1,0:T(8,128)(2,1)S(1)}, bf16[272,128]{1,0:T(8,128)(2,1)S(1)}, u32[]{:S(2)}, u32[]{:S(2)}) collective-permute-start(bf16[272,128]{1,0:T(8,128)(2,1)S(1)} %join_states.1), channel_id=1, source_target_pairs={{0,16},{4,20},{8,24},{12,28},{16,0},{20,4},{24,8},{28,12},{1,17},{... | collective-permute-start | bytes 208904 | tf_op jit(solution)/shard_map/ppermute | solution.py:300
  16.1 3.2 %collective-permute-done.3.last = bf16[272,128]{1,0:T(8,128)(2,1)S(1)} collective-permute-done((bf16[272,128]{1,0:T(8,128)(2,1)S(1)}, bf16[272,128]{1,0:T(8,128)(2,1)S(1)}, u32[]{:S(2)}, u32[]{:S(2)}) %collective-permute-start.3) | collective-permute-done | bytes 69664 | tf_op jit(solution)/shard_map/ppermute | solution.py:300
  19.5 0.7 %collective-permute-start.4 = (bf16[256,128]{1,0:T(8,128)(2,1)S(1)}, bf16[256,128]{1,0:T(8,128)(2,1)S(1)}, u32[]{:S(2)}, u32[]{:S(2)}) collective-permute-start(bf16[256,128]{1,0:T(8,128)(2,1)S(1)} %get-tuple-element.42), channel_id=1, source_target_pairs={{0,4},{4,0},{8,12},{12,8},{16,20},{20,16},{24,28},{28,24},{1,5},{5... | collective-permute-start | bytes 196616 | tf_op jit(solution)/shard_map/ppermute | solution.py:300
  20.3 2.7 %collective-permute-start.6 = (bf16[256,128]{1,0:T(8,128)(2,1)S(1)}, bf16[256,128]{1,0:T(8,128)(2,1)S(1)}, u32[]{:S(2)}, u32[]{:S(2)}) collective-permute-start(bf16[256,128]{1,0:T(8,128)(2,1)S(1)} %get-tuple-element.44), channel_id=1, source_target_pairs={{0,12},{4,8},{8,4},{12,0},{16,28},{20,24},{24,20},{28,16},{1,13},{... | collective-permute-start | bytes 196616 | tf_op jit(solution)/shard_map/ppermute | solution.py:300
  23.0 3.0 %within_far.1 = (f32[256,1024]{1,0:T(8,128)S(1)}, f32[256,1024]{1,0:T(8,128)S(1)}) custom-call(f32[4,48,128]{2,1,0:T(8,128)S(1)} %copy-done.6, f32[512,1024]{1,0:T(8,128)S(1)} %copy-done, f32[512,128]{1,0:T(8,128)S(1)} %bitcast.10, f32[512,128]{1,0:T(8,128)S(1)} %bitcast.12, bf16[512,1024]{1,0:T(8,128)(2,1)S(1)} %copy-done.5, f32[1,16]{1,0:T(1,128)S(1)} %bitcast.18), custom_call_target="tpu_custom_call" | custom-call | flops 4000000000 | bytes 3000000 | tf_op jit(solution)/shard_map/within_far/pallas_call | solution.py:420
  26.1 1.1 %finish_far.1 = (bf16[128,1024]{1,0:T(8,128)(2,1)S(1)}, f32[128,1024]{1,0:T(8,128)S(1)}, bf16[256,1024]{1,0:T(8,128)(2,1)S(1)}) custom-call(f32[256,1024]{1,0:T(8,128)S(1)} %get-tuple-element.35.own, f32[256,1024]{1,0:T(8,128)S(1)} %get-tuple-element.36.lead, f32[512,128]{1,0:T(8,128)S(1)} %bitcast.13, bf16[256,128]{1,0:T(8,128)(2,1)S(1)} %get-tuple-element.41.q0, ...), custom_call_target="tpu_custom_call" | custom-call | flops 536870912 | tf_op jit(solution)/shard_map/finish_far/pallas_call | solution.py:505
  27.3 1.0 %project_more.1 = (bf16[128,1536]{1,0:T(8,128)(2,1)S(1)}, f32[128,1536]{1,0:T(8,128)S(1)}) custom-call(bf16[256,1024]{1,0:T(8,128)(2,1)S(1)} %get-tuple-element.48.normed, bf16[1024,4096]{1,0:T(8,128)(2,1)S(1)} %bitcast.7), custom_call_target="tpu_custom_call" | custom-call | flops 805306368 | tf_op jit(solution)/shard_map/project_more/pallas_call | solution.py:505
  29.0 1.6 %collective-permute-start.12 = (bf16[128,1024]{1,0:T(8,128)(2,1)S(1)}, bf16[128,1024]{1,0:T(8,128)(2,1)S(1)}, u32[]{:S(2)}, u32[]{:S(2)}) collective-permute-start(bf16[128,1024]{1,0:T(8,128)(2,1)S(1)} %add_pair.4), channel_id=1, source_target_pairs={{0,2},{1,3},{2,0},{3,1},{4,6},{5,7},{6,4},{7,5},{8,10},{9,11},{10,... | collective-permute-start | bytes 786440 | tf_op jit(solution)/shard_map/ppermute | solution.py:666
  30.5 3.0 %within_near.1 = (f32[256,1024]{1,0:T(8,128)S(1)}, f32[256,1024]{1,0:T(8,128)S(1)}) custom-call(f32[4,48,128]{2,1,0:T(8,128)S(1)} %copy-done.6, f32[512,1024]{1,0:T(8,128)S(1)} %copy-done, f32[512,128]{1,0:T(8,128)S(1)} %bitcast.11, f32[512,128]{1,0:T(8,128)S(1)} %bitcast.14, bf16[512,1024]{1,0:T(8,128)(2,1)S(1)} %copy-done.5, f32[1,16]{1,0:T(1,128)S(1)} %bitcast.19), custom_call_target="tpu_custom_call" | custom-call | flops 4000000000 | bytes 3000000 | tf_op jit(solution)/shard_map/within_near/pallas_call | solution.py:420
  34.2 2.5 %finish_near.1 = (bf16[128,5632]{1,0:T(8,128)(2,1)S(1)}, f32[128,1536]{1,0:T(8,128)S(1)}, bf16[128,1024]{1,0:T(8,128)(2,1)S(1)}) custom-call(bf16[256,1024]{1,0:T(8,128)(2,1)S(1)} %get-tuple-element.48.normed, f32[256,1024]{1,0:T(8,128)S(1)} %get-tuple-element.52.own, f32[256,1024]{1,0:T(8,128)S(1)} %get-tuple-element.53.lead, f32[512,128]{1,0:T(8,128)S(1)} %bitcast.15, ...), custom_call_target="tpu_custom_call" | custom-call | flops 1879048192 | tf_op jit(solution)/shard_map/finish_near/pallas_call | solution.py:505
  36.8 1.4 %collective-permute-done.12.refs_0_ = bf16[128,1024]{1,0:T(8,128)(2,1)S(1)} collective-permute-done((bf16[128,1024]{1,0:T(8,128)(2,1)S(1)}, bf16[128,1024]{1,0:T(8,128)(2,1)S(1)}, u32[]{:S(2)}, u32[]{:S(2)}) %collective-permute-start.12) | collective-permute-done | bytes 262176 | tf_op jit(solution)/shard_map/ppermute | solution.py:666
  38.2 1.8 %collective-permute-done.9.come = bf16[128,5632]{1,0:T(8,128)(2,1)S(1)} collective-permute-done((bf16[128,5632]{1,0:T(8,128)(2,1)S(1)}, bf16[128,5632]{1,0:T(8,128)(2,1)S(1)}, u32[]{:S(2)}, u32[]{:S(2)}) %collective-permute-start.9) | collective-permute-done | bytes 1441824 | tf_op jit(solution)/shard_map/ppermute | solution.py:627
  40.1 1.6 %collective-permute-start.10 = (bf16[128,1536]{1,0:T(8,128)(2,1)S(1)}, bf16[128,1536]{1,0:T(8,128)(2,1)S(1)}, u32[]{:S(2)}, u32[]{:S(2)}) collective-permute-start(bf16[128,1536]{1,0:T(8,128)(2,1)S(1)} %add_pair.5), channel_id=1, source_target_pairs={{0,2},{1,3},{2,0},{3,1},{4,6},{5,7},{6,4},{7,5},{8,10},{9,11},{10,... | collective-permute-start | bytes 1179656 | tf_op jit(solution)/shard_map/ppermute | solution.py:669
  41.7 4.9 %collective-permute-done.11.refs_0_ = bf16[128,1536]{1,0:T(8,128)(2,1)S(1)} collective-permute-done((bf16[128,1536]{1,0:T(8,128)(2,1)S(1)}, bf16[128,1536]{1,0:T(8,128)(2,1)S(1)}, u32[]{:S(2)}, u32[]{:S(2)}) %collective-permute-start.11) | collective-permute-done | bytes 393248 | tf_op jit(solution)/shard_map/ppermute | solution.py:667
  46.6 1.3 %project_kept.1.kept = f32[128,4096]{1,0:T(8,128)S(1)} custom-call(bf16[128,1024]{1,0:T(8,128)(2,1)S(1)} %get-tuple-element.54.kept, bf16[128,5632]{1,0:T(8,128)(2,1)S(1)} %collective-permute-done.9.come, bf16[1024,4096]{1,0:T(8,128)(2,1)S(1)} %bitcast.7), custom_call_target="tpu_custom_call" | custom-call | flops 1073741824 | tf_op jit(solution)/shard_map/project_kept/pallas_call | solution.py:505
  47.9 1.0 %early_sums.1.refs_1_ = bf16[128,4096]{1,0:T(8,128)(2,1)} custom-call(f32[128,4096]{1,0:T(8,128)S(1)} %project_kept.1.kept, bf16[128,1024]{1,0:T(8,128)(2,1)S(1)} %get-tuple-element.59.first, bf16[128,1536]{1,0:T(8,128)(2,1)S(1)} %get-tuple-element.60.second), custom_call_target="tpu_custom_call" | custom-call | tf_op jit(solution)/shard_map/early_sums/pallas_call | solution.py:548
  48.9 5.3 %collective-permute-done.10.refs_0_ = bf16[128,1536]{1,0:T(8,128)(2,1)S(1)} collective-permute-done((bf16[128,1536]{1,0:T(8,128)(2,1)S(1)}, bf16[128,1536]{1,0:T(8,128)(2,1)S(1)}, u32[]{:S(2)}, u32[]{:S(2)}) %collective-permute-start.10) | collective-permute-done | bytes 393248 | tf_op jit(solution)/shard_map/ppermute | solution.py:669
  54.2 0.8 %last_sums.1 = bf16[128,4096]{1,0:T(8,128)(2,1)} custom-call(f32[128,4096]{1,0:T(8,128)S(1)} %project_kept.1.kept, bf16[128,1536]{1,0:T(8,128)(2,1)S(1)} %get-tuple-element.61.third, bf16[128,4096]{1,0:T(8,128)(2,1)} %get-tuple-element.62.filled), custom_call_target="tpu_custom_call", output_to_operand_aliasing={{}: (2, {})} | custom-call | tf_op jit(solution)/shard_map/last_sums/pallas_call | solution.py:580
  (41 shorter events, 2.5 us)
Async XLA Ops:
  0.0 8.0 %copy-start = (f32[512,1024]{1,0:T(8,128)S(1)}, f32[512,1024]{1,0:T(8,128)}, u32[]{:S(2)}) copy-start(f32[512,1024]{1,0:T(8,128)} %x_ref.3) | copy-start | bytes 6291460
  0.0 8.0 %copy-start.1 = (f32[512,1,128]{2,1,0:T(1,128)S(1)}, f32[512,1,128]{2,1,0:T(1,128)}, u32[]{:S(2)}) copy-start(f32[512,1,128]{2,1,0:T(1,128)} %param.13) | copy-start | bytes 786436
  0.0 23.0 %copy-start.7 = (f32[16]{0:T(128)S(1)}, f32[16]{0:T(128)}, u32[]{:S(2)}) copy-start(f32[16]{0:T(128)} %param.15) | copy-start | bytes 196
  3.4 19.6 %copy-start.2 = (f32[512,1,128]{2,1,0:T(1,128)S(1)}, f32[512,1,128]{2,1,0:T(1,128)}, u32[]{:S(2)}) copy-start(f32[512,1,128]{2,1,0:T(1,128)} %param.14) | copy-start | bytes 786436
  3.4 6.0 %collective-permute-start = (bf16[272,128]{1,0:T(8,128)(2,1)}, bf16[272,128]{1,0:T(8,128)(2,1)S(1)}, u32[]{:S(2)}, u32[]{:S(2)}) collective-permute-start(bf16[272,128]{1,0:T(8,128)(2,1)} %get-tuple-element.38), channel_id=1, source_target_pairs={{0,4},{4,0},{8,12},{12,8},{16,20},{20,16},{24,28},{28,24},{1,5},{5... | collective-permute-start | bytes 208904 | tf_op jit(solution)/shard_map/ppermute | solution.py:300
  6.4 5.1 %collective-permute-start.1 = (bf16[272,128]{1,0:T(8,128)(2,1)}, bf16[272,128]{1,0:T(8,128)(2,1)S(1)}, u32[]{:S(2)}, u32[]{:S(2)}) collective-permute-start(bf16[272,128]{1,0:T(8,128)(2,1)} %get-tuple-element.39), channel_id=1, source_target_pairs={{0,8},{4,12},{8,0},{12,4},{16,24},{20,28},{24,16},{28,20},{1,9},{5... | collective-permute-start | bytes 208904 | tf_op jit(solution)/shard_map/ppermute | solution.py:300
  8.0 5.4 %collective-permute-start.2 = (bf16[272,128]{1,0:T(8,128)(2,1)}, bf16[272,128]{1,0:T(8,128)(2,1)S(1)}, u32[]{:S(2)}, u32[]{:S(2)}) collective-permute-start(bf16[272,128]{1,0:T(8,128)(2,1)} %get-tuple-element.40), channel_id=1, source_target_pairs={{0,12},{4,8},{8,4},{12,0},{16,28},{20,24},{24,20},{28,16},{1,13},{... | collective-permute-start | bytes 208904 | tf_op jit(solution)/shard_map/ppermute | solution.py:300
  8.0 0.8 %copy-start.3 = (bf16[32,640]{1,0:T(8,128)(2,1)S(1)}, bf16[32,640]{1,0:T(8,128)(2,1)}, u32[]{:S(2)}) copy-start(bf16[32,640]{1,0:T(8,128)(2,1)} %get-tuple-element.37.wk) | copy-start | bytes 122884
  8.8 14.3 %copy-start.5 = (bf16[512,1024]{1,0:T(8,128)(2,1)S(1)}, bf16[512,1024]{1,0:T(8,128)(2,1)}, u32[]{:S(2)}) copy-start(bf16[512,1024]{1,0:T(8,128)(2,1)} %gate_ref.3) | copy-start | bytes 3145732
  8.8 14.3 %copy-start.6 = (f32[4,48,128]{2,1,0:T(8,128)S(1)}, f32[4,48,128]{2,1,0:T(8,128)}, u32[]{:S(2)}) copy-start(f32[4,48,128]{2,1,0:T(8,128)} %get-tuple-element.51.aux) | copy-start | bytes 294916
  13.5 5.9 %collective-permute-start.3 = (bf16[272,128]{1,0:T(8,128)(2,1)S(1)}, bf16[272,128]{1,0:T(8,128)(2,1)S(1)}, u32[]{:S(2)}, u32[]{:S(2)}) collective-permute-start(bf16[272,128]{1,0:T(8,128)(2,1)S(1)} %join_states.1), channel_id=1, source_target_pairs={{0,16},{4,20},{8,24},{12,28},{16,0},{20,4},{24,8},{28,12},{1,17},{... | collective-permute-start | bytes 208904 | tf_op jit(solution)/shard_map/ppermute | solution.py:300
  19.4 6.7 %slice-start = ((s8[8388608]{0:T(1024)(128)(4,1)}), s8[4194304]{0:T(1024)(128)(4,1)S(1)}, s32[]{:S(2)}) async-start(s8[8388608]{0:T(1024)(128)(4,1)} %bitcast.6), calls=%async_computation | async-start | bytes 8388608
  19.5 6.6 %collective-permute-start.4 = (bf16[256,128]{1,0:T(8,128)(2,1)S(1)}, bf16[256,128]{1,0:T(8,128)(2,1)S(1)}, u32[]{:S(2)}, u32[]{:S(2)}) collective-permute-start(bf16[256,128]{1,0:T(8,128)(2,1)S(1)} %get-tuple-element.42), channel_id=1, source_target_pairs={{0,4},{4,0},{8,12},{12,8},{16,20},{20,16},{24,28},{28,24},{1,5},{5... | collective-permute-start | bytes 196616 | tf_op jit(solution)/shard_map/ppermute | solution.py:300
  20.2 5.9 %collective-permute-start.5 = (bf16[256,128]{1,0:T(8,128)(2,1)S(1)}, bf16[256,128]{1,0:T(8,128)(2,1)S(1)}, u32[]{:S(2)}, u32[]{:S(2)}) collective-permute-start(bf16[256,128]{1,0:T(8,128)(2,1)S(1)} %get-tuple-element.43), channel_id=1, source_target_pairs={{0,8},{4,12},{8,0},{12,4},{16,24},{20,28},{24,16},{28,20},{1,9},{5... | collective-permute-start | bytes 196616 | tf_op jit(solution)/shard_map/ppermute | solution.py:300
  20.3 5.7 %collective-permute-start.6 = (bf16[256,128]{1,0:T(8,128)(2,1)S(1)}, bf16[256,128]{1,0:T(8,128)(2,1)S(1)}, u32[]{:S(2)}, u32[]{:S(2)}) collective-permute-start(bf16[256,128]{1,0:T(8,128)(2,1)S(1)} %get-tuple-element.44), channel_id=1, source_target_pairs={{0,12},{4,8},{8,4},{12,0},{16,28},{20,24},{24,20},{28,16},{1,13},{... | collective-permute-start | bytes 196616 | tf_op jit(solution)/shard_map/ppermute | solution.py:300
  23.0 3.1 %slice-start.1 = ((s8[8388608]{0:T(1024)(128)(4,1)}), s8[4194304]{0:T(1024)(128)(4,1)S(1)}, s32[]{:S(2)}) async-start(s8[8388608]{0:T(1024)(128)(4,1)} %bitcast.6), calls=%async_computation.1 | async-start | bytes 8388608
  23.0 3.1 %copy-start.4 = (f32[1024]{0:T(1024)S(1)}, f32[1024]{0:T(1024)}, u32[]{:S(2)}) copy-start(f32[1024]{0:T(1024)} %param.16) | copy-start | bytes 12292
  27.3 1.6 %collective-permute-start.8 = (bf16[128,1024]{1,0:T(8,128)(2,1)S(1)}, bf16[128,1024]{1,0:T(8,128)(2,1)S(1)}, u32[]{:S(2)}, u32[]{:S(2)}) collective-permute-start(bf16[128,1024]{1,0:T(8,128)(2,1)S(1)} %get-tuple-element.50), channel_id=1, source_target_pairs={{0,1},{1,0},{2,3},{3,2},{4,5},{5,4},{6,7},{7,6},{8,9},{9,8},{10,11... | collective-permute-start | bytes 786440 | tf_op jit(solution)/shard_map/ppermute | solution.py:627
  28.3 5.2 %collective-permute-start.7 = (bf16[128,1536]{1,0:T(8,128)(2,1)S(1)}, bf16[128,1536]{1,0:T(8,128)(2,1)S(1)}, u32[]{:S(2)}, u32[]{:S(2)}) collective-permute-start(bf16[128,1536]{1,0:T(8,128)(2,1)S(1)} %get-tuple-element.47), channel_id=1, source_target_pairs={{0,1},{1,0},{2,3},{3,2},{4,5},{5,4},{6,7},{7,6},{8,9},{9,8},{10,11... | collective-permute-start | bytes 1179656 | tf_op jit(solution)/shard_map/ppermute | solution.py:627
  29.0 9.2 %collective-permute-start.12 = (bf16[128,1024]{1,0:T(8,128)(2,1)S(1)}, bf16[128,1024]{1,0:T(8,128)(2,1)S(1)}, u32[]{:S(2)}, u32[]{:S(2)}) collective-permute-start(bf16[128,1024]{1,0:T(8,128)(2,1)S(1)} %add_pair.4), channel_id=1, source_target_pairs={{0,2},{1,3},{2,0},{3,1},{4,6},{5,7},{6,4},{7,5},{8,10},{9,11},{10,... | collective-permute-start | bytes 786440 | tf_op jit(solution)/shard_map/ppermute | solution.py:666
  33.6 13.0 %collective-permute-start.11 = (bf16[128,1536]{1,0:T(8,128)(2,1)S(1)}, bf16[128,1536]{1,0:T(8,128)(2,1)S(1)}, u32[]{:S(2)}, u32[]{:S(2)}) collective-permute-start(bf16[128,1536]{1,0:T(8,128)(2,1)S(1)} %add_pair.3), channel_id=1, source_target_pairs={{0,2},{1,3},{2,0},{3,1},{4,6},{5,7},{6,4},{7,5},{8,10},{9,11},{10,... | collective-permute-start | bytes 1179656 | tf_op jit(solution)/shard_map/ppermute | solution.py:667
  36.7 3.3 %collective-permute-start.9 = (bf16[128,5632]{1,0:T(8,128)(2,1)S(1)}, bf16[128,5632]{1,0:T(8,128)(2,1)S(1)}, u32[]{:S(2)}, u32[]{:S(2)}) collective-permute-start(bf16[128,5632]{1,0:T(8,128)(2,1)S(1)} %get-tuple-element.55), channel_id=1, source_target_pairs={{0,1},{1,0},{2,3},{3,2},{4,5},{5,4},{6,7},{7,6},{8,9},{9,8},{10,11... | collective-permute-start | bytes 4325384 | tf_op jit(solution)/shard_map/ppermute | solution.py:627
  40.1 14.1 %collective-permute-start.10 = (bf16[128,1536]{1,0:T(8,128)(2,1)S(1)}, bf16[128,1536]{1,0:T(8,128)(2,1)S(1)}, u32[]{:S(2)}, u32[]{:S(2)}) collective-permute-start(bf16[128,1536]{1,0:T(8,128)(2,1)S(1)} %add_pair.5), channel_id=1, source_target_pairs={{0,2},{1,3},{2,0},{3,1},{4,6},{5,7},{6,4},{7,5},{8,10},{9,11},{10,... | collective-permute-start | bytes 1179656 | tf_op jit(solution)/shard_map/ppermute | solution.py:669
